TPU v7x, 256 devices: a whole 4x4x8 slice. The times are simulated.
256 devices in a mesh: tm: 32 (over y, z_lo, core), seq: 8 (over x, z_hi).
Axes of the slice: x: 4, y: 4, z: 8 (z_hi: 2, z_lo: 4; z = z_hi * 4 + z_lo), core: 2. Of those that a mesh axis runs over, the one named last changes fastest.
Arguments:
- states: float32 [32, 512, 1536], P('tm', 'seq'), may hold values from -6 to 6
- qkv_weight: bfloat16 [1536, 3, 1536], P('tm', None, 'seq'), may hold values from -0.15625 to 0.15625
- text_kv: bfloat16 [32, 320, 2, 1536], P('tm', 'seq'), may hold values from -180 to 180
- mod_table: float32 [128, 3, 1536], replicated, may hold values from -3 to 3
- step_table: float32 [128], replicated, may hold values from 0.02 to 0.1
- step_ids: int32 [32], P('tm'), may hold values from 0 to 127, as said below
Outputs:
- latents: float32 [32, 512, 1536], P('tm', 'seq')
- changes: float32 [2, 32], P(None, 'tm')
Inputs may be any that keep to these rules, and one draw needn't show every extreme that they name: `step_ids`: distinct and strictly decreasing; the first is 127 and the last 0.
All inputs are finite; a program needn't handle non-finite values.
Results may differ from a plain program's by a relative error of at most 0.0017.
The roundings to bfloat16 on the way count: a program that leaves them out, or rounds other values in their place, can miss the bound.
Values may be sent and summed in bfloat16 or wider, within the bound.
No kernel may reach another device: no remote copies, remote signals or barrier semaphores. Data moves between devices by JAX's collectives and lax.ppermute only.
A program may use at most 128 MiB of HBM per device.

v0:
```python
import jax
import jax.numpy as jnp
from jax import lax
from jax.sharding import PartitionSpec as P

HEAD_DIM = 64
SWEEPS = 2


def prefix_2(value, axis, combine, identity):
    length, position = (lax.axis_size(axis), lax.axis_index(axis))
    everything = lax.all_gather(value, axis)
    start = jnp.broadcast_to(jnp.asarray(identity, value.dtype), value.shape)

    def step(k, before):
        reached = k < position
        new = combine(before, everything[k])
        return jnp.where(reached, new, before)

    return lax.fori_loop(0, length, step, start)


def modulate(latent, modulation):
    average = jnp.mean(latent, axis=-1, keepdims=True)
    centred = latent - average
    variance = jnp.mean(centred * centred, axis=-1, keepdims=True)
    normed = centred * lax.rsqrt(variance + 1e-06)
    return (normed * (1.0 + modulation[1]) + modulation[0]).astype(jnp.bfloat16)


def attend(projected, text_heads, head_width):
    heads_here = head_width // HEAD_DIM
    total_rows = projected.shape[0]
    queries = projected[:, 0].reshape(total_rows, heads_here, HEAD_DIM)
    key_rows = jnp.concatenate([projected[:, 1], text_heads[:, 0]], axis=0)
    key_rows = key_rows.reshape(key_rows.shape[0], heads_here, HEAD_DIM)
    value_rows = jnp.concatenate([projected[:, 2], text_heads[:, 1]], axis=0)
    value_rows = value_rows.reshape(value_rows.shape[0], heads_here, HEAD_DIM)
    block_rows = total_rows
    while block_rows > 512 and block_rows % 2 == 0:
        block_rows = block_rows // 2
    blocks = queries.reshape(total_rows // block_rows, block_rows, heads_here, HEAD_DIM)

    def one_block(query_block):
        scores = jnp.einsum(
            "qhd,khd->hqk", query_block, key_rows, preferred_element_type=jnp.float32
        ) * HEAD_DIM ** (-0.5)
        top = jnp.max(scores, axis=-1, keepdims=True)
        exp_scores = jnp.exp(scores - top)
        attn_weights = (exp_scores / jnp.sum(exp_scores, axis=-1, keepdims=True)).astype(
            jnp.bfloat16
        )
        return jnp.einsum(
            "hqk,khd->qhd", attn_weights, value_rows, preferred_element_type=jnp.float32
        ).astype(jnp.bfloat16)

    attended = lax.map(one_block, blocks)
    return attended.reshape(total_rows, head_width)


def add_terms(earlier, later):
    return earlier + later


def on_device(states, qkv_weight, text_kv, mod_table, step_table, step_ids):
    width = mod_table.shape[2]
    local_rows = states.shape[1]
    is_first = lax.axis_index("tm") == 0
    step_id = step_ids[0]
    modulation = lax.dynamic_index_in_dim(mod_table, step_id, 0, keepdims=False)
    step_size = -lax.dynamic_index_in_dim(step_table, step_id, 0, keepdims=False)
    text_heads = lax.all_to_all(text_kv[0], "seq", split_axis=2, concat_axis=0, tiled=True)
    head_width = qkv_weight.shape[2]
    weight_cols = lax.all_gather(qkv_weight, "seq", axis=2, tiled=True)
    weight_all = lax.all_gather(weight_cols, "tm", axis=0, tiled=True).reshape(width, 3 * width)
    latent = states[0]
    changes = []
    for sweep_index in range(SWEEPS):
        modulated = modulate(latent, modulation)
        projected = jnp.dot(modulated, weight_all, preferred_element_type=jnp.float32).astype(
            jnp.bfloat16
        )
        projected = projected.reshape(local_rows, 3, width)
        projected = lax.all_to_all(projected, "seq", split_axis=2, concat_axis=0, tiled=True)
        attended = attend(projected, text_heads, head_width)
        attended = lax.all_to_all(attended, "seq", split_axis=0, concat_axis=1, tiled=True)
        velocity = latent + modulation[2] * attended.astype(jnp.float32)
        carried = jnp.where(is_first, latent, 0.0)
        term = step_size * velocity + carried
        prefix = prefix_2(term, "tm", add_terms, jnp.zeros_like(term))
        updated = prefix + carried
        change = lax.pmax(jnp.max(jnp.abs(updated - latent)), "seq")
        changes.append(change)
        latent = updated
    return (latent[None], jnp.stack(changes).reshape(SWEEPS, 1))


def solution(mesh):
    in_specs = (
        P("tm", "seq", None),
        P("tm", None, "seq"),
        P("tm", "seq", None, None),
        P(),
        P(),
        P("tm"),
    )
    out_specs = (P("tm", "seq", None), P(None, "tm"))
    return jax.shard_map(
        on_device, mesh=mesh, in_specs=in_specs, out_specs=out_specs, check_vma=False
    )
```

profile of v0, /device:TPU:8, one launch (start us, length us, event | category | flops | bytes accessed | tf_op | source)
XLA Modules:
  0.0 597.6 jit_solution(5627441763289412195)
XLA Ops:
  8.3 78.4 %all_gather.16 = bf16[48,3,1536]{0,1,2:T(4,128)(2,1)S(1)} all-gather(bf16[48,3,192]{0,1,2:T(4,128)(2,1)S(1)} %copy.64), channel_id=1, replica_groups=mesh['tm'=32,'seq'=8] {'seq'}, dimensions={2}, use_global_device_ids=true | all-gather | bytes 497664 | tf_op jit(solution)/shard_map/all_gather | solution.py:74
  86.7 1.9 copy.65
  88.6 2.3 copy.71
  91.5 1.9 reshape.172
  93.4 4.7 all-to-all-start.1
  100.0 72.3 %all-gather.5.cloned.1.call-done = bf16[1536,3,1536]{2,0,1:T(8,128)(2,1)} async-done(((bf16[48,3,1536]{2,0,1:T(8,128)(2,1)}), bf16[1536,3,1536]{2,0,1:T(8,128)(2,1)}) %all-gather.5.cloned.1.call-update) | async-done | bytes 14155792 | tf_op jit(solution)/shard_map/all_gather | solution.py:75
  172.3 18.6 %copy.66 = bf16[1536,3,1536]{0,2,1:T(8,128)(2,1)} copy(bf16[1536,3,1536]{2,0,1:T(8,128)(2,1)} %all-gather.5.cloned.1.call-done) | data formatting | bytes 28311552 | tf_op jit(solution)/shard_map/all_gather | solution.py:75
  190.9 9.4 %convolution_convert_fusion.1 = bf16[64,4608]{1,0:T(8,128)(2,1)S(1)} fusion(bf16[1536,4608]{0,1:T(8,128)(2,1)} %bitcast.88, f32[1,64,1536]{2,1,0:T(8,128)S(1)} %copy-done, f32[1536]{0:T(1024)S(1)} %get-tuple-element.224, f32[1536]{0:T(1024)S(1)} %get-tuple-element.223, f32[64]{0:T(128)S(1)} %add_rsqrt_fusion.1, f32[64]{0:T(128)S(1)} %broadcast_multiply_fusion.1), kind=kOutput, calls=%fused_computation.5 | convolution fusion | flops 906756096 | bytes 15151616 | tf_op jit(solution)/shard_map/dot_general | solution.py:80
  200.7 1.2 copy.67
  202.0 2.2 reshape.170
  204.1 9.0 %all-to-all-start = ((bf16[8,2,18432]{2,1,0:T(2,128)(2,1)}), bf16[8,2,18432]{2,1,0:T(2,128)(2,1)S(1)}, u32[]{:S(2)}, u32[]{:S(2)}) async-start(bf16[8,2,18432]{2,1,0:T(2,128)(2,1)} %reshape.170), calls=%async_computation | async-start | bytes 1179648 | tf_op jit(solution)/shard_map/all_to_all | solution.py:84
  213.1 1.2 reshape.173
  216.4 11.9 %all-to-all-done = bf16[8,2,18432]{2,1,0:T(2,128)(2,1)S(1)} async-done(((bf16[8,2,18432]{2,1,0:T(2,128)(2,1)}), bf16[8,2,18432]{2,1,0:T(2,128)(2,1)S(1)}, u32[]{:S(2)}, u32[]{:S(2)}) %all-to-all-start) | async-done | bytes 589856 | tf_op jit(solution)/shard_map/all_to_all | solution.py:84
  229.4 1.7 copy.88
  231.6 5.0 fusion.58
  236.6 3.1 fusion.14
  240.9 6.8 %all-to-all-start.2 = ((bf16[8,64,192]{2,1,0:T(8,128)(2,1)}), bf16[8,64,192]{2,1,0:T(8,128)(2,1)S(1)}, u32[]{:S(2)}, u32[]{:S(2)}) async-start(bf16[8,64,192]{2,1,0:T(8,128)(2,1)} %copy.77), calls=%async_computation.2 | async-start | bytes 524288 | tf_op jit(solution)/shard_map/all_to_all | solution.py:86
  249.2 9.7 %all-to-all-done.2 = bf16[8,64,192]{2,1,0:T(8,128)(2,1)S(1)} async-done(((bf16[8,64,192]{2,1,0:T(8,128)(2,1)}), bf16[8,64,192]{2,1,0:T(8,128)(2,1)S(1)}, u32[]{:S(2)}, u32[]{:S(2)}) %all-to-all-start.2) | async-done | bytes 196640 | tf_op jit(solution)/shard_map/all_to_all | solution.py:86
  260.4 76.9 %all-gather.7.cloned.1.call-done = f32[32,64,1536]{2,1,0:T(8,128)} async-done(((f32[1,64,1536]{2,1,0:T(8,128)}), f32[32,64,1536]{2,1,0:T(8,128)}) %all-gather.7.cloned.1.call-update) | async-done | bytes 12582928 | tf_op jit(solution)/shard_map/all_gather | solution.py:12
  337.3 37.1 %while.36 = (s32[]{:T(128)}, f32[64,1536]{1,0:T(8,128)S(1)}, s32[]{:T(128)}, f32[32,64,1536]{2,1,0:T(8,128)}, s32[]{:T(128)}, /*index=5*/s32[]{:T(128)}) while((s32[]{:T(128)}, f32[64,1536]{1,0:T(8,128)S(1)}, s32[]{:T(128)}, f32[32,64,1536]{2,1,0:T(8,128)}, s32[]{:T(128)}, /*index=5*/s32[]{:T(128)}) %tuple.79), condition=%wide.region_5.6_spmd.clone, body=%wide.region_4.5_spmd.clone.sunk | while | flops 294916 | bytes 1179741 | solution.py:20
  338.5 1.1 add_select_fusion.4
  339.6 1.1 add_select_fusion.4
  340.8 1.1 add_select_fusion.4
  341.9 1.1 add_select_fusion.4
  343.1 1.1 add_select_fusion.4
  344.3 1.1 add_select_fusion.4
  345.4 1.1 add_select_fusion.4
  346.6 1.1 add_select_fusion.4
  347.7 1.1 add_select_fusion.4
  348.9 1.1 add_select_fusion.4
  350.1 1.1 add_select_fusion.4
  361.7 1.1 add_select_fusion.4
  371.0 1.1 add_select_fusion.4
  374.8 9.4 %convolution_convert_fusion = bf16[64,4608]{1,0:T(8,128)(2,1)S(1)} fusion(bf16[1536,4608]{0,1:T(8,128)(2,1)} %bitcast.89, f32[64,1536]{1,0:T(8,128)S(1)} %get-tuple-element.246, f32[1536]{0:T(1024)S(1)} %get-tuple-element.224, f32[1536]{0:T(1024)S(1)} %get-tuple-element.223, f32[64]{0:T(128)S(1)} %add_rsqrt_fusion, f32[64]{0:T(128)S(1)} %broadcast_multiply_fusion), kind=kOutput, calls=%fused_computation.4 | convolution fusion | flops 906756096 | bytes 15151616 | tf_op jit(solution)/shard_map/dot_general | solution.py:80
  384.6 1.2 copy.79
  387.0 26.4 %all_to_all.80 = bf16[8,2,18432]{2,1,0:T(2,128)(2,1)S(1)} all-to-all(bf16[8,2,18432]{2,1,0:T(2,128)(2,1)S(1)} %reshape.174), channel_id=1, replica_groups=mesh['tm'=32,'seq'=8] {'seq'}, dimensions={0} | all-to-all | bytes 1179648 | tf_op jit(solution)/shard_map/all_to_all | solution.py:84
  414.4 1.7 copy.90
  416.6 5.1 fusion.59
  421.7 3.1 fusion.15
  425.3 15.5 %all_to_all.81 = bf16[8,64,192]{2,1,0:T(8,128)(2,1)S(1)} all-to-all(bf16[8,64,192]{2,1,0:T(8,128)(2,1)S(1)} %copy.85), channel_id=1, replica_groups=mesh['tm'=32,'seq'=8] {'seq'}, dimensions={0} | all-to-all | bytes 393216 | tf_op jit(solution)/shard_map/all_to_all | solution.py:86
  442.1 76.1 %all-gather.9.cloned.1.call-done = f32[2048,1536]{1,0:T(8,128)} async-done(((f32[64,1536]{1,0:T(8,128)}), f32[2048,1536]{1,0:T(8,128)}) %all-gather.9.cloned.1.call-update) | async-done | bytes 12582928 | tf_op jit(solution)/shard_map/all_gather | solution.py:12
  518.3 37.1 %while.37 = (s32[]{:T(128)}, f32[64,1536]{1,0:T(8,128)S(1)}, s32[]{:T(128)}, f32[32,64,1536]{2,1,0:T(8,128)}, s32[]{:T(128)}, /*index=5*/s32[]{:T(128)}) while((s32[]{:T(128)}, f32[64,1536]{1,0:T(8,128)S(1)}, s32[]{:T(128)}, f32[32,64,1536]{2,1,0:T(8,128)}, s32[]{:T(128)}, /*index=5*/s32[]{:T(128)}) %tuple.91), condition=%wide.region_11.12_spmd.clone, body=%wide.region_10.11_spmd.clone.sunk | while | flops 294916 | bytes 1179741 | solution.py:20
  529.9 1.1 add_select_fusion.5
  539.2 1.1 add_select_fusion.5
  551.9 1.1 add_select_fusion.5
  555.4 1.5 fusion.24
  556.9 32.4 %all-reduce = (f32[1]{0:T(128)}, f32[1]{0:T(128)}) all-reduce(f32[1]{0:T(128)} %bitcast.35, f32[1]{0:T(128)} %bitcast.34), channel_id=1, replica_groups=mesh['tm'=32,'seq'=8] {'seq'}, use_global_device_ids=true, to_apply=%region_15.16 | all-reduce | flops 2 | bytes 16 | tf_op jit(solution)/shard_map/pmax | solution.py:92
  589.2 1.8 maximum_bitcast_fusion
  (106 shorter events, 70.1 us)
Async XLA Ops:
  7.2 91.6 %copy-start = (f32[1,64,1536]{2,1,0:T(8,128)S(1)}, f32[1,64,1536]{2,1,0:T(8,128)}, u32[]{:S(2)}) copy-start(f32[1,64,1536]{2,1,0:T(8,128)} %param.10) | copy-start | bytes 1179652
  7.2 165.1 %all-gather.5.cloned.1.call-start = ((), (), s32[]{:S(2)}) async-start(), calls=%async_computation.5 | async-start | bytes 14598144 | tf_op jit(solution)/shard_map/all_gather | solution.py:75
  93.4 110.7 %all-to-all-start.1 = ((bf16[8,2,7680]{2,1,0:T(2,128)(2,1)}), bf16[8,2,7680]{2,1,0:T(2,128)(2,1)S(1)}, u32[]{:S(2)}, u32[]{:S(2)}) async-start(bf16[8,2,7680]{2,1,0:T(2,128)(2,1)} %reshape.172), calls=%async_computation.1 | async-start | bytes 491520 | tf_op jit(solution)/shard_map/all_to_all | solution.py:72
  204.1 24.2 %all-to-all-start = ((bf16[8,2,18432]{2,1,0:T(2,128)(2,1)}), bf16[8,2,18432]{2,1,0:T(2,128)(2,1)S(1)}, u32[]{:S(2)}, u32[]{:S(2)}) async-start(bf16[8,2,18432]{2,1,0:T(2,128)(2,1)} %reshape.170), calls=%async_computation | async-start | bytes 1179648 | tf_op jit(solution)/shard_map/all_to_all | solution.py:84
  216.4 20.2 %copy-start.1 = (bf16[320,1,192]{0,2,1:T(8,128)(2,1)}, bf16[320,1,192]{0,2,1:T(8,128)(2,1)S(1)}, u32[]{:S(2)}) copy-start(bf16[320,1,192]{0,2,1:T(8,128)(2,1)S(1)} %copy.73) | copy-start | bytes 368644
  236.6 11.3 %copy-start.3 = (f32[128]{0:T(128)S(1)}, f32[128]{0:T(128)}, u32[]{:S(2)}) copy-start(f32[128]{0:T(128)} %param.14) | copy-start | bytes 1540
  240.9 18.0 %all-to-all-start.2 = ((bf16[8,64,192]{2,1,0:T(8,128)(2,1)}), bf16[8,64,192]{2,1,0:T(8,128)(2,1)S(1)}, u32[]{:S(2)}, u32[]{:S(2)}) async-start(bf16[8,64,192]{2,1,0:T(8,128)(2,1)} %copy.77), calls=%async_computation.2 | async-start | bytes 524288 | tf_op jit(solution)/shard_map/all_to_all | solution.py:86
  247.7 89.6 %all-gather.7.cloned.1.call-start = ((), (), s32[]{:S(2)}) async-start(), calls=%async_computation.6 | async-start | bytes 12976128 | tf_op jit(solution)/shard_map/all_gather | solution.py:12
  260.3 258.0 %all-gather.9.cloned.1.call-start = ((), (), s32[]{:S(2)}) async-start(), calls=%async_computation.7 | async-start | bytes 12976128 | tf_op jit(solution)/shard_map/all_gather | solution.py:12
  416.2 5.5 copy-start.2
Sparse Core Ops, SparseCore 0:
  88.7 83.4 all-gather.4
  260.4 76.8 all-gather.6
  442.2 75.9 all-gather.8
where the time goes:
time: 601 us; the launch traced here: 598 us
  waiting for transfers between devices  247 us (41%)
  blocking collectives  153 us (25%)
  other arithmetic  79.4 us (13%)
  local copies, waits for them, and re-layouts  45.9 us (8%)
  matrix products  35 us (6%)
  starting transfers between devices  20.8 us (3%)
  between operations  15.4 us (3%)
    all_gather x2, waiting for transfers between devices, prefix_2(): everything = lax.all_gather(value, axis)  153 us
    all_gather x1, blocking collectives, on_device(): weight_cols = lax.all_gather(qkv_weight, 'seq', axis=2, tiled=True)  78.4 us
    select_n x64, other arithmetic, step(): return jnp.where(reached, new, before)  72.7 us
    all_gather x1, waiting for transfers between devices, on_device(): lax.all_gather(weight_cols, 'tm', axis=0, tiled=True)  72.3 us
    pmax x1, blocking collectives, on_device(): change = lax.pmax(jnp.max(jnp.abs(updated - latent)), 'seq')  32.4 us
    all_to_all x1, blocking collectives, on_device(): lax.all_to_all(projected, 'seq', split_axis=2, concat_axis=0, tiled=True)  26.4 us
    dot_general x2, matrix products, on_device(): jnp.dot(modulated, weight_all, preferred_element_type=jnp.float32)  18.8 us
    all_gather x1, local copies, waits for them, and re-layouts, on_device(): lax.all_gather(weight_cols, 'tm', axis=0, tiled=True)  18.6 us
  transfers between devices with their start and end apart: 6, of which 5 were waited for; matrix products, arithmetic and copies ran while one was open for 7% of the time, Pallas kernels for 0%

commit v1 on v0

v1 whole, which is shorter than its diff:
```python
import functools
import itertools

import jax
import jax.numpy as jnp
from jax import lax
from jax.experimental import pallas as pl
from jax.experimental.pallas import tpu as pltpu
from jax.sharding import Mesh, PartitionSpec as P

AXES = ("y", "zl", "c", "x", "zh")
SIZES = {"y": 4, "zl": 4, "c": 2, "x": 4, "zh": 2}

HEAD_DIM = 64
SWEEPS = 2
D = 1536
HALF = 768
HW = 192
ROWS = 64
TOK = 512
TXT = 320
KEYS = TOK + TXT
VMEM_LIMIT = 48 * 1024 * 1024
f32, bf16 = jnp.float32, jnp.bfloat16


def permute(value, axes, move):
    def index(place):
        flat = 0
        for name in axes:
            flat = flat * SIZES[name] + place[name] % SIZES[name]
        return flat

    pairs = []
    for coords in itertools.product(*[range(SIZES[name]) for name in axes]):
        place = dict(zip(axes, coords))
        target = move(dict(place))
        if target is not None:
            pairs.append((index(place), index(target)))
    return lax.ppermute(value, axes if len(axes) > 1 else axes[0], pairs)


def shift(value, axis, amount):
    return permute(value, (axis,), lambda p: {axis: p[axis] + amount})


def forward(value, axis, amount):
    return permute(
        value, (axis,),
        lambda p: {axis: p[axis] + amount} if p[axis] + amount < SIZES[axis] else None,
    )


def shift_z(value, amount):
    def move(p):
        ring = (p["zh"] * 4 + p["zl"] + amount) % 8
        return {"zl": ring % 4, "zh": ring // 4}

    return permute(value, ("zl", "zh"), move)


def swap_core_zh(value, same):
    moved = permute(
        value, ("c", "zh"),
        lambda p: None if p["c"] == p["zh"] else {"c": p["zh"], "zh": p["c"]},
    )
    return jnp.where(same, value, moved)


def call(kernel, out_shape, n_vmem, n_smem, flops=0, nbytes=0, scratch=()):
    return pl.pallas_call(
        kernel,
        out_shape=out_shape,
        in_specs=[pl.BlockSpec(memory_space=pltpu.SMEM)] * n_smem
        + [pl.BlockSpec(memory_space=pltpu.VMEM)] * n_vmem,
        out_specs=jax.tree.map(lambda _: pl.BlockSpec(memory_space=pltpu.VMEM), out_shape),
        scratch_shapes=list(scratch),
        compiler_params=pltpu.CompilerParams(vmem_limit_bytes=VMEM_LIMIT),
        cost_estimate=pl.CostEstimate(flops=flops, bytes_accessed=nbytes, transcendentals=0),
    )


def struct(*shape, dtype=f32):
    return jax.ShapeDtypeStruct(shape, dtype)


def first_norm_kernel(lat_ref, mod_ref, out_ref, send_ref):
    latent = lat_ref[...]
    average = jnp.mean(latent, axis=-1, keepdims=True)
    centred = latent - average
    variance = jnp.mean(centred * centred, axis=-1, keepdims=True)
    normed = centred * lax.rsqrt(variance + 1e-06)
    modulated = (normed * (1.0 + mod_ref[1:2, :]) + mod_ref[0:1, :]).astype(bf16)
    for half in range(2):
        cols = [slice(k * 2 * HW + half * HW, k * 2 * HW + (half + 1) * HW) for k in range(4)]
        out_ref[:, half * HALF:(half + 1) * HALF] = jnp.concatenate(
            [modulated[:, s] for s in cols], axis=1
        )
        piece = jnp.concatenate([latent[:, s] for s in cols], axis=1)
        for sub in range(4):
            send_ref[sub * 2 + half] = piece[sub * 16:(sub + 1) * 16]


def weight_kernel(place_ref, *refs):
    pieces, out_ref = refs[:4], refs[4]
    y, zl = place_ref[0], place_ref[1]
    for ky in range(4):
        from_y = lax.rem(y - ky + 4, 4)
        for kz in range(4):
            from_zl = lax.rem(zl - kz + 4, 4)
            row = (from_zl // 2) * HALF + from_y * HW + lax.rem(from_zl, 2) * 96
            out_ref[pl.ds(pl.multiple_of(row, 32), 96), :] = pieces[ky][kz]


def attention_kernel(first, place_ref, *refs):
    blocks = refs[:8]
    w_ref, tk_ref, tv_ref, out_ref, k01, v01, k2, v2, q01, q2 = refs[8:]
    core, x = place_ref[2], place_ref[3]
    if first:
        rows = jnp.concatenate([b[...] for b in blocks], axis=0)
        qkv = jnp.dot(rows, w_ref[...], preferred_element_type=f32)
    else:
        mine = jnp.concatenate([b[...] for b in blocks[:4]], axis=0)
        other = jnp.concatenate([b[...] for b in blocks[4:]], axis=0)
        w_mine = w_ref[pl.ds(pl.multiple_of(core * HALF, HALF), HALF), :]
        w_other = w_ref[pl.ds(pl.multiple_of((1 - core) * HALF, HALF), HALF), :]
        qkv = jnp.dot(mine, w_mine, preferred_element_type=f32)
        qkv = qkv + jnp.dot(other, w_other, preferred_element_type=f32)
    scale = HEAD_DIM ** (-0.5)
    q01[...] = (qkv[:, 0:128] * scale).astype(bf16)
    k01[0:TOK, :] = qkv[:, 128:256].astype(bf16)
    v01[0:TOK, :] = qkv[:, 256:384].astype(bf16)
    q2[...] = (qkv[:, 384:448] * scale).astype(bf16)
    k2[0:TOK, :] = qkv[:, 448:512].astype(bf16)
    v2[0:TOK, :] = qkv[:, 512:576].astype(bf16)
    k01[TOK:, :] = tk_ref[:, 0:128]
    v01[TOK:, :] = tv_ref[:, 0:128]
    k2[TOK:, :] = tk_ref[:, 128:192]
    v2[TOK:, :] = tv_ref[:, 128:192]
    lane = lax.broadcasted_iota(jnp.int32, (128, 128), 1)

    def attend(query, keys, values):
        scores = lax.dot_general(
            query, keys, (((1,), (1,)), ((), ())), preferred_element_type=f32
        )
        top = jnp.max(scores, axis=-1, keepdims=True)
        exp_scores = jnp.exp(scores - top)
        total = jnp.sum(exp_scores, axis=-1, keepdims=True)
        weights = (exp_scores * (1.0 / total)).astype(bf16)
        return jnp.dot(weights, values, preferred_element_type=f32)

    for chunk in range(4):
        span = slice(chunk * 128, (chunk + 1) * 128)
        pair = q01[span, :]
        zero = jnp.zeros_like(pair)
        out0 = attend(jnp.where(lane < 64, pair, zero), k01[...], v01[...])
        out1 = attend(jnp.where(lane < 64, zero, pair), k01[...], v01[...])
        out01 = jnp.where(lane < 64, out0, out1).astype(bf16)
        out2 = attend(q2[span, :], k2[...], v2[...]).astype(bf16)
        from_x = lax.rem(x - (chunk if not first else chunk) + 4, 4)
        for part in range(8):
            if first:
                sub = part % 4
                zh = core if part < 4 else 1 - core
            else:
                sub, zh = part // 2, part % 2
            target = (sub * 4 + from_x) * 2 + zh
            out_ref[target, :, 0:128] = out01[part * 16:(part + 1) * 16]
            out_ref[target, :, 128:HW] = out2[part * 16:(part + 1) * 16]


def terms_kernel(first_ref, dt_ref, att_ref, lat_ref, gate_ref, part_ref, total_ref):
    run = lat_ref[0] * first_ref[0]
    for j in range(8):
        part_ref[j] = run
        sub, zh = j // 2, j % 2
        attended = jnp.concatenate(
            [att_ref[(sub * 4 + k) * 2 + zh].astype(f32) for k in range(4)], axis=1
        )
        run = run + dt_ref[j] * (lat_ref[j] + gate_ref[j:j + 1, :] * attended)
    total_ref[...] = run


def update_kernel(with_stats, part_ref, lat_ref, t1_ref, t2_ref, t3_ref, new_ref, chg_ref,
                  *stats_ref):
    offset = t1_ref[...] + t2_ref[...] + t3_ref[...]
    lane = lax.broadcasted_iota(jnp.int32, (16, 128), 1)
    for j in range(8):
        new = part_ref[j] + offset
        new_ref[j] = new
        change = jnp.max(jnp.abs(new - lat_ref[j]))
        chg_ref[j:j + 1, :] = jnp.full((1, 128), change, f32)
        if with_stats:
            average = jnp.mean(new, axis=-1, keepdims=True)
            centred = new - average
            spread = jnp.sum(centred * centred, axis=-1, keepdims=True)
            stats_ref[0][j] = jnp.where(lane == 0, average, spread)


def modulate_kernel(new_ref, mine_ref, other_ref, shift_ref, scale_ref, out_ref):
    for j in range(8):
        mean_a, mean_b = mine_ref[j][:, 0:1], other_ref[j][:, 0:1]
        spread = mine_ref[j][:, 1:2] + other_ref[j][:, 1:2]
        average = (mean_a + mean_b) * 0.5
        gap = mean_a - mean_b
        variance = (spread + gap * gap * (HALF * 0.5)) * (1.0 / D)
        normed = (new_ref[j] - average) * lax.rsqrt(variance + 1e-06)
        out_ref[j] = (
            normed * (1.0 + scale_ref[j:j + 1, :]) + shift_ref[j:j + 1, :]
        ).astype(bf16)


def place_kernel(in_ref, out_ref):
    for sub in range(4):
        for k in range(4):
            cols = slice(k * HW, (k + 1) * HW)
            out_ref[sub * 16:(sub + 1) * 16, k * 2 * HW:(k + 1) * 2 * HW] = jnp.concatenate(
                [in_ref[sub * 2][:, cols], in_ref[sub * 2 + 1][:, cols]], axis=1
            )


def on_device(states, qkv_weight, text_kv, mod_table, step_table, step_ids):
    y, zl, c, x, zh = (lax.axis_index(name) for name in AXES)
    same = c == zh
    place = jnp.stack([y, zl, c, x]).astype(jnp.int32)
    latent = states[0]

    with jax.named_scope("norm_first"):
        mod_own = lax.dynamic_index_in_dim(mod_table, step_ids[0], 0, keepdims=False)
        modulated, state_send = call(
            first_norm_kernel, (struct(ROWS, D, dtype=bf16), struct(8, 16, HALF)), 2, 0
        )(latent, mod_own)
    with jax.named_scope("gather_first"):
        modulated = swap_core_zh(modulated, same)
        mine = [modulated] + [shift(modulated, "x", k) for k in (1, 2, 3)]
        other = [shift(b, "c", 1) for b in mine]
        blocks = [b for pair in zip(mine, other) for b in pair]

    with jax.named_scope("weights"):
        w = qkv_weight
        w = jnp.concatenate(
            [w[:, 0, :128], w[:, 1, :128], w[:, 2, :128],
             w[:, 0, 128:], w[:, 1, 128:], w[:, 2, 128:]], axis=1
        )
        w_a = permute(w, ("c", "zh"), lambda p: None if p["c"] == p["zh"] else
                      {"c": 1 - p["c"], "zh": p["zh"]})
        w_b = [permute(w, ("c", "zh"), lambda p, k=k: {"c": p["zh"], "zh": 1 - p["zh"]}
                       if p["c"] == k else None) for k in range(2)]
        w0 = jnp.where(same, jnp.where(c == 0, w, w_a), w_b[0])
        w1 = jnp.where(same, jnp.where(c == 1, w, w_a), w_b[1])
        w2 = jnp.concatenate([w0, w1], axis=0)
        w8 = jnp.stack([w2, shift_z(w2, 1), shift_z(w2, 2), shift_z(w2, -1)])
        pieces = [w8] + [shift(w8, "y", k) for k in (1, 2, 3)]
        weight = call(weight_kernel, struct(D, 3 * HW, dtype=bf16), 4, 1)(place, *pieces)

    with jax.named_scope("text"):
        text = text_kv[0].reshape(40, 2, 8, HW).transpose(2, 1, 0, 3)
        text = lax.all_to_all(text, ("x", "zh"), 0, 0)
        text = swap_core_zh(text, same)
        text = text.transpose(1, 0, 2, 3).reshape(2, TXT, HW)

    with jax.named_scope("plan"):
        step_id = step_ids[0].reshape(1, 1)
        mate = shift(step_id, "c", 1)
        pair = jnp.where(c == 0, jnp.concatenate([step_id, mate], 1),
                         jnp.concatenate([mate, step_id], 1))
        pairs = jnp.concatenate([pair] + [shift(pair, "zl", k) for k in (1, 2, 3)], axis=0)
        ids = jnp.take(pairs, lax.rem(zl - jnp.arange(4) + 4, 4), axis=0).reshape(8)
        mods = jnp.take(mod_table, ids, axis=0).reshape(8, 3, 4, 2, HW)
        mods = lax.dynamic_index_in_dim(mods, c, 3, keepdims=False).reshape(8, 3, HALF)
        shifts, scales, gates = mods[:, 0], mods[:, 1], mods[:, 2]
        dts = -jnp.take(step_table, ids)
        is_first = (y == 0).astype(f32).reshape(1)

    with jax.named_scope("states"):
        lat = lax.all_to_all(state_send, ("zl", "c"), 0, 0)

    changes = []
    for sweep in range(SWEEPS):
        last = sweep == SWEEPS - 1
        with jax.named_scope("attention"):
            attended = call(
                functools.partial(attention_kernel, sweep == 0),
                struct(32, 16, HW, dtype=bf16), 11, 1,
                flops=2 * TOK * D * 3 * HW + 4 * TOK * KEYS * HW, nbytes=4 << 20,
                scratch=[
                    pltpu.VMEM((KEYS, 128), bf16), pltpu.VMEM((KEYS, 128), bf16),
                    pltpu.VMEM((KEYS, 64), bf16), pltpu.VMEM((KEYS, 64), bf16),
                    pltpu.VMEM((TOK, 128), bf16), pltpu.VMEM((TOK, 64), bf16),
                ],
            )(place, *blocks, weight, text[0], text[1])
        with jax.named_scope("to_prefix"):
            attended = lax.all_to_all(attended, ("zl", "x", "zh"), 0, 0)
        with jax.named_scope("prefix"):
            part, total = call(
                terms_kernel, (struct(8, 16, HALF), struct(16, HALF)), 3, 2
            )(is_first, dts, attended, lat, gates)
            earlier = [forward(total, "y", k) for k in (1, 2, 3)]
            outs = (struct(8, 16, HALF), struct(8, 128))
            if not last:
                outs = outs + (struct(8, 16, 128),)
            new, change, *stats = call(
                functools.partial(update_kernel, not last), outs, 5, 0
            )(part, lat, *earlier)
        changes.append(change)
        lat = new
        if not last:
            with jax.named_scope("norm"):
                stats = stats[0]
                modulated = call(
                    modulate_kernel, struct(8, 16, HALF, dtype=bf16), 5, 0
                )(new, stats, shift(stats, "c", 1), shifts, scales)
            with jax.named_scope("gather"):
                modulated = lax.all_to_all(modulated, ("zl", "zh"), 0, 0).reshape(128, HALF)
                mine = [modulated] + [shift(modulated, "x", k) for k in (1, 2, 3)]
                blocks = mine + [shift(b, "c", 1) for b in mine]
    with jax.named_scope("place"):
        out = lax.all_to_all(lat, ("zl", "c"), 0, 0)
        out = call(place_kernel, struct(ROWS, D), 1, 0)(out)
    with jax.named_scope("changes"):
        top = jnp.concatenate(changes, axis=0)
        top = jnp.maximum(top, shift(top, "c", 1))
        top = functools.reduce(jnp.maximum, [top] + [shift(top, "x", k) for k in (1, 2, 3)])
        for amount in (1, 2):
            top = jnp.maximum(top, permute(top, ("zl",), lambda p: {"zl": p["zl"] ^ amount}))
        top = jnp.maximum(top, shift(top, "zh", 1))
        top = top[:, 0].reshape(SWEEPS, 8)
        top = lax.dynamic_slice_in_dim(top, zl * 2 + c, 1, axis=1)
    return out[None], top


def solution(mesh):
    fine = Mesh(mesh.devices.reshape([SIZES[name] for name in AXES]), AXES)
    tm, seq = ("y", "zl", "c"), ("x", "zh")
    in_specs = (
        P(tm, seq, None), P(tm, None, seq), P(tm, seq, None, None), P(), P(), P(tm),
    )
    out_specs = (P(tm, seq, None), P(None, tm))
    return jax.shard_map(
        on_device, mesh=fine, in_specs=in_specs, out_specs=out_specs, check_vma=False
    )
```

time: 601 us -> 228 us (0.38)
  waiting for transfers between devices: 247 us -> 67 us
  blocking collectives: 153 us -> 30.3 us
  other arithmetic: 79.4 us -> 3.74 us
  starting transfers between devices: 20.8 us -> 88 us
  matrix products: 35 us -> 0 us
  local copies, waits for them, and re-layouts: 45.9 us -> 13.9 us
  Pallas kernels: 0 us -> 21.8 us
  between operations: 15.4 us -> 1.77 us
    all_gather x3 -> x0, waiting for transfers between devices: 225 us -> none  [the longest x2 153 us: prefix_2(): everything = lax.all_gather(value, axis)]
    all_gather x1 -> x0, blocking collectives: 78.4 us -> none  [on_device(): weight_cols = lax.all_gather(qkv_weight, 'seq', axis=2, tiled=True)]
    select_n x64 -> x7, other arithmetic: 72.7 us -> 2.34 us  [the longest x1 0.87 us: on_device(): w0 = jnp.where(same, jnp.where(c == 0, w, w_a), w_b[0])]
    ppermute x0 -> x43, starting transfers between devices: none -> 61.8 us  [permute(): return lax.ppermute(value, axes if len(axes) > 1 else axes[0], pairs)]
    ppermute x0 -> x43, waiting for transfers between devices: none -> 56.8 us  [permute(): return lax.ppermute(value, axes if len(axes) > 1 else axes[0], pairs)]
    pmax x1 -> x0, blocking collectives: 32.4 us -> none  [on_device(): change = lax.pmax(jnp.max(jnp.abs(updated - latent)), 'seq')]
    dot_general x4 -> x0, matrix products: 24.9 us -> none  [the longest x2 18.8 us: on_device(): jnp.dot(modulated, weight_all, preferred_element_type=jnp.float32)]
    pallas_call x0 -> x10, Pallas kernels: none -> 21.8 us  [the longest x2 16.5 us: on_device(): call(functools.partial(attention_kernel, sweep == 0), struct(32, 16, HW,...]
  transfers between devices with their start and end apart: 6 -> 47, of which waited for: 5 -> 22; matrix products, arithmetic and copies ran while one was open for 7% -> 6% of each run, Pallas kernels for 0% -> 5%
where the time goes in v1:
time: 228 us; the launch traced here: 227 us
  starting transfers between devices  88 us (39%)
  waiting for transfers between devices  67 us (29%)
  blocking collectives  30.3 us (13%)
  Pallas kernels  21.8 us (10%)
  local copies, waits for them, and re-layouts  13.9 us (6%)
  other arithmetic  3.74 us (2%)
    ppermute x43, starting transfers between devices, permute(): return lax.ppermute(value, axes if len(axes) > 1 else axes[0], pairs)  61.8 us
    ppermute x43, waiting for transfers between devices, permute(): return lax.ppermute(value, axes if len(axes) > 1 else axes[0], pairs)  56.8 us
    all_to_all x1, blocking collectives, on_device(): attended = lax.all_to_all(attended, ('zl', 'x', 'zh'), 0, 0)  18.6 us
    pallas_call x2, Pallas kernels, on_device(): call(functools.partial(attention_kernel, sweep == 0), struct(32, 16, HW,...  16.5 us
    all_to_all x1, blocking collectives, on_device(): modulated = lax.all_to_all(modulated, ('zl', 'zh'), 0, 0).reshape(128, HALF)  11.7 us
    all_to_all x1, starting transfers between devices, on_device(): attended = lax.all_to_all(attended, ('zl', 'x', 'zh'), 0, 0)  10.5 us
    all_to_all x1, waiting for transfers between devices, on_device(): attended = lax.all_to_all(attended, ('zl', 'x', 'zh'), 0, 0)  10.2 us
    all_to_all x1, starting transfers between devices, on_device(): text = lax.all_to_all(text, ('x', 'zh'), 0, 0)  8.28 us
  transfers between devices with their start and end apart: 47, of which 22 were waited for; matrix products, arithmetic and copies ran while one was open for 6% of the time, Pallas kernels for 5%

profile of v1, /device:TPU:8, one launch (start us, length us, event | category | flops | bytes accessed | tf_op | source)
XLA Modules:
  0.0 226.5 jit_solution(16315146486620076988)
XLA Ops:
  3.1 10.3 %collective-permute-start.13 = (bf16[48,576]{1,0:T(8,128)(2,1)S(1)}, bf16[48,576]{1,0:T(8,128)(2,1)}, u32[]{:S(2)}, u32[]{:S(2)}) collective-permute-start(bf16[48,576]{1,0:T(8,128)(2,1)S(1)} %concatenate.40), channel_id=1, source_target_pairs={{0,1},{1,8},{2,3},{3,10},{4,5},{5,12},{6,7},{7,14},{16,17},{17,24}... | collective-permute-start | bytes 165896 | tf_op jit(solution)/shard_map/weights/ppermute | solution.py:40
  14.7 1.7 collective-permute-start
  18.5 8.3 %all-to-all-start = ((bf16[8,2,40,192]{3,2,1,0:T(8,128)(2,1)}), bf16[8,2,40,192]{3,2,1,0:T(8,128)(2,1)}, u32[]{:S(2)}, u32[]{:S(2)}) async-start(bf16[8,2,40,192]{3,2,1,0:T(8,128)(2,1)} %copy.17), calls=%async_computation | async-start | bytes 655360 | tf_op jit(solution)/shard_map/text/all_to_all | solution.py:258
  30.1 1.9 collective-permute-start.3
  32.0 4.1 %collective-permute-done.3 = s32[1,2]{1,0:T(1,128)S(1)} collective-permute-done((s32[1,2]{1,0:T(1,128)S(1)}, s32[1,2]{1,0:T(1,128)S(1)}, u32[]{:S(2)}, u32[]{:S(2)}) %collective-permute-start.3) | collective-permute-done | bytes 40 | tf_op jit(solution)/shard_map/plan/ppermute | solution.py:40
  36.1 4.4 %collective-permute-done.2 = s32[1,2]{1,0:T(1,128)S(1)} collective-permute-done((s32[1,2]{1,0:T(1,128)S(1)}, s32[1,2]{1,0:T(1,128)S(1)}, u32[]{:S(2)}, u32[]{:S(2)}) %collective-permute-start.2) | collective-permute-done | bytes 40 | tf_op jit(solution)/shard_map/plan/ppermute | solution.py:40
  40.5 5.3 %collective-permute-done.1 = s32[1,2]{1,0:T(1,128)S(1)} collective-permute-done((s32[1,2]{1,0:T(1,128)S(1)}, s32[1,2]{1,0:T(1,128)S(1)}, u32[]{:S(2)}, u32[]{:S(2)}) %collective-permute-start.1) | collective-permute-done | bytes 40 | tf_op jit(solution)/shard_map/plan/ppermute | solution.py:40
  48.0 6.3 %collective-permute-start.17 = (bf16[96,576]{1,0:T(8,128)(2,1)S(1)}, bf16[96,576]{1,0:T(8,128)(2,1)S(1)}, u32[]{:S(2)}, u32[]{:S(2)}) collective-permute-start(bf16[96,576]{1,0:T(8,128)(2,1)S(1)} %get-tuple-element.37), channel_id=1, source_target_pairs={{0,49},{1,48},{16,0},{17,1},{32,16},{33,17},{48,32},{49,33},{2,51}... | collective-permute-start | bytes 331784 | tf_op jit(solution)/shard_map/weights/ppermute | solution.py:40
  54.3 2.8 %collective-permute-start.10 = (bf16[64,1536]{1,0:T(8,128)(2,1)S(1)}, bf16[64,1536]{1,0:T(8,128)(2,1)}, u32[]{:S(2)}, u32[]{:S(2)}) collective-permute-start(bf16[64,1536]{1,0:T(8,128)(2,1)S(1)} %broadcast_select_fusion.refs_0_), channel_id=1, source_target_pairs={{0,6},{2,0},{4,2},{6,4},{1,7},{3,1},{5,3},{7,5},{8,14},{10,8},{12,... | collective-permute-start | bytes 589832 | tf_op jit(solution)/shard_map/gather_first/ppermute | solution.py:40
  57.9 3.7 %collective-permute-done.15 = bf16[96,576]{1,0:T(8,128)(2,1)S(1)} collective-permute-done((bf16[96,576]{1,0:T(8,128)(2,1)S(1)}, bf16[96,576]{1,0:T(8,128)(2,1)S(1)}, u32[]{:S(2)}, u32[]{:S(2)}) %collective-permute-start.15) | collective-permute-done | bytes 110624 | tf_op jit(solution)/shard_map/weights/ppermute | solution.py:40
  62.2 2.6 %collective-permute-start.19 = (bf16[4,96,576]{2,1,0:T(8,128)(2,1)S(1)}, bf16[4,96,576]{2,1,0:T(8,128)(2,1)}, u32[]{:S(2)}, u32[]{:S(2)}) collective-permute-start(bf16[4,96,576]{2,1,0:T(8,128)(2,1)S(1)} %pad_maximum_fusion.refs_0_), channel_id=1, source_target_pairs={{0,128},{64,192},{128,0},{192,64},{1,129},{65,193},{129,1},{193,65... | collective-permute-start | bytes 1327112 | tf_op jit(solution)/shard_map/weights/ppermute | solution.py:40
  64.8 1.9 collective-permute-start.18
  67.4 4.0 %all-to-all-start.2 = ((f32[8,16,768]{2,1,0:T(8,128)}), f32[8,16,768]{2,1,0:T(8,128)S(1)}, u32[]{:S(2)}, u32[]{:S(2)}) async-start(f32[8,16,768]{2,1,0:T(8,128)} %copy-done.4), calls=%async_computation.2 | async-start | bytes 786432 | tf_op jit(solution)/shard_map/states/all_to_all | solution.py:276
  71.4 1.5 collective-permute-start.6
  72.9 1.4 collective-permute-start.21
  74.3 1.4 gather_fusion.2
  75.7 1.8 gather.17
  78.6 1.5 collective-permute-done.6.refs_2_
  80.0 2.2 collective-permute-start.5
  82.5 2.5 %collective-permute-done.19.refs_2_ = bf16[4,96,576]{2,1,0:T(8,128)(2,1)} collective-permute-done((bf16[4,96,576]{2,1,0:T(8,128)(2,1)S(1)}, bf16[4,96,576]{2,1,0:T(8,128)(2,1)}, u32[]{:S(2)}, u32[]{:S(2)}) %collective-permute-start.19) | collective-permute-done | bytes 442400 | tf_op jit(solution)/shard_map/weights/ppermute | solution.py:40
  85.8 1.5 weights.1.refs_8_
  88.4 8.7 %attention.2 = bf16[32,16,192]{2,1,0:T(8,128)(2,1)} custom-call(s32[4]{0:T(128)S(1)} %pad_add_fusion.1.place_ref, bf16[64,1536]{1,0:T(8,128)(2,1)S(1)} %broadcast_select_fusion.refs_0_, bf16[64,1536]{1,0:T(8,128)(2,1)S(1)} %collective-permute-done.5.refs_1_, bf16[64,1536]{1,0:T(8,128)(2,1)} %collective-permute-done.6.refs_2_, ...), custom_call_target="tpu_custom_call" | custom-call | flops 1233125376 | bytes 4194304 | tf_op jit(solution)/shard_map/attention/pallas_call | solution.py:282
  97.1 1.3 copy-done.1
  99.1 10.5 %all-to-all-start.1 = ((bf16[32,16,192]{2,1,0:T(8,128)(2,1)}), bf16[32,16,192]{2,1,0:T(8,128)(2,1)S(1)}, u32[]{:S(2)}, u32[]{:S(2)}) async-start(bf16[32,16,192]{2,1,0:T(8,128)(2,1)} %attention.2), calls=%async_computation.1 | async-start | bytes 524288 | tf_op jit(solution)/shard_map/to_prefix/all_to_all | solution.py:293
  111.4 10.2 %all-to-all-done.1.att_ref = bf16[32,16,192]{2,1,0:T(8,128)(2,1)S(1)} async-done(((bf16[32,16,192]{2,1,0:T(8,128)(2,1)}), bf16[32,16,192]{2,1,0:T(8,128)(2,1)S(1)}, u32[]{:S(2)}, u32[]{:S(2)}) %all-to-all-start.1) | async-done | bytes 196640 | tf_op jit(solution)/shard_map/to_prefix/all_to_all | solution.py:293
  122.9 3.8 %collective-permute-start.23 = (f32[16,768]{1,0:T(8,128)S(1)}, f32[16,768]{1,0:T(8,128)S(1)}, u32[]{:S(2)}, u32[]{:S(2)}) collective-permute-start(f32[16,768]{1,0:T(8,128)S(1)} %get-tuple-element.16), channel_id=1, source_target_pairs={{0,128},{64,192},{1,129},{65,193},{2,130},{66,194},{3,131},{67,195... | collective-permute-start | bytes 147464 | tf_op jit(solution)/shard_map/prefix/ppermute | solution.py:40
  126.7 1.9 collective-permute-start.22
  128.7 4.0 %collective-permute-done.22.t1_ref = f32[16,768]{1,0:T(8,128)S(1)} collective-permute-done((f32[16,768]{1,0:T(8,128)S(1)}, f32[16,768]{1,0:T(8,128)S(1)}, u32[]{:S(2)}, u32[]{:S(2)}) %collective-permute-start.22) | collective-permute-done | bytes 49184 | tf_op jit(solution)/shard_map/prefix/ppermute | solution.py:40
  134.5 11.7 %all_to_all.30 = bf16[8,16,768]{2,1,0:T(8,128)(2,1)S(1)} all-to-all(bf16[8,16,768]{2,1,0:T(8,128)(2,1)S(1)} %norm.1), channel_id=1, replica_groups=mesh['y'=4,'zl'=4,'c'=2,'x'=4,'zh'=2] {'zl','zh'}, dimensions={0} | all-to-all | bytes 393216 | tf_op jit(solution)/shard_map/gather/all_to_all | solution.py:314
  146.2 1.5 collective-permute-start.28
  148.8 6.0 %collective-permute-done.28.refs_3_ = bf16[128,768]{1,0:T(8,128)(2,1)S(1)} collective-permute-done((bf16[128,768]{1,0:T(8,128)(2,1)S(1)}, bf16[128,768]{1,0:T(8,128)(2,1)S(1)}, u32[]{:S(2)}, u32[]{:S(2)}) %collective-permute-start.28) | collective-permute-done | bytes 196640 | tf_op jit(solution)/shard_map/gather/ppermute | solution.py:40
  154.8 1.7 collective-permute-done.27.refs_2_
  156.5 2.0 collective-permute-done.26.refs_1_
  158.5 1.4 collective-permute-done.30.refs_5_
  159.9 7.8 %attention.3 = bf16[32,16,192]{2,1,0:T(8,128)(2,1)S(1)} custom-call(s32[4]{0:T(128)S(1)} %pad_add_fusion.1.place_ref, bf16[128,768]{1,0:T(8,128)(2,1)S(1)} %bitcast.62, bf16[128,768]{1,0:T(8,128)(2,1)S(1)} %collective-permute-done.26.refs_1_, bf16[128,768]{1,0:T(8,128)(2,1)S(1)} %collective-permute-done.27.refs_2_, ...), custom_call_target="tpu_custom_call" | custom-call | flops 1233125376 | bytes 4194304 | tf_op jit(solution)/shard_map/attention/pallas_call | solution.py:282
  167.7 18.6 %all_to_all.31.att_ref = bf16[32,16,192]{2,1,0:T(8,128)(2,1)S(1)} all-to-all(bf16[32,16,192]{2,1,0:T(8,128)(2,1)S(1)} %attention.3), channel_id=1, replica_groups=mesh['y'=4,'zl'=4,'c'=2,'x'=4,'zh'=2] {'zl','x','zh'}, dimensions={0} | all-to-all | bytes 393216 | tf_op jit(solution)/shard_map/to_prefix/all_to_all | solution.py:293
  187.7 2.1 collective-permute-start.34
  189.8 1.9 collective-permute-start.33
  191.8 4.0 %collective-permute-done.33.t1_ref = f32[16,768]{1,0:T(8,128)S(1)} collective-permute-done((f32[16,768]{1,0:T(8,128)S(1)}, f32[16,768]{1,0:T(8,128)S(1)}, u32[]{:S(2)}, u32[]{:S(2)}) %collective-permute-start.33) | collective-permute-done | bytes 49184 | tf_op jit(solution)/shard_map/prefix/ppermute | solution.py:40
  196.6 3.5 %all-to-all-start.5 = ((f32[8,16,768]{2,1,0:T(8,128)}), f32[8,16,768]{2,1,0:T(8,128)S(1)}, u32[]{:S(2)}, u32[]{:S(2)}) async-start(f32[8,16,768]{2,1,0:T(8,128)} %get-tuple-element.21), calls=%async_computation.5 | async-start | bytes 786432 | tf_op jit(solution)/shard_map/place/all_to_all | solution.py:318
  201.4 2.2 collective-permute-start.39
  205.0 3.7 %collective-permute-done.38 = f32[16,128]{1,0:T(8,128)S(1)} collective-permute-done((f32[16,128]{1,0:T(8,128)S(1)}, f32[16,128]{1,0:T(8,128)S(1)}, u32[]{:S(2)}, u32[]{:S(2)}) %collective-permute-start.38) | collective-permute-done | bytes 8224 | tf_op jit(solution)/shard_map/changes/ppermute | solution.py:40
  208.9 2.0 collective-permute-start.40
  210.9 1.8 collective-permute-done.40
  212.7 2.6 %collective-permute-start.41 = (f32[16,128]{1,0:T(8,128)S(1)}, f32[16,128]{1,0:T(8,128)S(1)}, u32[]{:S(2)}, u32[]{:S(2)}) collective-permute-start(f32[16,128]{1,0:T(8,128)S(1)} %max.25), channel_id=1, source_target_pairs={{0,32},{16,48},{32,0},{48,16},{1,33},{17,49},{33,1},{49,17},{2,34}... | collective-permute-start | bytes 24584 | tf_op jit(solution)/shard_map/changes/ppermute | solution.py:40
  215.3 1.9 collective-permute-done.41
  217.2 2.3 collective-permute-start.42
  219.5 5.3 %collective-permute-done.42 = f32[16,128]{1,0:T(8,128)S(1)} collective-permute-done((f32[16,128]{1,0:T(8,128)S(1)}, f32[16,128]{1,0:T(8,128)S(1)}, u32[]{:S(2)}, u32[]{:S(2)}) %collective-permute-start.42) | collective-permute-done | bytes 8224 | tf_op jit(solution)/shard_map/changes/ppermute | solution.py:40
  (118 shorter events, 29.2 us)
Async XLA Ops:
  2.4 44.3 %collective-permute-start.14 = (bf16[48,576]{1,0:T(8,128)(2,1)S(1)}, bf16[48,576]{1,0:T(8,128)(2,1)S(1)}, u32[]{:S(2)}, u32[]{:S(2)}) collective-permute-start(bf16[48,576]{1,0:T(8,128)(2,1)S(1)} %concatenate.40), channel_id=1, source_target_pairs={{8,1},{9,8},{10,3},{11,10},{12,5},{13,12},{14,7},{15,14},{24,17},{... | collective-permute-start | bytes 165896 | tf_op jit(solution)/shard_map/weights/ppermute | solution.py:40
  3.1 43.6 %collective-permute-start.13 = (bf16[48,576]{1,0:T(8,128)(2,1)S(1)}, bf16[48,576]{1,0:T(8,128)(2,1)}, u32[]{:S(2)}, u32[]{:S(2)}) collective-permute-start(bf16[48,576]{1,0:T(8,128)(2,1)S(1)} %concatenate.40), channel_id=1, source_target_pairs={{0,1},{1,8},{2,3},{3,10},{4,5},{5,12},{6,7},{7,14},{16,17},{17,24}... | collective-permute-start | bytes 165896 | tf_op jit(solution)/shard_map/weights/ppermute | solution.py:40
  13.4 33.3 %collective-permute-start.12 = (bf16[48,576]{1,0:T(8,128)(2,1)S(1)}, bf16[48,576]{1,0:T(8,128)(2,1)}, u32[]{:S(2)}, u32[]{:S(2)}) collective-permute-start(bf16[48,576]{1,0:T(8,128)(2,1)S(1)} %concatenate.40), channel_id=1, source_target_pairs={{1,9},{8,0},{3,11},{10,2},{5,13},{12,4},{7,15},{14,6},{17,25},{24,... | collective-permute-start | bytes 165896 | tf_op jit(solution)/shard_map/weights/ppermute | solution.py:40
  14.7 14.7 %collective-permute-start = (s32[1,1]{1,0:T(1,128)}, s32[1,1]{1,0:T(1,128)}, u32[]{:S(2)}, u32[]{:S(2)}) collective-permute-start(s32[1,1]{1,0:T(1,128)} %bitcast.1), channel_id=1, source_target_pairs={{0,8},{8,0},{1,9},{9,1},{2,10},{10,2},{3,11},{11,3},{4,12},{12,4},... | collective-permute-start | bytes 20 | tf_op jit(solution)/shard_map/plan/ppermute | solution.py:40
  18.5 48.9 %all-to-all-start = ((bf16[8,2,40,192]{3,2,1,0:T(8,128)(2,1)}), bf16[8,2,40,192]{3,2,1,0:T(8,128)(2,1)}, u32[]{:S(2)}, u32[]{:S(2)}) async-start(bf16[8,2,40,192]{3,2,1,0:T(8,128)(2,1)} %copy.17), calls=%async_computation | async-start | bytes 655360 | tf_op jit(solution)/shard_map/text/all_to_all | solution.py:258
  28.6 25.7 %collective-permute-start.4 = (bf16[64,1536]{1,0:T(8,128)(2,1)S(1)}, bf16[64,1536]{1,0:T(8,128)(2,1)S(1)}, u32[]{:S(2)}, u32[]{:S(2)}) collective-permute-start(bf16[64,1536]{1,0:T(8,128)(2,1)S(1)} %get-tuple-element.13), channel_id=1, source_target_pairs={{1,8},{8,1},{3,10},{10,3},{5,12},{12,5},{7,14},{14,7},{17,24},{24,... | collective-permute-start | bytes 589832 | tf_op jit(solution)/shard_map/gather_first/ppermute | solution.py:40
  30.1 6.0 %collective-permute-start.3 = (s32[1,2]{1,0:T(1,128)S(1)}, s32[1,2]{1,0:T(1,128)S(1)}, u32[]{:S(2)}, u32[]{:S(2)}) collective-permute-start(s32[1,2]{1,0:T(1,128)S(1)} %broadcast_select_fusion.2), channel_id=1, source_target_pairs={{0,48},{16,0},{32,16},{48,32},{1,49},{17,1},{33,17},{49,33},{2,50}... | collective-permute-start | bytes 32 | tf_op jit(solution)/shard_map/plan/ppermute | solution.py:40
  36.1 4.4 %collective-permute-start.2 = (s32[1,2]{1,0:T(1,128)S(1)}, s32[1,2]{1,0:T(1,128)S(1)}, u32[]{:S(2)}, u32[]{:S(2)}) collective-permute-start(s32[1,2]{1,0:T(1,128)S(1)} %broadcast_select_fusion.2), channel_id=1, source_target_pairs={{0,32},{16,48},{32,0},{48,16},{1,33},{17,49},{33,1},{49,17},{2,34}... | collective-permute-start | bytes 32 | tf_op jit(solution)/shard_map/plan/ppermute | solution.py:40
  40.5 5.3 %collective-permute-start.1 = (s32[1,2]{1,0:T(1,128)S(1)}, s32[1,2]{1,0:T(1,128)S(1)}, u32[]{:S(2)}, u32[]{:S(2)}) collective-permute-start(s32[1,2]{1,0:T(1,128)S(1)} %broadcast_select_fusion.2), channel_id=1, source_target_pairs={{0,16},{16,32},{32,48},{48,0},{1,17},{17,33},{33,49},{49,1},{2,18}... | collective-permute-start | bytes 32 | tf_op jit(solution)/shard_map/plan/ppermute | solution.py:40
  47.6 10.3 %collective-permute-start.16 = (bf16[96,576]{1,0:T(8,128)(2,1)S(1)}, bf16[96,576]{1,0:T(8,128)(2,1)S(1)}, u32[]{:S(2)}, u32[]{:S(2)}) collective-permute-start(bf16[96,576]{1,0:T(8,128)(2,1)S(1)} %get-tuple-element.37), channel_id=1, source_target_pairs={{0,32},{1,33},{16,48},{17,49},{32,1},{33,0},{48,17},{49,16},{2,34}... | collective-permute-start | bytes 331784 | tf_op jit(solution)/shard_map/weights/ppermute | solution.py:40
  47.7 13.9 %collective-permute-start.15 = (bf16[96,576]{1,0:T(8,128)(2,1)S(1)}, bf16[96,576]{1,0:T(8,128)(2,1)S(1)}, u32[]{:S(2)}, u32[]{:S(2)}) collective-permute-start(bf16[96,576]{1,0:T(8,128)(2,1)S(1)} %get-tuple-element.37), channel_id=1, source_target_pairs={{0,16},{1,17},{16,32},{17,33},{32,48},{33,49},{48,1},{49,0},{2,18}... | collective-permute-start | bytes 331784 | tf_op jit(solution)/shard_map/weights/ppermute | solution.py:40
  48.0 13.6 %collective-permute-start.17 = (bf16[96,576]{1,0:T(8,128)(2,1)S(1)}, bf16[96,576]{1,0:T(8,128)(2,1)S(1)}, u32[]{:S(2)}, u32[]{:S(2)}) collective-permute-start(bf16[96,576]{1,0:T(8,128)(2,1)S(1)} %get-tuple-element.37), channel_id=1, source_target_pairs={{0,49},{1,48},{16,0},{17,1},{32,16},{33,17},{48,32},{49,33},{2,51}... | collective-permute-start | bytes 331784 | tf_op jit(solution)/shard_map/weights/ppermute | solution.py:40
  54.3 17.1 %collective-permute-start.10 = (bf16[64,1536]{1,0:T(8,128)(2,1)S(1)}, bf16[64,1536]{1,0:T(8,128)(2,1)}, u32[]{:S(2)}, u32[]{:S(2)}) collective-permute-start(bf16[64,1536]{1,0:T(8,128)(2,1)S(1)} %broadcast_select_fusion.refs_0_), channel_id=1, source_target_pairs={{0,6},{2,0},{4,2},{6,4},{1,7},{3,1},{5,3},{7,5},{8,14},{10,8},{12,... | collective-permute-start | bytes 589832 | tf_op jit(solution)/shard_map/gather_first/ppermute | solution.py:40
  57.1 15.9 %collective-permute-start.8 = (bf16[64,1536]{1,0:T(8,128)(2,1)S(1)}, bf16[64,1536]{1,0:T(8,128)(2,1)}, u32[]{:S(2)}, u32[]{:S(2)}) collective-permute-start(bf16[64,1536]{1,0:T(8,128)(2,1)S(1)} %broadcast_select_fusion.refs_0_), channel_id=1, source_target_pairs={{0,4},{2,6},{4,0},{6,2},{1,5},{3,7},{5,1},{7,3},{8,12},{10,14},{12... | collective-permute-start | bytes 589832 | tf_op jit(solution)/shard_map/gather_first/ppermute | solution.py:40
  61.7 20.5 %collective-permute-start.20 = (bf16[4,96,576]{2,1,0:T(8,128)(2,1)S(1)}, bf16[4,96,576]{2,1,0:T(8,128)(2,1)}, u32[]{:S(2)}, u32[]{:S(2)}) collective-permute-start(bf16[4,96,576]{2,1,0:T(8,128)(2,1)S(1)} %pad_maximum_fusion.refs_0_), channel_id=1, source_target_pairs={{0,192},{64,0},{128,64},{192,128},{1,193},{65,1},{129,65},{193,129... | collective-permute-start | bytes 1327112 | tf_op jit(solution)/shard_map/weights/ppermute | solution.py:40
  62.2 22.8 %collective-permute-start.19 = (bf16[4,96,576]{2,1,0:T(8,128)(2,1)S(1)}, bf16[4,96,576]{2,1,0:T(8,128)(2,1)}, u32[]{:S(2)}, u32[]{:S(2)}) collective-permute-start(bf16[4,96,576]{2,1,0:T(8,128)(2,1)S(1)} %pad_maximum_fusion.refs_0_), channel_id=1, source_target_pairs={{0,128},{64,192},{128,0},{192,64},{1,129},{65,193},{129,1},{193,65... | collective-permute-start | bytes 1327112 | tf_op jit(solution)/shard_map/weights/ppermute | solution.py:40
  64.8 21.0 %collective-permute-start.18 = (bf16[4,96,576]{2,1,0:T(8,128)(2,1)S(1)}, bf16[4,96,576]{2,1,0:T(8,128)(2,1)}, u32[]{:S(2)}, u32[]{:S(2)}) collective-permute-start(bf16[4,96,576]{2,1,0:T(8,128)(2,1)S(1)} %pad_maximum_fusion.refs_0_), channel_id=1, source_target_pairs={{0,64},{64,128},{128,192},{192,0},{1,65},{65,129},{129,193},{193,1... | collective-permute-start | bytes 1327112 | tf_op jit(solution)/shard_map/weights/ppermute | solution.py:40
  67.4 31.8 %all-to-all-start.2 = ((f32[8,16,768]{2,1,0:T(8,128)}), f32[8,16,768]{2,1,0:T(8,128)S(1)}, u32[]{:S(2)}, u32[]{:S(2)}) async-start(f32[8,16,768]{2,1,0:T(8,128)} %copy-done.4), calls=%async_computation.2 | async-start | bytes 786432 | tf_op jit(solution)/shard_map/states/all_to_all | solution.py:276
  71.4 8.6 %collective-permute-start.6 = (bf16[64,1536]{1,0:T(8,128)(2,1)S(1)}, bf16[64,1536]{1,0:T(8,128)(2,1)}, u32[]{:S(2)}, u32[]{:S(2)}) collective-permute-start(bf16[64,1536]{1,0:T(8,128)(2,1)S(1)} %broadcast_select_fusion.refs_0_), channel_id=1, source_target_pairs={{0,2},{2,4},{4,6},{6,0},{1,3},{3,5},{5,7},{7,1},{8,10},{10,12},{12... | collective-permute-start | bytes 589832 | tf_op jit(solution)/shard_map/gather_first/ppermute | solution.py:40
  72.9 14.4 %collective-permute-start.21 = (bf16[8,2,40,192]{3,2,1,0:T(8,128)(2,1)}, bf16[8,2,40,192]{3,2,1,0:T(8,128)(2,1)}, u32[]{:S(2)}, u32[]{:S(2)}) collective-permute-start(bf16[8,2,40,192]{3,2,1,0:T(8,128)(2,1)} %all-to-all-done), channel_id=1, source_target_pairs={{1,8},{8,1},{3,10},{10,3},{5,12},{12,5},{7,14},{14,7},{17,24},{24,... | collective-permute-start | bytes 737288 | tf_op jit(solution)/shard_map/text/ppermute | solution.py:40
  80.0 8.4 %collective-permute-start.5 = (bf16[64,1536]{1,0:T(8,128)(2,1)S(1)}, bf16[64,1536]{1,0:T(8,128)(2,1)S(1)}, u32[]{:S(2)}, u32[]{:S(2)}) collective-permute-start(bf16[64,1536]{1,0:T(8,128)(2,1)S(1)} %broadcast_select_fusion.refs_0_), channel_id=1, source_target_pairs={{0,8},{8,0},{1,9},{9,1},{2,10},{10,2},{3,11},{11,3},{4,12},{12,4},... | collective-permute-start | bytes 589832 | tf_op jit(solution)/shard_map/gather_first/ppermute | solution.py:40
  82.2 6.2 %collective-permute-start.11 = (bf16[64,1536]{1,0:T(8,128)(2,1)}, bf16[64,1536]{1,0:T(8,128)(2,1)S(1)}, u32[]{:S(2)}, u32[]{:S(2)}) collective-permute-start(bf16[64,1536]{1,0:T(8,128)(2,1)} %collective-permute-done.10.refs_6_), channel_id=1, source_target_pairs={{0,8},{8,0},{1,9},{9,1},{2,10},{10,2},{3,11},{11,3},{4,12},{12,4},... | collective-permute-start | bytes 589832 | tf_op jit(solution)/shard_map/gather_first/ppermute | solution.py:40
  85.0 3.4 %collective-permute-start.9 = (bf16[64,1536]{1,0:T(8,128)(2,1)}, bf16[64,1536]{1,0:T(8,128)(2,1)S(1)}, u32[]{:S(2)}, u32[]{:S(2)}) collective-permute-start(bf16[64,1536]{1,0:T(8,128)(2,1)} %collective-permute-done.8.refs_4_), channel_id=1, source_target_pairs={{0,8},{8,0},{1,9},{9,1},{2,10},{10,2},{3,11},{11,3},{4,12},{12,4},... | collective-permute-start | bytes 589832 | tf_op jit(solution)/shard_map/gather_first/ppermute | solution.py:40
  85.8 2.6 %collective-permute-start.7 = (bf16[64,1536]{1,0:T(8,128)(2,1)}, bf16[64,1536]{1,0:T(8,128)(2,1)S(1)}, u32[]{:S(2)}, u32[]{:S(2)}) collective-permute-start(bf16[64,1536]{1,0:T(8,128)(2,1)} %collective-permute-done.6.refs_2_), channel_id=1, source_target_pairs={{0,8},{8,0},{1,9},{9,1},{2,10},{10,2},{3,11},{11,3},{4,12},{12,4},... | collective-permute-start | bytes 589832 | tf_op jit(solution)/shard_map/gather_first/ppermute | solution.py:40
  99.1 60.8 %copy-start.6 = (bf16[1,8,40,192]{3,2,0,1:T(8,128)(2,1)S(1)}, bf16[1,8,40,192]{3,2,0,1:T(8,128)(2,1)}, u32[]{:S(2)}) copy-start(bf16[1,8,40,192]{3,2,0,1:T(8,128)(2,1)} %copy-done.5) | copy-start | bytes 368644
  99.1 22.5 %all-to-all-start.1 = ((bf16[32,16,192]{2,1,0:T(8,128)(2,1)}), bf16[32,16,192]{2,1,0:T(8,128)(2,1)S(1)}, u32[]{:S(2)}, u32[]{:S(2)}) async-start(bf16[32,16,192]{2,1,0:T(8,128)(2,1)} %attention.2), calls=%async_computation.1 | async-start | bytes 524288 | tf_op jit(solution)/shard_map/to_prefix/all_to_all | solution.py:293
  122.3 6.4 %collective-permute-start.24 = (f32[16,768]{1,0:T(8,128)S(1)}, f32[16,768]{1,0:T(8,128)S(1)}, u32[]{:S(2)}, u32[]{:S(2)}) collective-permute-start(f32[16,768]{1,0:T(8,128)S(1)} %get-tuple-element.16), channel_id=1, source_target_pairs={{0,192},{1,193},{2,194},{3,195},{4,196},{5,197},{6,198},{7,199},{8... | collective-permute-start | bytes 147464 | tf_op jit(solution)/shard_map/prefix/ppermute | solution.py:40
  122.9 5.7 %collective-permute-start.23 = (f32[16,768]{1,0:T(8,128)S(1)}, f32[16,768]{1,0:T(8,128)S(1)}, u32[]{:S(2)}, u32[]{:S(2)}) collective-permute-start(f32[16,768]{1,0:T(8,128)S(1)} %get-tuple-element.16), channel_id=1, source_target_pairs={{0,128},{64,192},{1,129},{65,193},{2,130},{66,194},{3,131},{67,195... | collective-permute-start | bytes 147464 | tf_op jit(solution)/shard_map/prefix/ppermute | solution.py:40
  126.7 6.0 %collective-permute-start.22 = (f32[16,768]{1,0:T(8,128)S(1)}, f32[16,768]{1,0:T(8,128)S(1)}, u32[]{:S(2)}, u32[]{:S(2)}) collective-permute-start(f32[16,768]{1,0:T(8,128)S(1)} %get-tuple-element.16), channel_id=1, source_target_pairs={{0,64},{64,128},{128,192},{1,65},{65,129},{129,193},{2,66},{66,130... | collective-permute-start | bytes 147464 | tf_op jit(solution)/shard_map/prefix/ppermute | solution.py:40
  132.9 1.3 collective-permute-start.25
  146.2 8.6 %collective-permute-start.28 = (bf16[128,768]{1,0:T(8,128)(2,1)S(1)}, bf16[128,768]{1,0:T(8,128)(2,1)S(1)}, u32[]{:S(2)}, u32[]{:S(2)}) collective-permute-start(bf16[128,768]{1,0:T(8,128)(2,1)S(1)} %bitcast.58), channel_id=1, source_target_pairs={{0,6},{2,0},{4,2},{6,4},{1,7},{3,1},{5,3},{7,5},{8,14},{10,8},{12,... | collective-permute-start | bytes 589832 | tf_op jit(solution)/shard_map/gather/ppermute | solution.py:40
  147.7 8.8 %collective-permute-start.27 = (bf16[128,768]{1,0:T(8,128)(2,1)S(1)}, bf16[128,768]{1,0:T(8,128)(2,1)S(1)}, u32[]{:S(2)}, u32[]{:S(2)}) collective-permute-start(bf16[128,768]{1,0:T(8,128)(2,1)S(1)} %bitcast.59), channel_id=1, source_target_pairs={{0,4},{2,6},{4,0},{6,2},{1,5},{3,7},{5,1},{7,3},{8,12},{10,14},{12... | collective-permute-start | bytes 589832 | tf_op jit(solution)/shard_map/gather/ppermute | solution.py:40
  148.8 9.7 %collective-permute-start.26 = (bf16[128,768]{1,0:T(8,128)(2,1)S(1)}, bf16[128,768]{1,0:T(8,128)(2,1)S(1)}, u32[]{:S(2)}, u32[]{:S(2)}) collective-permute-start(bf16[128,768]{1,0:T(8,128)(2,1)S(1)} %bitcast.60), channel_id=1, source_target_pairs={{0,2},{2,4},{4,6},{6,0},{1,3},{3,5},{5,7},{7,1},{8,10},{10,12},{12... | collective-permute-start | bytes 589832 | tf_op jit(solution)/shard_map/gather/ppermute | solution.py:40
  148.8 9.7 %collective-permute-start.29 = (bf16[128,768]{1,0:T(8,128)(2,1)S(1)}, bf16[128,768]{1,0:T(8,128)(2,1)S(1)}, u32[]{:S(2)}, u32[]{:S(2)}) collective-permute-start(bf16[128,768]{1,0:T(8,128)(2,1)S(1)} %bitcast.61), channel_id=1, source_target_pairs={{0,8},{8,0},{1,9},{9,1},{2,10},{10,2},{3,11},{11,3},{4,12},{12,4},... | collective-permute-start | bytes 589832 | tf_op jit(solution)/shard_map/gather/ppermute | solution.py:40
  154.8 3.7 %collective-permute-start.32 = (bf16[128,768]{1,0:T(8,128)(2,1)S(1)}, bf16[128,768]{1,0:T(8,128)(2,1)S(1)}, u32[]{:S(2)}, u32[]{:S(2)}) collective-permute-start(bf16[128,768]{1,0:T(8,128)(2,1)S(1)} %collective-permute-done.28.refs_3_), channel_id=1, source_target_pairs={{0,8},{8,0},{1,9},{9,1},{2,10},{10,2},{3,11},{11,3},{4,12},{12,4},... | collective-permute-start | bytes 589832 | tf_op jit(solution)/shard_map/gather/ppermute | solution.py:40
  156.5 2.0 collective-permute-start.31
  158.5 1.4 collective-permute-start.30
  187.0 4.7 %collective-permute-start.35 = (f32[16,768]{1,0:T(8,128)S(1)}, f32[16,768]{1,0:T(8,128)S(1)}, u32[]{:S(2)}, u32[]{:S(2)}) collective-permute-start(f32[16,768]{1,0:T(8,128)S(1)} %get-tuple-element.20), channel_id=1, source_target_pairs={{0,192},{1,193},{2,194},{3,195},{4,196},{5,197},{6,198},{7,199},{8... | collective-permute-start | bytes 147464 | tf_op jit(solution)/shard_map/prefix/ppermute | solution.py:40
  187.7 4.1 %collective-permute-start.34 = (f32[16,768]{1,0:T(8,128)S(1)}, f32[16,768]{1,0:T(8,128)S(1)}, u32[]{:S(2)}, u32[]{:S(2)}) collective-permute-start(f32[16,768]{1,0:T(8,128)S(1)} %get-tuple-element.20), channel_id=1, source_target_pairs={{0,128},{64,192},{1,129},{65,193},{2,130},{66,194},{3,131},{67,195... | collective-permute-start | bytes 147464 | tf_op jit(solution)/shard_map/prefix/ppermute | solution.py:40
  189.8 6.0 %collective-permute-start.33 = (f32[16,768]{1,0:T(8,128)S(1)}, f32[16,768]{1,0:T(8,128)S(1)}, u32[]{:S(2)}, u32[]{:S(2)}) collective-permute-start(f32[16,768]{1,0:T(8,128)S(1)} %get-tuple-element.20), channel_id=1, source_target_pairs={{0,64},{64,128},{128,192},{1,65},{65,129},{129,193},{2,66},{66,130... | collective-permute-start | bytes 147464 | tf_op jit(solution)/shard_map/prefix/ppermute | solution.py:40
  196.6 29.1 %all-to-all-start.5 = ((f32[8,16,768]{2,1,0:T(8,128)}), f32[8,16,768]{2,1,0:T(8,128)S(1)}, u32[]{:S(2)}, u32[]{:S(2)}) async-start(f32[8,16,768]{2,1,0:T(8,128)} %get-tuple-element.21), calls=%async_computation.5 | async-start | bytes 786432 | tf_op jit(solution)/shard_map/place/all_to_all | solution.py:318
  200.1 1.3 collective-permute-start.36
  201.4 3.7 %collective-permute-start.39 = (f32[16,128]{1,0:T(8,128)S(1)}, f32[16,128]{1,0:T(8,128)S(1)}, u32[]{:S(2)}, u32[]{:S(2)}) collective-permute-start(f32[16,128]{1,0:T(8,128)S(1)} %max.21), channel_id=1, source_target_pairs={{0,6},{2,0},{4,2},{6,4},{1,7},{3,1},{5,3},{7,5},{8,14},{10,8},{12,... | collective-permute-start | bytes 24584 | tf_op jit(solution)/shard_map/changes/ppermute | solution.py:40
  203.6 5.2 %collective-permute-start.38 = (f32[16,128]{1,0:T(8,128)S(1)}, f32[16,128]{1,0:T(8,128)S(1)}, u32[]{:S(2)}, u32[]{:S(2)}) collective-permute-start(f32[16,128]{1,0:T(8,128)S(1)} %max.21), channel_id=1, source_target_pairs={{0,4},{2,6},{4,0},{6,2},{1,5},{3,7},{5,1},{7,3},{8,12},{10,14},{12... | collective-permute-start | bytes 24584 | tf_op jit(solution)/shard_map/changes/ppermute | solution.py:40
  204.0 4.9 %collective-permute-start.37 = (f32[16,128]{1,0:T(8,128)S(1)}, f32[16,128]{1,0:T(8,128)S(1)}, u32[]{:S(2)}, u32[]{:S(2)}) collective-permute-start(f32[16,128]{1,0:T(8,128)S(1)} %max.21), channel_id=1, source_target_pairs={{0,2},{2,4},{4,6},{6,0},{1,3},{3,5},{5,7},{7,1},{8,10},{10,12},{12... | collective-permute-start | bytes 24584 | tf_op jit(solution)/shard_map/changes/ppermute | solution.py:40
  208.9 3.8 %collective-permute-start.40 = (f32[16,128]{1,0:T(8,128)S(1)}, f32[16,128]{1,0:T(8,128)S(1)}, u32[]{:S(2)}, u32[]{:S(2)}) collective-permute-start(f32[16,128]{1,0:T(8,128)S(1)} %maximum_maximum_fusion), channel_id=1, source_target_pairs={{0,16},{16,0},{32,48},{48,32},{1,17},{17,1},{33,49},{49,33},{2,18}... | collective-permute-start | bytes 24584 | tf_op jit(solution)/shard_map/changes/ppermute | solution.py:40
  212.7 4.5 %collective-permute-start.41 = (f32[16,128]{1,0:T(8,128)S(1)}, f32[16,128]{1,0:T(8,128)S(1)}, u32[]{:S(2)}, u32[]{:S(2)}) collective-permute-start(f32[16,128]{1,0:T(8,128)S(1)} %max.25), channel_id=1, source_target_pairs={{0,32},{16,48},{32,0},{48,16},{1,33},{17,49},{33,1},{49,17},{2,34}... | collective-permute-start | bytes 24584 | tf_op jit(solution)/shard_map/changes/ppermute | solution.py:40
  217.2 7.6 %collective-permute-start.42 = (f32[16,128]{1,0:T(8,128)S(1)}, f32[16,128]{1,0:T(8,128)S(1)}, u32[]{:S(2)}, u32[]{:S(2)}) collective-permute-start(f32[16,128]{1,0:T(8,128)S(1)} %max.26), channel_id=1, source_target_pairs={{0,1},{1,0},{2,3},{3,2},{4,5},{5,4},{6,7},{7,6},{8,9},{9,8},{10,11... | collective-permute-start | bytes 24584 | tf_op jit(solution)/shard_map/changes/ppermute | solution.py:40
  (7 other events, 144.1 us)

commit v2 on v1

v2 whole, which is shorter than its diff:
```python
import functools
import itertools

import jax
import jax.numpy as jnp
from jax import lax
from jax.experimental import pallas as pl
from jax.experimental.pallas import tpu as pltpu
from jax.sharding import Mesh, PartitionSpec as P

AXES = ("y", "zl", "c", "x", "zh")
SIZES = {"y": 4, "zl": 4, "c": 2, "x": 4, "zh": 2}

HEAD_DIM = 64
SWEEPS = 2
D = 1536
HALF = 768
BLOCK = 384
HW = 192
ROWS = 64
TOK = 512
TXT = 320
KEYS = TOK + TXT
MIB = 1024 * 1024
f32, bf16 = jnp.float32, jnp.bfloat16


def permute(value, axes, move):
    def index(place):
        flat = 0
        for name in axes:
            flat = flat * SIZES[name] + place[name] % SIZES[name]
        return flat

    pairs = []
    for coords in itertools.product(*[range(SIZES[name]) for name in axes]):
        place = dict(zip(axes, coords))
        target = move(dict(place))
        if target is not None:
            pairs.append((index(place), index(target)))
    return lax.ppermute(value, axes if len(axes) > 1 else axes[0], pairs)


def shift(value, axis, amount):
    return permute(value, (axis,), lambda p: {axis: p[axis] + amount})


def shift_z(value, amount):
    def move(p):
        ring = (p["zh"] * 4 + p["zl"] + amount) % 8
        return {"zl": ring % 4, "zh": ring // 4}

    return permute(value, ("zl", "zh"), move)


def swap_core_zh(value, same):
    moved = permute(
        value, ("c", "zh"),
        lambda p: None if p["c"] == p["zh"] else {"c": p["zh"], "zh": p["c"]},
    )
    return jnp.where(same, value, moved)


def call(kernel, out_shape, n_vmem, n_smem, limit=6, after=0):
    return pl.pallas_call(
        kernel,
        out_shape=out_shape,
        in_specs=[pl.BlockSpec(memory_space=pltpu.SMEM)] * n_smem
        + [pl.BlockSpec(memory_space=pltpu.VMEM)] * n_vmem
        + [pl.BlockSpec(memory_space=pl.ANY)] * after,
        out_specs=jax.tree.map(lambda _: pl.BlockSpec(memory_space=pltpu.VMEM), out_shape),
        compiler_params=pltpu.CompilerParams(vmem_limit_bytes=limit * MIB),
    )


def struct(*shape, dtype=f32):
    return jax.ShapeDtypeStruct(shape, dtype)


def half_columns(half):
    return [slice(k * 2 * HW + half * HW, k * 2 * HW + (half + 1) * HW) for k in range(4)]


def columns_kernel(w_ref, after_ref, out_ref):
    raw = w_ref[...].astype(f32)
    parts = [raw[:, k, :128] for k in range(3)] + [raw[:, k, 128:] for k in range(3)]
    out_ref[...] = jnp.concatenate(parts, axis=1).astype(bf16)


def start_kernel(place_ref, ids_ref, steps_ref, lat_ref, mod_ref, text_ref,
                 out_ref, keep_ref, mate_ref):
    latent = lat_ref[0]
    average = jnp.mean(latent, axis=-1, keepdims=True)
    centred = latent - average
    variance = jnp.mean(centred * centred, axis=-1, keepdims=True)
    normed = centred * lax.rsqrt(variance + 1e-06)
    modulated = (normed * (1.0 + mod_ref[1:2, :]) + mod_ref[0:1, :]).astype(bf16)
    raw = text_ref[0].astype(f32)
    rows = jnp.concatenate([raw[:, 0, :], raw[:, 1, :]], axis=0).astype(bf16)
    step = jnp.full((5, HALF), -steps_ref[ids_ref[0]], f32)
    for half in range(2):
        piece = jnp.concatenate([modulated[:, s] for s in half_columns(half)], axis=1)
        out_ref[half * 2, 0:64] = piece[:, 0:BLOCK]
        out_ref[half * 2 + 1, 0:64] = piece[:, BLOCK:]
        piece = jnp.concatenate([latent[:, s] for s in half_columns(half)], axis=1)
        mods = jnp.concatenate([mod_ref[:, s] for s in half_columns(half)], axis=1)
        below = jnp.concatenate([mods, step], axis=0)
        for ref, wanted in ((keep_ref, place_ref[2]), (mate_ref, 1 - place_ref[2])):
            @pl.when(wanted == half)
            def _(ref=ref, piece=piece, below=below):
                for sub in range(4):
                    ref[sub, 0:16] = piece[sub * 16:(sub + 1) * 16]
                    ref[sub, 16:24] = below
    for k in range(4):
        out_ref[k, 64:144] = rows[:, k * BLOCK:(k + 1) * BLOCK]


def hold_kernel(in_ref, *refs):
    refs[-1][...] = in_ref[...]


def message_kernel(place_ref, keep_ref, mate_ref, after_ref, *out_refs):
    zl, core = place_ref[1], place_ref[2]
    for k in range(4):
        target = lax.rem(zl + k, 4)
        out_refs[k][core] = keep_ref[target]
        out_refs[k][1 - core] = mate_ref[target]


def send_kernel(place_ref, in_ref, *out_refs):
    x = place_ref[3]
    for k in range(4):
        for block in range(4):
            out_refs[k][block * 64:(block + 1) * 64] = in_ref[block, 0:64]
        out_refs[k][256:336] = in_ref[lax.rem(x + k, 4), 64:144]


def weight_rows(place_ref):
    y, zl = place_ref[0], place_ref[1]
    for ky in range(4):
        from_y = lax.rem(y - ky + 4, 4)
        for kz in range(4):
            from_zl = lax.rem(zl - kz + 4, 4)
            row = (from_zl // 2) * HALF + from_y * HW + lax.rem(from_zl, 2) * 96
            yield ky, kz, pl.ds(pl.multiple_of(row, 32), 96)


def weight_piece(pieces, ky, kz):
    own, after, far_a, far_b, last = pieces
    if ky == 2:
        return (far_a if kz < 2 else far_b).at[kz % 2]
    return (own, after, None, last)[ky].at[kz]


def weight_kernel(place_ref, *refs):
    for ky, kz, rows in weight_rows(place_ref):
        refs[-1][rows, :] = weight_piece(refs[:5], ky, kz)[...]


def attention_kernel(first, place_ref, *refs):
    blocks, refs = refs[:8], refs[8:]
    if first:
        w_ref, out_ref, keep_ref, k01, v01, k2, v2, q01, q2 = refs
    else:
        w_ref, text_ref, out_ref, k01, v01, k2, v2, q01, q2 = refs
    core, x = place_ref[2], place_ref[3]
    if first:
        rows = jnp.concatenate([
            jnp.concatenate([blocks[k + e * 4][n * 64:(n + 1) * 64] for n in range(4)], axis=1)
            for k in range(4) for e in range(2)
        ], axis=0)
        for which in range(2):
            span = slice(256 + which * 40, 256 + (which + 1) * 40)
            text = jnp.concatenate([b[span].astype(f32) for b in blocks], axis=0)
            keep_ref[which] = jnp.where(core == 0, text[:, :HW], text[:, HW:]).astype(bf16)
        text_ref = keep_ref
        qkv = jnp.dot(rows, w_ref[...], preferred_element_type=f32)
    else:
        mine = jnp.concatenate([b[...] for b in blocks[:4]], axis=0)
        other = jnp.concatenate([b[...] for b in blocks[4:]], axis=0)
        w_mine = w_ref[pl.ds(pl.multiple_of(core * HALF, HALF), HALF), :]
        w_other = w_ref[pl.ds(pl.multiple_of((1 - core) * HALF, HALF), HALF), :]
        qkv = jnp.dot(mine, w_mine, preferred_element_type=f32)
        qkv = qkv + jnp.dot(other, w_other, preferred_element_type=f32)
    scale = HEAD_DIM ** (-0.5)
    q01[...] = (qkv[:, 0:128] * scale).astype(bf16)
    k01[0:TOK, :] = qkv[:, 128:256].astype(bf16)
    v01[0:TOK, :] = qkv[:, 256:384].astype(bf16)
    q2[...] = (qkv[:, 384:448] * scale).astype(bf16)
    k2[0:TOK, :] = qkv[:, 448:512].astype(bf16)
    v2[0:TOK, :] = qkv[:, 512:576].astype(bf16)
    k01[TOK:, :] = text_ref[0, :, 0:128]
    v01[TOK:, :] = text_ref[1, :, 0:128]
    k2[TOK:, :] = text_ref[0, :, 128:192]
    v2[TOK:, :] = text_ref[1, :, 128:192]
    lane = lax.broadcasted_iota(jnp.int32, (128, 128), 1)

    def attend(query, keys, values):
        scores = lax.dot_general(
            query, keys, (((1,), (1,)), ((), ())), preferred_element_type=f32
        )
        top = jnp.max(scores, axis=-1, keepdims=True)
        exp_scores = jnp.exp(scores - top)
        total = jnp.sum(exp_scores, axis=-1, keepdims=True)
        weights = (exp_scores * (1.0 / total)).astype(bf16)
        return jnp.dot(weights, values, preferred_element_type=f32)

    for chunk in range(4):
        span = slice(chunk * 128, (chunk + 1) * 128)
        pair = q01[span, :]
        zero = jnp.zeros_like(pair)
        out0 = attend(jnp.where(lane < 64, pair, zero), k01[...], v01[...])
        out1 = attend(jnp.where(lane < 64, zero, pair), k01[...], v01[...])
        out01 = jnp.where(lane < 64, out0, out1).astype(bf16)
        out2 = attend(q2[span, :], k2[...], v2[...])
        from_x = lax.rem(x - chunk + 4, 4)
        for part in range(8):
            if first:
                sub = part % 4
                zh = core if part < 4 else 1 - core
            else:
                sub, zh = part // 2, part % 2
            target = (sub * 4 + from_x) * 2 + zh
            out_ref[target, 0:16] = out01[part * 16:(part + 1) * 16]
            out_ref[target, 16:24] = jnp.concatenate(
                [out2[part * 16:part * 16 + 8], out2[part * 16 + 8:(part + 1) * 16]], axis=1
            ).astype(bf16)


def terms_kernel(first, place_ref, att_ref, *refs):
    if first:
        messages, (part_ref, total_ref, mod_ref) = refs[:4], refs[4:]
        for k in range(4):
            from_zl = lax.rem(place_ref[1] - k + 4, 4)
            for core in range(2):
                mod_ref[from_zl * 2 + core] = messages[k][core]
        lat_ref = mod_ref
    else:
        lat_ref, mod_ref, part_ref, total_ref = refs
    run = jnp.where(place_ref[0] == 0, lat_ref[0, 0:16], 0.0)
    for j in range(8):
        part_ref[j] = run
        sub, zh = j // 2, j % 2
        pieces = []
        for k in range(4):
            piece = att_ref[(sub * 4 + k) * 2 + zh].astype(f32)
            tail = jnp.concatenate([piece[16:24, 0:64], piece[16:24, 64:128]], axis=0)
            pieces += [piece[0:16], tail]
        attended = jnp.concatenate(pieces, axis=1)
        run = run + mod_ref[j, 19:20] * (lat_ref[j, 0:16] + mod_ref[j, 18:19] * attended)
    for k in range(4):
        total_ref[k] = run


def later_offset(place_ref, totals_ref):
    offset = jnp.zeros((16, HALF), f32)
    for k in range(3):
        offset = offset + jnp.where(k < place_ref[0], totals_ref[k], 0.0)
    return offset


def change_kernel(place_ref, part_ref, lat_ref, totals_ref, chg_ref):
    offset = later_offset(place_ref, totals_ref)
    for j in range(8):
        change = jnp.max(jnp.abs(part_ref[j] + offset - lat_ref[j, 0:16]))
        chg_ref[j:j + 1, :] = jnp.full((1, 128), change, f32)


def new_kernel(place_ref, part_ref, totals_ref, after_ref, new_ref):
    offset = later_offset(place_ref, totals_ref)
    for j in range(8):
        new_ref[j] = part_ref[j] + offset


def update_kernel(place_ref, part_ref, lat_ref, totals_ref, new_ref, chg_ref, stats_ref):
    offset = later_offset(place_ref, totals_ref)
    lane = lax.broadcasted_iota(jnp.int32, (16, 128), 1)
    for j in range(8):
        new = part_ref[j] + offset
        new_ref[j] = new
        change = jnp.max(jnp.abs(new - lat_ref[j, 0:16]))
        chg_ref[j:j + 1, :] = jnp.full((1, 128), change, f32)
        average = jnp.mean(new, axis=-1, keepdims=True)
        centred = new - average
        spread = jnp.sum(centred * centred, axis=-1, keepdims=True)
        stats_ref[j] = jnp.where(lane == 0, average, spread)


def modulate_kernel(new_ref, mine_ref, other_ref, mod_ref, out_ref):
    for j in range(8):
        mean_a, mean_b = mine_ref[j][:, 0:1], other_ref[j][:, 0:1]
        spread = mine_ref[j][:, 1:2] + other_ref[j][:, 1:2]
        average = (mean_a + mean_b) * 0.5
        gap = mean_a - mean_b
        variance = (spread + gap * gap * (HALF * 0.5)) * (1.0 / D)
        normed = (new_ref[j] - average) * lax.rsqrt(variance + 1e-06)
        out_ref[j] = (
            normed * (1.0 + mod_ref[j, 17:18]) + mod_ref[j, 16:17]
        ).astype(bf16)


def place_kernel(in_ref, out_ref):
    for sub in range(4):
        for k in range(4):
            cols = slice(k * HW, (k + 1) * HW)
            out_ref[sub * 16:(sub + 1) * 16, k * 2 * HW:(k + 1) * 2 * HW] = jnp.concatenate(
                [in_ref[sub * 2][:, cols], in_ref[sub * 2 + 1][:, cols]], axis=1
            )


def on_device(states, qkv_weight, text_kv, mod_table, step_table, step_ids):
    y, zl, c, x, zh = (lax.axis_index(name) for name in AXES)
    same = c == zh
    place = jnp.stack([y, zl, c, x]).astype(jnp.int32)

    with jax.named_scope("start"):
        mod_own = lax.dynamic_index_in_dim(mod_table, step_ids[0], 0, keepdims=False)
        packed, keep, mate = call(
            start_kernel,
            (struct(4, 144, BLOCK, dtype=bf16), struct(4, 24, HALF), struct(4, 24, HALF)),
            3, 3,
        )(place, step_ids, step_table, states, mod_own, text_kv)
    with jax.named_scope("weights"):
        w = call(columns_kernel, struct(48, 3 * HW, dtype=bf16), 1, 0, after=1)(
            qkv_weight, packed
        )
        w_b = [permute(w, ("c", "zh"), lambda p, k=k: {"c": p["zh"], "zh": 1 - p["zh"]}
                       if p["c"] == k else None) for k in range(2)]
        w_a = permute(w, ("c", "zh"), lambda p: None if p["c"] == p["zh"] else
                      {"c": 1 - p["c"], "zh": p["zh"]})
        w0 = jnp.where(same, jnp.where(c == 0, w, w_a), w_b[0])
        w1 = jnp.where(same, jnp.where(c == 1, w, w_a), w_b[1])
        w2 = jnp.concatenate([w0, w1], axis=0)
        w8 = jnp.stack([w2, shift_z(w2, 1), shift_z(w2, 2), shift_z(w2, -1)])

    with jax.named_scope("gather_first"):
        packed = swap_core_zh(packed, same)
        sends = call(send_kernel, (struct(336, BLOCK, dtype=bf16),) * 4, 1, 1)(place, packed)
        mine = [sends[0]] + [shift(sends[k], "x", k) for k in (1, 2, 3)]
        blocks = mine + [shift(b, "c", 1) for b in mine]

    with jax.named_scope("weights_y"):
        w_next, w_last = shift(w8, "y", 1), shift(w8, "y", -1)
        far_a, far_b = shift(w_next[:2], "y", 1), shift(w_last[2:], "y", -1)
        pieces = (w8, w_next, far_a, far_b, w_last)

    with jax.named_scope("states"):
        messages = call(message_kernel, (struct(2, 24, HALF),) * 4, 2, 1, after=1)(
            place, keep, shift(mate, "c", 1), far_b
        )
        messages = [messages[0]] + [shift(messages[k], "zl", k) for k in (1, 2, 3)]

    with jax.named_scope("weights_y"):
        weight = call(weight_kernel, struct(D, 3 * HW, dtype=bf16), 5, 1)(place, *pieces)

    text = None
    for sweep in range(SWEEPS):
        last = sweep == SWEEPS - 1
        with jax.named_scope("attention"):
            outs = (struct(32, 24, 128, dtype=bf16),)
            scratch = [
                pltpu.VMEM((KEYS, 128), bf16), pltpu.VMEM((KEYS, 128), bf16),
                pltpu.VMEM((KEYS, 64), bf16), pltpu.VMEM((KEYS, 64), bf16),
                pltpu.VMEM((TOK, 128), bf16), pltpu.VMEM((TOK, 64), bf16),
            ]
            if sweep == 0:
                operands = (*blocks, weight)
                outs = outs + (struct(2, TXT, HW, dtype=bf16),)
            else:
                operands = (*blocks, weight, text)
            spaces = [pltpu.SMEM] + [pltpu.VMEM] * len(operands)
            attended, *text_out = pl.pallas_call(
                functools.partial(attention_kernel, sweep == 0),
                out_shape=outs,
                in_specs=[pl.BlockSpec(memory_space=space) for space in spaces],
                out_specs=tuple(pl.BlockSpec(memory_space=pltpu.VMEM) for _ in outs),
                compiler_params=pltpu.CompilerParams(vmem_limit_bytes=20 * MIB),
                cost_estimate=pl.CostEstimate(
                    flops=2 * TOK * D * 3 * HW + 4 * TOK * KEYS * HW,
                    bytes_accessed=24 << 20, transcendentals=3 * TOK * KEYS,
                ),
                scratch_shapes=scratch,
            )(place, *operands)
            text = text_out[0] if text_out else text
        with jax.named_scope("to_prefix"):
            if sweep == 0:
                attended = call(hold_kernel, struct(32, 24, 128, dtype=bf16), 1, 0, after=3)(
                    attended, *messages[1:]
                )
            attended = lax.all_to_all(attended, ("zl", "x", "zh"), 0, 0)
        with jax.named_scope("prefix"):
            outs = (struct(8, 16, HALF), struct(4, 16, HALF))
            if sweep == 0:
                part, total, mods = call(
                    functools.partial(terms_kernel, True), outs + (struct(8, 24, HALF),), 5, 1
                )(place, attended, *messages)
                lat = mods
            else:
                part, total = call(functools.partial(terms_kernel, False), outs, 3, 1)(
                    place, attended, lat, mods
                )
            totals = lax.all_to_all(total, "y", 0, 0)
            if last:
                break
            lat, change, stats = call(
                update_kernel, (struct(8, 16, HALF), struct(8, 128), struct(8, 16, 128)), 3, 1
            )(place, part, lat, totals)
        if not last:
            with jax.named_scope("norm"):
                modulated = call(
                    modulate_kernel, struct(8, 16, HALF, dtype=bf16), 4, 0
                )(lat, stats, shift(stats, "c", 1), mods)
            with jax.named_scope("gather"):
                modulated = lax.all_to_all(modulated, ("zl", "zh"), 0, 0).reshape(128, HALF)
                mine = [modulated] + [shift(modulated, "x", k) for k in (1, 2, 3)]
                blocks = mine + [shift(b, "c", 1) for b in mine]
    with jax.named_scope("changes"):
        top = call(change_kernel, struct(8, 128), 3, 1)(place, part, lat, totals)
        top = jnp.concatenate([change, top], axis=0)
        top = functools.reduce(jnp.maximum, [top] + [shift(top, "zl", k) for k in (1, 2, 3)])
    with jax.named_scope("place"):
        out = call(new_kernel, struct(8, 16, HALF), 2, 1, after=1)(place, part, totals, top)
        out = lax.all_to_all(out, ("zl", "c"), 0, 0)
        out = call(place_kernel, struct(ROWS, D), 1, 0)(out)
    with jax.named_scope("changes"):
        top = jnp.maximum(top, shift(top, "zh", 1))
        top = functools.reduce(jnp.maximum, [top] + [shift(top, "x", k) for k in (1, 2, 3)])
        top = jnp.maximum(top, shift(top, "c", 1))
        top = top[:, 0].reshape(SWEEPS, 8)
        top = lax.dynamic_slice_in_dim(top, zl * 2 + c, 1, axis=1)
    return out[None], top


def solution(mesh):
    fine = Mesh(mesh.devices.reshape([SIZES[name] for name in AXES]), AXES)
    tm, seq = ("y", "zl", "c"), ("x", "zh")
    in_specs = (
        P(tm, seq, None), P(tm, None, seq), P(tm, seq, None, None), P(), P(), P(tm),
    )
    out_specs = (P(tm, seq, None), P(None, tm))
    return jax.shard_map(
        on_device, mesh=fine, in_specs=in_specs, out_specs=out_specs, check_vma=False
    )
```

time: 228 us -> 219 us (0.961)
  starting transfers between devices: 88 us -> 49.7 us
  blocking collectives: 30.3 us -> 68 us
  local copies, waits for them, and re-layouts: 13.9 us -> 5.23 us
  other arithmetic: 3.74 us -> 1.24 us
    all_to_all x4 -> x1, starting transfers between devices: 26.3 us -> 3.45 us  [on_device(): out = lax.all_to_all(out, ('zl', 'c'), 0, 0)]
    all_to_all x0 -> x2, blocking collectives: none -> 19.2 us  [on_device(): totals = lax.all_to_all(total, 'y', 0, 0)]
    all_to_all x1 -> x2, blocking collectives: 18.6 us -> 37.4 us  [on_device(): attended = lax.all_to_all(attended, ('zl', 'x', 'zh'), 0, 0)]
    ppermute x43 -> x38, starting transfers between devices: 61.8 us -> 46.2 us  [permute(): return lax.ppermute(value, axes if len(axes) > 1 else axes[0], pairs)]
    all_to_all x4 -> x1, waiting for transfers between devices: 10.2 us -> 0.01 us  [on_device(): out = lax.all_to_all(out, ('zl', 'c'), 0, 0)]
    ppermute x43 -> x38, waiting for transfers between devices: 56.8 us -> 66.1 us  [permute(): return lax.ppermute(value, axes if len(axes) > 1 else axes[0], pairs)]
    gather x4 -> x0, local copies, waits for them, and re-layouts: 4.4 us -> none  [the longest x2 3.19 us: on_device(): mods = jnp.take(mod_table, ids, axis=0).reshape(8, 3, 4, 2, HW)]
    pallas_call x9 -> x14, Pallas kernels: 20.9 us -> 23.1 us  [the longest x2 15.4 us: on_device(): pl.pallas_call(functools.partial(attention_kernel, sweep == 0), out_shape...]
  transfers between devices with their start and end apart: 47 -> 39, of which waited for: 22 -> 21; matrix products, arithmetic and copies ran while one was open for 6% -> 1% of each run, Pallas kernels for 5% -> 4%
where the time goes in v2:
time: 219 us; the launch traced here: 216 us
  blocking collectives  68 us (31%)
  waiting for transfers between devices  66.1 us (30%)
  starting transfers between devices  49.7 us (23%)
  Pallas kernels  24 us (11%)
  local copies, waits for them, and re-layouts  5.23 us (2%)
    ppermute x38, waiting for transfers between devices, permute(): return lax.ppermute(value, axes if len(axes) > 1 else axes[0], pairs)  66.1 us
    ppermute x38, starting transfers between devices, permute(): return lax.ppermute(value, axes if len(axes) > 1 else axes[0], pairs)  46.2 us
    all_to_all x2, blocking collectives, on_device(): attended = lax.all_to_all(attended, ('zl', 'x', 'zh'), 0, 0)  37.4 us
    all_to_all x2, blocking collectives, on_device(): totals = lax.all_to_all(total, 'y', 0, 0)  19.2 us
    pallas_call x2, Pallas kernels, on_device(): pl.pallas_call(functools.partial(attention_kernel, sweep == 0), out_shape...  15.4 us
    all_to_all x1, blocking collectives, on_device(): modulated = lax.all_to_all(modulated, ('zl', 'zh'), 0, 0).reshape(128, HALF)  11.4 us
    unnamed x11, local copies, waits for them, and re-layouts  5.01 us
  transfers between devices with their start and end apart: 39, of which 21 were waited for; matrix products, arithmetic and copies ran while one was open for 1% of the time, Pallas kernels for 4%

profile of v2, /device:TPU:8, one launch (start us, length us, event | category | flops | bytes accessed | tf_op | source)
XLA Modules:
  0.0 215.9 jit_solution(16966706286290582947)
XLA Ops:
  3.4 1.0 copy-done.1
  6.0 1.2 start.1
  7.9 10.4 %collective-permute-start.9 = (bf16[48,576]{1,0:T(8,128)(2,1)S(1)}, bf16[48,576]{1,0:T(8,128)(2,1)}, u32[]{:S(2)}, u32[]{:S(2)}) collective-permute-start(bf16[48,576]{1,0:T(8,128)(2,1)S(1)} %weights.1), channel_id=1, source_target_pairs={{0,1},{1,8},{2,3},{3,10},{4,5},{5,12},{6,7},{7,14},{16,17},{17,24}... | collective-permute-start | bytes 165896 | tf_op jit(solution)/shard_map/weights/ppermute | solution.py:41
  18.3 1.3 collective-permute-start.8
  19.6 1.4 collective-permute-start
  22.4 1.6 collective-permute-start.12
  24.0 1.0 collective-permute-start.11
  25.0 3.6 %collective-permute-start.13 = (bf16[96,576]{1,0:T(8,128)(2,1)S(1)}, bf16[96,576]{1,0:T(8,128)(2,1)S(1)}, u32[]{:S(2)}, u32[]{:S(2)}) collective-permute-start(bf16[96,576]{1,0:T(8,128)(2,1)S(1)} %get-tuple-element.49), channel_id=1, source_target_pairs={{0,49},{1,48},{16,0},{17,1},{32,16},{33,17},{48,32},{49,33},{2,51}... | collective-permute-start | bytes 331784 | tf_op jit(solution)/shard_map/weights/ppermute | solution.py:41
  28.7 16.7 %collective-permute-done.12 = bf16[96,576]{1,0:T(8,128)(2,1)S(1)} collective-permute-done((bf16[96,576]{1,0:T(8,128)(2,1)S(1)}, bf16[96,576]{1,0:T(8,128)(2,1)S(1)}, u32[]{:S(2)}, u32[]{:S(2)}) %collective-permute-start.12) | collective-permute-done | bytes 110624 | tf_op jit(solution)/shard_map/weights/ppermute | solution.py:41
  45.3 1.0 collective-permute-done.11
  47.3 1.6 collective-permute-start.14
  49.5 1.6 collective-permute-start.1
  51.1 2.7 %collective-permute-start.2 = (bf16[336,384]{1,0:T(8,128)(2,1)S(1)}, bf16[336,384]{1,0:T(8,128)(2,1)S(1)}, u32[]{:S(2)}, u32[]{:S(2)}) collective-permute-start(bf16[336,384]{1,0:T(8,128)(2,1)S(1)} %get-tuple-element.26), channel_id=1, source_target_pairs={{0,4},{2,6},{4,0},{6,2},{1,5},{3,7},{5,1},{7,3},{8,12},{10,14},{12... | collective-permute-start | bytes 774152 | tf_op jit(solution)/shard_map/gather_first/ppermute | solution.py:41
  53.8 6.4 %collective-permute-done.16.refs_4_ = bf16[4,96,576]{2,1,0:T(8,128)(2,1)S(1)} collective-permute-done((bf16[4,96,576]{2,1,0:T(8,128)(2,1)S(1)}, bf16[4,96,576]{2,1,0:T(8,128)(2,1)S(1)}, u32[]{:S(2)}, u32[]{:S(2)}) %collective-permute-start.16) | collective-permute-done | bytes 442400 | tf_op jit(solution)/shard_map/weights_y/ppermute | solution.py:41
  60.2 2.8 %collective-permute-start.3 = (bf16[336,384]{1,0:T(8,128)(2,1)S(1)}, bf16[336,384]{1,0:T(8,128)(2,1)S(1)}, u32[]{:S(2)}, u32[]{:S(2)}) collective-permute-start(bf16[336,384]{1,0:T(8,128)(2,1)S(1)} %get-tuple-element.27), channel_id=1, source_target_pairs={{0,6},{2,0},{4,2},{6,4},{1,7},{3,1},{5,3},{7,5},{8,14},{10,8},{12,... | collective-permute-start | bytes 774152 | tf_op jit(solution)/shard_map/gather_first/ppermute | solution.py:41
  63.0 1.1 collective-permute-start.17
  64.6 1.8 collective-permute-done.2.refs_2_
  66.4 2.0 collective-permute-done.3.refs_3_
  68.5 2.0 collective-permute-done.17.refs_3_.after_ref
  70.5 2.3 %collective-permute-start.15 = (bf16[2,96,576]{2,1,0:T(8,128)(2,1)S(1)}, bf16[2,96,576]{2,1,0:T(8,128)(2,1)S(1)}, u32[]{:S(2)}, u32[]{:S(2)}) collective-permute-start(bf16[2,96,576]{2,1,0:T(8,128)(2,1)S(1)} %slice.12), channel_id=1, source_target_pairs={{0,64},{64,128},{128,192},{192,0},{1,65},{65,129},{129,193},{193,1... | collective-permute-start | bytes 663560 | tf_op jit(solution)/shard_map/weights_y/ppermute | solution.py:41
  73.7 3.8 %collective-permute-done.15.refs_2_ = bf16[2,96,576]{2,1,0:T(8,128)(2,1)S(1)} collective-permute-done((bf16[2,96,576]{2,1,0:T(8,128)(2,1)S(1)}, bf16[2,96,576]{2,1,0:T(8,128)(2,1)S(1)}, u32[]{:S(2)}, u32[]{:S(2)}) %collective-permute-start.15) | collective-permute-done | bytes 221216 | tf_op jit(solution)/shard_map/weights_y/ppermute | solution.py:41
  77.5 1.3 collective-permute-start.21
  79.6 7.5 %attention.2 = (bf16[32,24,128]{2,1,0:T(8,128)(2,1)S(1)}, bf16[2,320,192]{2,1,0:T(8,128)(2,1)S(1)}) custom-call(s32[4]{0:T(128)S(1)} %pad_add_fusion.place_ref, bf16[336,384]{1,0:T(8,128)(2,1)S(1)} %get-tuple-element.24.refs_0_, bf16[336,384]{1,0:T(8,128)(2,1)S(1)} %collective-permute-done.1.refs_1_, bf16[336,384]{1,0:T(8,128)(2,1)S(1)} %collective-permute-done.2.refs_2_, ...), custom_call_target="tpu_custom_call" | custom-call | flops 1233125376 | bytes 25165824 | tf_op jit(solution)/shard_map/attention/pallas_call | solution.py:372
  87.2 19.9 %all_to_all.30.att_ref = bf16[32,24,128]{2,1,0:T(8,128)(2,1)S(1)} all-to-all(bf16[32,24,128]{2,1,0:T(8,128)(2,1)S(1)} %to_prefix.1), channel_id=1, replica_groups=mesh['y'=4,'zl'=4,'c'=2,'x'=4,'zh'=2] {'zl','x','zh'}, dimensions={0} | all-to-all | bytes 393216 | tf_op jit(solution)/shard_map/to_prefix/all_to_all | solution.py:390
  107.9 10.5 %all_to_all.31.totals_ref = f32[4,16,768]{2,1,0:T(8,128)S(1)} all-to-all(f32[4,16,768]{2,1,0:T(8,128)S(1)} %get-tuple-element.37), channel_id=1, replica_groups=mesh['y'=4,'zl'=4,'c'=2,'x'=4,'zh'=2] {'y'}, dimensions={0} | all-to-all | bytes 393216 | tf_op jit(solution)/shard_map/prefix/all_to_all | solution.py:402
  119.3 1.2 collective-permute-done.22.other_ref
  120.7 11.4 %all_to_all.32 = bf16[8,16,768]{2,1,0:T(8,128)(2,1)S(1)} all-to-all(bf16[8,16,768]{2,1,0:T(8,128)(2,1)S(1)} %norm.1), channel_id=1, replica_groups=mesh['y'=4,'zl'=4,'c'=2,'x'=4,'zh'=2] {'zl','zh'}, dimensions={0} | all-to-all | bytes 393216 | tf_op jit(solution)/shard_map/gather/all_to_all | solution.py:414
  132.2 1.7 collective-permute-start.25
  133.8 1.0 collective-permute-start.24
  134.9 6.1 %collective-permute-done.25.refs_3_ = bf16[128,768]{1,0:T(8,128)(2,1)S(1)} collective-permute-done((bf16[128,768]{1,0:T(8,128)(2,1)S(1)}, bf16[128,768]{1,0:T(8,128)(2,1)S(1)}, u32[]{:S(2)}, u32[]{:S(2)}) %collective-permute-start.25) | collective-permute-done | bytes 196640 | tf_op jit(solution)/shard_map/gather/ppermute | solution.py:41
  141.0 1.7 collective-permute-done.24.refs_2_
  142.6 2.0 collective-permute-done.23.refs_1_
  144.6 1.4 collective-permute-done.27.refs_5_
  146.1 7.8 %attention.3 = bf16[32,24,128]{2,1,0:T(8,128)(2,1)S(1)} custom-call(s32[4]{0:T(128)S(1)} %pad_add_fusion.place_ref, bf16[128,768]{1,0:T(8,128)(2,1)S(1)} %bitcast.22, bf16[128,768]{1,0:T(8,128)(2,1)S(1)} %collective-permute-done.23.refs_1_, bf16[128,768]{1,0:T(8,128)(2,1)S(1)} %collective-permute-done.24.refs_2_, ...), custom_call_target="tpu_custom_call" | custom-call | flops 1233125376 | bytes 25165824 | tf_op jit(solution)/shard_map/attention/pallas_call | solution.py:372
  153.9 17.4 %all_to_all.33.att_ref = bf16[32,24,128]{2,1,0:T(8,128)(2,1)S(1)} all-to-all(bf16[32,24,128]{2,1,0:T(8,128)(2,1)S(1)} %attention.3), channel_id=1, replica_groups=mesh['y'=4,'zl'=4,'c'=2,'x'=4,'zh'=2] {'zl','x','zh'}, dimensions={0} | all-to-all | bytes 393216 | tf_op jit(solution)/shard_map/to_prefix/all_to_all | solution.py:390
  172.0 8.7 %all_to_all.34.totals_ref = f32[4,16,768]{2,1,0:T(8,128)S(1)} all-to-all(f32[4,16,768]{2,1,0:T(8,128)S(1)} %get-tuple-element.42), channel_id=1, replica_groups=mesh['y'=4,'zl'=4,'c'=2,'x'=4,'zh'=2] {'y'}, dimensions={0} | all-to-all | bytes 393216 | tf_op jit(solution)/shard_map/prefix/all_to_all | solution.py:402
  181.5 1.9 collective-permute-start.31
  183.4 2.3 %collective-permute-start.32 = (f32[16,128]{1,0:T(8,128)S(1)}, f32[16,128]{1,0:T(8,128)S(1)}, u32[]{:S(2)}, u32[]{:S(2)}) collective-permute-start(f32[16,128]{1,0:T(8,128)S(1)} %pad_maximum_fusion.2), channel_id=1, source_target_pairs={{0,48},{16,0},{32,16},{48,32},{1,49},{17,1},{33,17},{49,33},{2,50}... | collective-permute-start | bytes 24584 | tf_op jit(solution)/shard_map/changes/ppermute | solution.py:41
  187.0 4.1 %collective-permute-done.30 = f32[16,128]{1,0:T(8,128)S(1)} collective-permute-done((f32[16,128]{1,0:T(8,128)S(1)}, f32[16,128]{1,0:T(8,128)S(1)}, u32[]{:S(2)}, u32[]{:S(2)}) %collective-permute-start.30) | collective-permute-done | bytes 8224 | tf_op jit(solution)/shard_map/changes/ppermute | solution.py:41
  191.1 1.3 place.2
  192.4 3.5 %all-to-all-start.5 = ((f32[8,16,768]{2,1,0:T(8,128)}), f32[8,16,768]{2,1,0:T(8,128)S(1)}, u32[]{:S(2)}, u32[]{:S(2)}) async-start(f32[8,16,768]{2,1,0:T(8,128)} %place.2), calls=%async_computation.5 | async-start | bytes 786432 | tf_op jit(solution)/shard_map/place/all_to_all | solution.py:423
  195.9 1.5 collective-permute-start.33
  197.4 8.0 %collective-permute-done.33 = f32[16,128]{1,0:T(8,128)S(1)} collective-permute-done((f32[16,128]{1,0:T(8,128)S(1)}, f32[16,128]{1,0:T(8,128)S(1)}, u32[]{:S(2)}, u32[]{:S(2)}) %collective-permute-start.33) | collective-permute-done | bytes 8224 | tf_op jit(solution)/shard_map/changes/ppermute | solution.py:41
  205.4 1.3 collective-permute-start.36
  206.7 1.4 collective-permute-start.35
  209.1 2.8 %collective-permute-done.35 = f32[16,128]{1,0:T(8,128)S(1)} collective-permute-done((f32[16,128]{1,0:T(8,128)S(1)}, f32[16,128]{1,0:T(8,128)S(1)}, u32[]{:S(2)}, u32[]{:S(2)}) %collective-permute-start.35) | collective-permute-done | bytes 8224 | tf_op jit(solution)/shard_map/changes/ppermute | solution.py:41
  211.8 1.1 collective-permute-done.34
  213.0 1.2 collective-permute-done.37
  (76 shorter events, 17.1 us)
Async XLA Ops:
  0.6 1.7 copy-start
  3.4 1.0 copy-start.1
  4.4 0.9 copy-start.2
  5.3 0.7 copy-start.3
  7.3 13.8 %collective-permute-start.10 = (bf16[48,576]{1,0:T(8,128)(2,1)S(1)}, bf16[48,576]{1,0:T(8,128)(2,1)S(1)}, u32[]{:S(2)}, u32[]{:S(2)}) collective-permute-start(bf16[48,576]{1,0:T(8,128)(2,1)S(1)} %weights.1), channel_id=1, source_target_pairs={{8,1},{9,8},{10,3},{11,10},{12,5},{13,12},{14,7},{15,14},{24,17},{... | collective-permute-start | bytes 165896 | tf_op jit(solution)/shard_map/weights/ppermute | solution.py:41
  7.9 13.1 %collective-permute-start.9 = (bf16[48,576]{1,0:T(8,128)(2,1)S(1)}, bf16[48,576]{1,0:T(8,128)(2,1)}, u32[]{:S(2)}, u32[]{:S(2)}) collective-permute-start(bf16[48,576]{1,0:T(8,128)(2,1)S(1)} %weights.1), channel_id=1, source_target_pairs={{0,1},{1,8},{2,3},{3,10},{4,5},{5,12},{6,7},{7,14},{16,17},{17,24}... | collective-permute-start | bytes 165896 | tf_op jit(solution)/shard_map/weights/ppermute | solution.py:41
  18.3 3.3 %collective-permute-start.8 = (bf16[48,576]{1,0:T(8,128)(2,1)S(1)}, bf16[48,576]{1,0:T(8,128)(2,1)}, u32[]{:S(2)}, u32[]{:S(2)}) collective-permute-start(bf16[48,576]{1,0:T(8,128)(2,1)S(1)} %weights.1), channel_id=1, source_target_pairs={{1,9},{8,0},{3,11},{10,2},{5,13},{12,4},{7,15},{14,6},{17,25},{24,... | collective-permute-start | bytes 165896 | tf_op jit(solution)/shard_map/weights/ppermute | solution.py:41
  19.6 29.3 %collective-permute-start = (bf16[4,144,384]{2,1,0:T(8,128)(2,1)S(1)}, bf16[4,144,384]{2,1,0:T(8,128)(2,1)}, u32[]{:S(2)}, u32[]{:S(2)}) collective-permute-start(bf16[4,144,384]{2,1,0:T(8,128)(2,1)S(1)} %get-tuple-element.23.after_ref), channel_id=1, source_target_pairs={{1,8},{8,1},{3,10},{10,3},{5,12},{12,5},{7,14},{14,7},{17,24},{24,... | collective-permute-start | bytes 1327112 | tf_op jit(solution)/shard_map/gather_first/ppermute | solution.py:41
  22.4 22.9 %collective-permute-start.12 = (bf16[96,576]{1,0:T(8,128)(2,1)S(1)}, bf16[96,576]{1,0:T(8,128)(2,1)S(1)}, u32[]{:S(2)}, u32[]{:S(2)}) collective-permute-start(bf16[96,576]{1,0:T(8,128)(2,1)S(1)} %get-tuple-element.49), channel_id=1, source_target_pairs={{0,32},{1,33},{16,48},{17,49},{32,1},{33,0},{48,17},{49,16},{2,34}... | collective-permute-start | bytes 331784 | tf_op jit(solution)/shard_map/weights/ppermute | solution.py:41
  24.0 22.3 %collective-permute-start.11 = (bf16[96,576]{1,0:T(8,128)(2,1)S(1)}, bf16[96,576]{1,0:T(8,128)(2,1)S(1)}, u32[]{:S(2)}, u32[]{:S(2)}) collective-permute-start(bf16[96,576]{1,0:T(8,128)(2,1)S(1)} %get-tuple-element.49), channel_id=1, source_target_pairs={{0,16},{1,17},{16,32},{17,33},{32,48},{33,49},{48,1},{49,0},{2,18}... | collective-permute-start | bytes 331784 | tf_op jit(solution)/shard_map/weights/ppermute | solution.py:41
  25.0 21.3 %collective-permute-start.13 = (bf16[96,576]{1,0:T(8,128)(2,1)S(1)}, bf16[96,576]{1,0:T(8,128)(2,1)S(1)}, u32[]{:S(2)}, u32[]{:S(2)}) collective-permute-start(bf16[96,576]{1,0:T(8,128)(2,1)S(1)} %get-tuple-element.49), channel_id=1, source_target_pairs={{0,49},{1,48},{16,0},{17,1},{32,16},{33,17},{48,32},{49,33},{2,51}... | collective-permute-start | bytes 331784 | tf_op jit(solution)/shard_map/weights/ppermute | solution.py:41
  46.4 13.8 %collective-permute-start.16 = (bf16[4,96,576]{2,1,0:T(8,128)(2,1)S(1)}, bf16[4,96,576]{2,1,0:T(8,128)(2,1)S(1)}, u32[]{:S(2)}, u32[]{:S(2)}) collective-permute-start(bf16[4,96,576]{2,1,0:T(8,128)(2,1)S(1)} %pad_maximum_fusion.refs_0_), channel_id=1, source_target_pairs={{0,192},{64,0},{128,64},{192,128},{1,193},{65,1},{129,65},{193,129... | collective-permute-start | bytes 1327112 | tf_op jit(solution)/shard_map/weights_y/ppermute | solution.py:41
  46.9 16.1 %collective-permute-start.18 = (f32[4,24,768]{2,1,0:T(8,128)S(1)}, f32[4,24,768]{2,1,0:T(8,128)S(1)}, u32[]{:S(2)}, u32[]{:S(2)}) collective-permute-start(f32[4,24,768]{2,1,0:T(8,128)S(1)} %get-tuple-element.30), channel_id=1, source_target_pairs={{0,8},{8,0},{1,9},{9,1},{2,10},{10,2},{3,11},{11,3},{4,12},{12,4},... | collective-permute-start | bytes 884744 | tf_op jit(solution)/shard_map/states/ppermute | solution.py:41
  47.3 16.8 %collective-permute-start.14 = (bf16[4,96,576]{2,1,0:T(8,128)(2,1)S(1)}, bf16[4,96,576]{2,1,0:T(8,128)(2,1)S(1)}, u32[]{:S(2)}, u32[]{:S(2)}) collective-permute-start(bf16[4,96,576]{2,1,0:T(8,128)(2,1)S(1)} %pad_maximum_fusion.refs_0_), channel_id=1, source_target_pairs={{0,64},{64,128},{128,192},{192,0},{1,65},{65,129},{129,193},{193,1... | collective-permute-start | bytes 1327112 | tf_op jit(solution)/shard_map/weights_y/ppermute | solution.py:41
  49.5 14.5 %collective-permute-start.1 = (bf16[336,384]{1,0:T(8,128)(2,1)S(1)}, bf16[336,384]{1,0:T(8,128)(2,1)S(1)}, u32[]{:S(2)}, u32[]{:S(2)}) collective-permute-start(bf16[336,384]{1,0:T(8,128)(2,1)S(1)} %get-tuple-element.25), channel_id=1, source_target_pairs={{0,2},{2,4},{4,6},{6,0},{1,3},{3,5},{5,7},{7,1},{8,10},{10,12},{12... | collective-permute-start | bytes 774152 | tf_op jit(solution)/shard_map/gather_first/ppermute | solution.py:41
  51.1 15.3 %collective-permute-start.2 = (bf16[336,384]{1,0:T(8,128)(2,1)S(1)}, bf16[336,384]{1,0:T(8,128)(2,1)S(1)}, u32[]{:S(2)}, u32[]{:S(2)}) collective-permute-start(bf16[336,384]{1,0:T(8,128)(2,1)S(1)} %get-tuple-element.26), channel_id=1, source_target_pairs={{0,4},{2,6},{4,0},{6,2},{1,5},{3,7},{5,1},{7,3},{8,12},{10,14},{12... | collective-permute-start | bytes 774152 | tf_op jit(solution)/shard_map/gather_first/ppermute | solution.py:41
  60.2 8.2 %collective-permute-start.3 = (bf16[336,384]{1,0:T(8,128)(2,1)S(1)}, bf16[336,384]{1,0:T(8,128)(2,1)S(1)}, u32[]{:S(2)}, u32[]{:S(2)}) collective-permute-start(bf16[336,384]{1,0:T(8,128)(2,1)S(1)} %get-tuple-element.27), channel_id=1, source_target_pairs={{0,6},{2,0},{4,2},{6,4},{1,7},{3,1},{5,3},{7,5},{8,14},{10,8},{12,... | collective-permute-start | bytes 774152 | tf_op jit(solution)/shard_map/gather_first/ppermute | solution.py:41
  63.0 7.5 %collective-permute-start.17 = (bf16[2,96,576]{2,1,0:T(8,128)(2,1)S(1)}, bf16[2,96,576]{2,1,0:T(8,128)(2,1)S(1)}, u32[]{:S(2)}, u32[]{:S(2)}) collective-permute-start(bf16[2,96,576]{2,1,0:T(8,128)(2,1)S(1)} %slice.13), channel_id=1, source_target_pairs={{0,192},{64,0},{128,64},{192,128},{1,193},{65,1},{129,65},{193,129... | collective-permute-start | bytes 663560 | tf_op jit(solution)/shard_map/weights_y/ppermute | solution.py:41
  64.1 9.4 %collective-permute-start.4 = (bf16[336,384]{1,0:T(8,128)(2,1)S(1)}, bf16[336,384]{1,0:T(8,128)(2,1)S(1)}, u32[]{:S(2)}, u32[]{:S(2)}) collective-permute-start(bf16[336,384]{1,0:T(8,128)(2,1)S(1)} %get-tuple-element.24.refs_0_), channel_id=1, source_target_pairs={{0,8},{8,0},{1,9},{9,1},{2,10},{10,2},{3,11},{11,3},{4,12},{12,4},... | collective-permute-start | bytes 774152 | tf_op jit(solution)/shard_map/gather_first/ppermute | solution.py:41
  64.1 13.4 %collective-permute-start.5 = (bf16[336,384]{1,0:T(8,128)(2,1)S(1)}, bf16[336,384]{1,0:T(8,128)(2,1)S(1)}, u32[]{:S(2)}, u32[]{:S(2)}) collective-permute-start(bf16[336,384]{1,0:T(8,128)(2,1)S(1)} %collective-permute-done.1.refs_1_), channel_id=1, source_target_pairs={{0,8},{8,0},{1,9},{9,1},{2,10},{10,2},{3,11},{11,3},{4,12},{12,4},... | collective-permute-start | bytes 774152 | tf_op jit(solution)/shard_map/gather_first/ppermute | solution.py:41
  66.4 13.2 %collective-permute-start.6 = (bf16[336,384]{1,0:T(8,128)(2,1)S(1)}, bf16[336,384]{1,0:T(8,128)(2,1)S(1)}, u32[]{:S(2)}, u32[]{:S(2)}) collective-permute-start(bf16[336,384]{1,0:T(8,128)(2,1)S(1)} %collective-permute-done.2.refs_2_), channel_id=1, source_target_pairs={{0,8},{8,0},{1,9},{9,1},{2,10},{10,2},{3,11},{11,3},{4,12},{12,4},... | collective-permute-start | bytes 774152 | tf_op jit(solution)/shard_map/gather_first/ppermute | solution.py:41
  68.5 11.1 %collective-permute-start.7 = (bf16[336,384]{1,0:T(8,128)(2,1)S(1)}, bf16[336,384]{1,0:T(8,128)(2,1)S(1)}, u32[]{:S(2)}, u32[]{:S(2)}) collective-permute-start(bf16[336,384]{1,0:T(8,128)(2,1)S(1)} %collective-permute-done.3.refs_3_), channel_id=1, source_target_pairs={{0,8},{8,0},{1,9},{9,1},{2,10},{10,2},{3,11},{11,3},{4,12},{12,4},... | collective-permute-start | bytes 774152 | tf_op jit(solution)/shard_map/gather_first/ppermute | solution.py:41
  70.5 7.0 %collective-permute-start.15 = (bf16[2,96,576]{2,1,0:T(8,128)(2,1)S(1)}, bf16[2,96,576]{2,1,0:T(8,128)(2,1)S(1)}, u32[]{:S(2)}, u32[]{:S(2)}) collective-permute-start(bf16[2,96,576]{2,1,0:T(8,128)(2,1)S(1)} %slice.12), channel_id=1, source_target_pairs={{0,64},{64,128},{128,192},{192,0},{1,65},{65,129},{129,193},{193,1... | collective-permute-start | bytes 663560 | tf_op jit(solution)/shard_map/weights_y/ppermute | solution.py:41
  73.5 13.7 %collective-permute-start.19 = (f32[2,24,768]{2,1,0:T(8,128)S(1)}, f32[2,24,768]{2,1,0:T(8,128)S(1)}, u32[]{:S(2)}, u32[]{:S(2)}) collective-permute-start(f32[2,24,768]{2,1,0:T(8,128)S(1)} %get-tuple-element.31), channel_id=1, source_target_pairs={{0,16},{16,32},{32,48},{48,0},{1,17},{17,33},{33,49},{49,1},{2,18}... | collective-permute-start | bytes 442376 | tf_op jit(solution)/shard_map/states/ppermute | solution.py:41
  77.5 9.6 %collective-permute-start.20 = (f32[2,24,768]{2,1,0:T(8,128)S(1)}, f32[2,24,768]{2,1,0:T(8,128)S(1)}, u32[]{:S(2)}, u32[]{:S(2)}) collective-permute-start(f32[2,24,768]{2,1,0:T(8,128)S(1)} %get-tuple-element.32), channel_id=1, source_target_pairs={{0,32},{16,48},{32,0},{48,16},{1,33},{17,49},{33,1},{49,17},{2,34}... | collective-permute-start | bytes 442376 | tf_op jit(solution)/shard_map/states/ppermute | solution.py:41
  77.5 9.7 %collective-permute-start.21 = (f32[2,24,768]{2,1,0:T(8,128)S(1)}, f32[2,24,768]{2,1,0:T(8,128)S(1)}, u32[]{:S(2)}, u32[]{:S(2)}) collective-permute-start(f32[2,24,768]{2,1,0:T(8,128)S(1)} %get-tuple-element.33), channel_id=1, source_target_pairs={{0,48},{16,0},{32,16},{48,32},{1,49},{17,1},{33,17},{49,33},{2,50}... | collective-permute-start | bytes 442376 | tf_op jit(solution)/shard_map/states/ppermute | solution.py:41
  119.2 1.3 collective-permute-start.22
  132.2 8.8 %collective-permute-start.25 = (bf16[128,768]{1,0:T(8,128)(2,1)S(1)}, bf16[128,768]{1,0:T(8,128)(2,1)S(1)}, u32[]{:S(2)}, u32[]{:S(2)}) collective-permute-start(bf16[128,768]{1,0:T(8,128)(2,1)S(1)} %bitcast.18), channel_id=1, source_target_pairs={{0,6},{2,0},{4,2},{6,4},{1,7},{3,1},{5,3},{7,5},{8,14},{10,8},{12,... | collective-permute-start | bytes 589832 | tf_op jit(solution)/shard_map/gather/ppermute | solution.py:41
  133.8 8.8 %collective-permute-start.24 = (bf16[128,768]{1,0:T(8,128)(2,1)S(1)}, bf16[128,768]{1,0:T(8,128)(2,1)S(1)}, u32[]{:S(2)}, u32[]{:S(2)}) collective-permute-start(bf16[128,768]{1,0:T(8,128)(2,1)S(1)} %bitcast.19), channel_id=1, source_target_pairs={{0,4},{2,6},{4,0},{6,2},{1,5},{3,7},{5,1},{7,3},{8,12},{10,14},{12... | collective-permute-start | bytes 589832 | tf_op jit(solution)/shard_map/gather/ppermute | solution.py:41
  134.8 9.8 %collective-permute-start.23 = (bf16[128,768]{1,0:T(8,128)(2,1)S(1)}, bf16[128,768]{1,0:T(8,128)(2,1)S(1)}, u32[]{:S(2)}, u32[]{:S(2)}) collective-permute-start(bf16[128,768]{1,0:T(8,128)(2,1)S(1)} %bitcast.20), channel_id=1, source_target_pairs={{0,2},{2,4},{4,6},{6,0},{1,3},{3,5},{5,7},{7,1},{8,10},{10,12},{12... | collective-permute-start | bytes 589832 | tf_op jit(solution)/shard_map/gather/ppermute | solution.py:41
  134.9 9.8 %collective-permute-start.26 = (bf16[128,768]{1,0:T(8,128)(2,1)S(1)}, bf16[128,768]{1,0:T(8,128)(2,1)S(1)}, u32[]{:S(2)}, u32[]{:S(2)}) collective-permute-start(bf16[128,768]{1,0:T(8,128)(2,1)S(1)} %bitcast.21), channel_id=1, source_target_pairs={{0,8},{8,0},{1,9},{9,1},{2,10},{10,2},{3,11},{11,3},{4,12},{12,4},... | collective-permute-start | bytes 589832 | tf_op jit(solution)/shard_map/gather/ppermute | solution.py:41
  141.0 3.7 %collective-permute-start.29 = (bf16[128,768]{1,0:T(8,128)(2,1)S(1)}, bf16[128,768]{1,0:T(8,128)(2,1)S(1)}, u32[]{:S(2)}, u32[]{:S(2)}) collective-permute-start(bf16[128,768]{1,0:T(8,128)(2,1)S(1)} %collective-permute-done.25.refs_3_), channel_id=1, source_target_pairs={{0,8},{8,0},{1,9},{9,1},{2,10},{10,2},{3,11},{11,3},{4,12},{12,4},... | collective-permute-start | bytes 589832 | tf_op jit(solution)/shard_map/gather/ppermute | solution.py:41
  142.6 2.0 collective-permute-start.28
  144.6 1.4 collective-permute-start.27
  181.5 4.6 %collective-permute-start.31 = (f32[16,128]{1,0:T(8,128)S(1)}, f32[16,128]{1,0:T(8,128)S(1)}, u32[]{:S(2)}, u32[]{:S(2)}) collective-permute-start(f32[16,128]{1,0:T(8,128)S(1)} %pad_maximum_fusion.2), channel_id=1, source_target_pairs={{0,32},{16,48},{32,0},{48,16},{1,33},{17,49},{33,1},{49,17},{2,34}... | collective-permute-start | bytes 24584 | tf_op jit(solution)/shard_map/changes/ppermute | solution.py:41
  183.4 3.7 %collective-permute-start.32 = (f32[16,128]{1,0:T(8,128)S(1)}, f32[16,128]{1,0:T(8,128)S(1)}, u32[]{:S(2)}, u32[]{:S(2)}) collective-permute-start(f32[16,128]{1,0:T(8,128)S(1)} %pad_maximum_fusion.2), channel_id=1, source_target_pairs={{0,48},{16,0},{32,16},{48,32},{1,49},{17,1},{33,17},{49,33},{2,50}... | collective-permute-start | bytes 24584 | tf_op jit(solution)/shard_map/changes/ppermute | solution.py:41
  185.6 5.4 %collective-permute-start.30 = (f32[16,128]{1,0:T(8,128)S(1)}, f32[16,128]{1,0:T(8,128)S(1)}, u32[]{:S(2)}, u32[]{:S(2)}) collective-permute-start(f32[16,128]{1,0:T(8,128)S(1)} %pad_maximum_fusion.2), channel_id=1, source_target_pairs={{0,16},{16,32},{32,48},{48,0},{1,17},{17,33},{33,49},{49,1},{2,18}... | collective-permute-start | bytes 24584 | tf_op jit(solution)/shard_map/changes/ppermute | solution.py:41
  192.4 22.6 %all-to-all-start.5 = ((f32[8,16,768]{2,1,0:T(8,128)}), f32[8,16,768]{2,1,0:T(8,128)S(1)}, u32[]{:S(2)}, u32[]{:S(2)}) async-start(f32[8,16,768]{2,1,0:T(8,128)} %place.2), calls=%async_computation.5 | async-start | bytes 786432 | tf_op jit(solution)/shard_map/place/all_to_all | solution.py:423
  195.9 9.5 %collective-permute-start.33 = (f32[16,128]{1,0:T(8,128)S(1)}, f32[16,128]{1,0:T(8,128)S(1)}, u32[]{:S(2)}, u32[]{:S(2)}) collective-permute-start(f32[16,128]{1,0:T(8,128)S(1)} %maximum_maximum_fusion.1.after_ref), channel_id=1, source_target_pairs={{0,1},{1,0},{2,3},{3,2},{4,5},{5,4},{6,7},{7,6},{8,9},{9,8},{10,11... | collective-permute-start | bytes 24584 | tf_op jit(solution)/shard_map/changes/ppermute | solution.py:41
  205.4 3.7 %collective-permute-start.36 = (f32[16,128]{1,0:T(8,128)S(1)}, f32[16,128]{1,0:T(8,128)S(1)}, u32[]{:S(2)}, u32[]{:S(2)}) collective-permute-start(f32[16,128]{1,0:T(8,128)S(1)} %max.27), channel_id=1, source_target_pairs={{0,6},{2,0},{4,2},{6,4},{1,7},{3,1},{5,3},{7,5},{8,14},{10,8},{12,... | collective-permute-start | bytes 24584 | tf_op jit(solution)/shard_map/changes/ppermute | solution.py:41
  206.7 5.2 %collective-permute-start.35 = (f32[16,128]{1,0:T(8,128)S(1)}, f32[16,128]{1,0:T(8,128)S(1)}, u32[]{:S(2)}, u32[]{:S(2)}) collective-permute-start(f32[16,128]{1,0:T(8,128)S(1)} %max.27), channel_id=1, source_target_pairs={{0,4},{2,6},{4,0},{6,2},{1,5},{3,7},{5,1},{7,3},{8,12},{10,14},{12... | collective-permute-start | bytes 24584 | tf_op jit(solution)/shard_map/changes/ppermute | solution.py:41
  208.1 4.9 %collective-permute-start.34 = (f32[16,128]{1,0:T(8,128)S(1)}, f32[16,128]{1,0:T(8,128)S(1)}, u32[]{:S(2)}, u32[]{:S(2)}) collective-permute-start(f32[16,128]{1,0:T(8,128)S(1)} %max.27), channel_id=1, source_target_pairs={{0,2},{2,4},{4,6},{6,0},{1,3},{3,5},{5,7},{7,1},{8,10},{10,12},{12... | collective-permute-start | bytes 24584 | tf_op jit(solution)/shard_map/changes/ppermute | solution.py:41
  213.0 1.2 collective-permute-start.37

commit v3 on v2

--- a/solution.py
+++ b/solution.py
@@ -81,13 +81,13 @@
     return [slice(k * 2 * HW + half * HW, k * 2 * HW + (half + 1) * HW) for k in range(4)]
 
 
-def columns_kernel(w_ref, after_ref, out_ref):
+def columns_kernel(w_ref, out_ref):
     raw = w_ref[...].astype(f32)
     parts = [raw[:, k, :128] for k in range(3)] + [raw[:, k, 128:] for k in range(3)]
     out_ref[...] = jnp.concatenate(parts, axis=1).astype(bf16)
 
 
-def start_kernel(place_ref, ids_ref, steps_ref, lat_ref, mod_ref, text_ref,
+def start_kernel(place_ref, ids_ref, steps_ref, lat_ref, mod_ref, text_ref, after_ref,
                  out_ref, keep_ref, mate_ref):
     latent = lat_ref[0]
     average = jnp.mean(latent, axis=-1, keepdims=True)
@@ -119,8 +119,10 @@
     refs[-1][...] = in_ref[...]
 
 
-def message_kernel(place_ref, keep_ref, mate_ref, after_ref, *out_refs):
+def message_kernel(place_ref, keep_ref, mate_ref, extra_ref, *out_refs):
     zl, core = place_ref[1], place_ref[2]
+    if len(out_refs) == 5:
+        out_refs[4][...] = extra_ref[...]
     for k in range(4):
         target = lax.rem(zl + k, 4)
         out_refs[k][core] = keep_ref[target]
@@ -135,26 +137,14 @@
         out_refs[k][256:336] = in_ref[lax.rem(x + k, 4), 64:144]
 
 
-def weight_rows(place_ref):
+def weight_kernel(place_ref, *refs):
     y, zl = place_ref[0], place_ref[1]
-    for ky in range(4):
+    for piece, ky in enumerate((0, 1, -1, 2)):
         from_y = lax.rem(y - ky + 4, 4)
         for kz in range(4):
             from_zl = lax.rem(zl - kz + 4, 4)
             row = (from_zl // 2) * HALF + from_y * HW + lax.rem(from_zl, 2) * 96
-            yield ky, kz, pl.ds(pl.multiple_of(row, 32), 96)
-
-
-def weight_piece(pieces, ky, kz):
-    own, after, far_a, far_b, last = pieces
-    if ky == 2:
-        return (far_a if kz < 2 else far_b).at[kz % 2]
-    return (own, after, None, last)[ky].at[kz]
-
-
-def weight_kernel(place_ref, *refs):
-    for ky, kz, rows in weight_rows(place_ref):
-        refs[-1][rows, :] = weight_piece(refs[:5], ky, kz)[...]
+            refs[4][pl.ds(pl.multiple_of(row, 32), 96), :] = refs[piece][kz]
 
 
 def attention_kernel(first, place_ref, *refs):
@@ -193,7 +183,7 @@
     v01[TOK:, :] = text_ref[1, :, 0:128]
     k2[TOK:, :] = text_ref[0, :, 128:192]
     v2[TOK:, :] = text_ref[1, :, 128:192]
-    lane = lax.broadcasted_iota(jnp.int32, (128, 128), 1)
+    lane = lax.broadcasted_iota(jnp.int32, (TOK, 128), 1)
 
     def attend(query, keys, values):
         scores = lax.dot_general(
@@ -205,26 +195,24 @@
         weights = (exp_scores * (1.0 / total)).astype(bf16)
         return jnp.dot(weights, values, preferred_element_type=f32)
 
-    for chunk in range(4):
-        span = slice(chunk * 128, (chunk + 1) * 128)
-        pair = q01[span, :]
-        zero = jnp.zeros_like(pair)
-        out0 = attend(jnp.where(lane < 64, pair, zero), k01[...], v01[...])
-        out1 = attend(jnp.where(lane < 64, zero, pair), k01[...], v01[...])
-        out01 = jnp.where(lane < 64, out0, out1).astype(bf16)
-        out2 = attend(q2[span, :], k2[...], v2[...])
-        from_x = lax.rem(x - chunk + 4, 4)
-        for part in range(8):
-            if first:
-                sub = part % 4
-                zh = core if part < 4 else 1 - core
-            else:
-                sub, zh = part // 2, part % 2
-            target = (sub * 4 + from_x) * 2 + zh
-            out_ref[target, 0:16] = out01[part * 16:(part + 1) * 16]
-            out_ref[target, 16:24] = jnp.concatenate(
-                [out2[part * 16:part * 16 + 8], out2[part * 16 + 8:(part + 1) * 16]], axis=1
-            ).astype(bf16)
+    pair = q01[...]
+    zero = jnp.zeros_like(pair)
+    out0 = attend(jnp.where(lane < 64, pair, zero), k01[...], v01[...])
+    out1 = attend(jnp.where(lane < 64, zero, pair), k01[...], v01[...])
+    out01 = jnp.where(lane < 64, out0, out1).astype(bf16)
+    out2 = attend(q2[...], k2[...], v2[...])
+    for part in range(TOK // 16):
+        slot, place = part // 8, part % 8
+        if first:
+            sub, zh = place % 4, (core if place < 4 else 1 - core)
+        else:
+            sub, zh = place // 2, place % 2
+        target = (sub * 4 + lax.rem(x - slot + 4, 4)) * 2 + zh
+        start = part * 16
+        out_ref[target, 0:16] = out01[start:start + 16]
+        out_ref[target, 16:24] = jnp.concatenate(
+            [out2[start:start + 8], out2[start + 8:start + 16]], axis=1
+        ).astype(bf16)
 
 
 def terms_kernel(first, place_ref, att_ref, *refs):
@@ -259,17 +247,16 @@
     return offset
 
 
-def change_kernel(place_ref, part_ref, lat_ref, totals_ref, chg_ref):
+def final_kernel(place_ref, part_ref, lat_ref, totals_ref, chg_ref, keep_ref, mate_ref):
     offset = later_offset(place_ref, totals_ref)
+    core = place_ref[2]
     for j in range(8):
-        change = jnp.max(jnp.abs(part_ref[j] + offset - lat_ref[j, 0:16]))
-        chg_ref[j:j + 1, :] = jnp.full((1, 128), change, f32)
-
-
-def new_kernel(place_ref, part_ref, totals_ref, after_ref, new_ref):
-    offset = later_offset(place_ref, totals_ref)
-    for j in range(8):
-        new_ref[j] = part_ref[j] + offset
+        new = part_ref[j] + offset
+        chg_ref[j:j + 1, :] = jnp.full((1, 128), jnp.max(jnp.abs(new - lat_ref[j])), f32)
+        for ref, wanted in ((keep_ref, core), (mate_ref, 1 - core)):
+            @pl.when(wanted == j % 2)
+            def _(ref=ref, new=new, j=j):
+                ref[j // 2] = new
 
 
 def update_kernel(place_ref, part_ref, lat_ref, totals_ref, new_ref, chg_ref, stats_ref):
@@ -299,12 +286,14 @@
         ).astype(bf16)
 
 
-def place_kernel(in_ref, out_ref):
-    for sub in range(4):
-        for k in range(4):
-            cols = slice(k * HW, (k + 1) * HW)
-            out_ref[sub * 16:(sub + 1) * 16, k * 2 * HW:(k + 1) * 2 * HW] = jnp.concatenate(
-                [in_ref[sub * 2][:, cols], in_ref[sub * 2 + 1][:, cols]], axis=1
+def place_kernel(place_ref, *refs):
+    out_ref = refs[4]
+    for k in range(4):
+        row = pl.multiple_of(lax.rem(place_ref[1] - k + 4, 4) * 16, 16)
+        for x in range(4):
+            cols = slice(x * HW, (x + 1) * HW)
+            out_ref[pl.ds(row, 16), x * 2 * HW:(x + 1) * 2 * HW] = jnp.concatenate(
+                [refs[k][0][:, cols], refs[k][1][:, cols]], axis=1
             )
 
 
@@ -313,17 +302,8 @@
     same = c == zh
     place = jnp.stack([y, zl, c, x]).astype(jnp.int32)
 
-    with jax.named_scope("start"):
-        mod_own = lax.dynamic_index_in_dim(mod_table, step_ids[0], 0, keepdims=False)
-        packed, keep, mate = call(
-            start_kernel,
-            (struct(4, 144, BLOCK, dtype=bf16), struct(4, 24, HALF), struct(4, 24, HALF)),
-            3, 3,
-        )(place, step_ids, step_table, states, mod_own, text_kv)
     with jax.named_scope("weights"):
-        w = call(columns_kernel, struct(48, 3 * HW, dtype=bf16), 1, 0, after=1)(
-            qkv_weight, packed
-        )
+        w = call(columns_kernel, struct(48, 3 * HW, dtype=bf16), 1, 0)(qkv_weight)
         w_b = [permute(w, ("c", "zh"), lambda p, k=k: {"c": p["zh"], "zh": 1 - p["zh"]}
                        if p["c"] == k else None) for k in range(2)]
         w_a = permute(w, ("c", "zh"), lambda p: None if p["c"] == p["zh"] else
@@ -333,6 +313,13 @@
         w2 = jnp.concatenate([w0, w1], axis=0)
         w8 = jnp.stack([w2, shift_z(w2, 1), shift_z(w2, 2), shift_z(w2, -1)])
 
+    with jax.named_scope("start"):
+        mod_own = lax.dynamic_index_in_dim(mod_table, step_ids[0], 0, keepdims=False)
+        packed, keep, mate = call(
+            start_kernel,
+            (struct(4, 144, BLOCK, dtype=bf16), struct(4, 24, HALF), struct(4, 24, HALF)),
+            3, 3, after=1,
+        )(place, step_ids, step_table, states, mod_own, text_kv, w8)
     with jax.named_scope("gather_first"):
         packed = swap_core_zh(packed, same)
         sends = call(send_kernel, (struct(336, BLOCK, dtype=bf16),) * 4, 1, 1)(place, packed)
@@ -340,18 +327,16 @@
         blocks = mine + [shift(b, "c", 1) for b in mine]
 
     with jax.named_scope("weights_y"):
-        w_next, w_last = shift(w8, "y", 1), shift(w8, "y", -1)
-        far_a, far_b = shift(w_next[:2], "y", 1), shift(w_last[2:], "y", -1)
-        pieces = (w8, w_next, far_a, far_b, w_last)
+        pieces = [w8] + [shift(w8, "y", k) for k in (1, -1, 2)]
 
     with jax.named_scope("states"):
         messages = call(message_kernel, (struct(2, 24, HALF),) * 4, 2, 1, after=1)(
-            place, keep, shift(mate, "c", 1), far_b
+            place, keep, shift(mate, "c", 1), pieces[2]
         )
         messages = [messages[0]] + [shift(messages[k], "zl", k) for k in (1, 2, 3)]
 
     with jax.named_scope("weights_y"):
-        weight = call(weight_kernel, struct(D, 3 * HW, dtype=bf16), 5, 1)(place, *pieces)
+        weight = call(weight_kernel, struct(D, 3 * HW, dtype=bf16), 4, 1)(place, *pieces)
 
     text = None
     for sweep in range(SWEEPS):
@@ -374,7 +359,7 @@
                 out_shape=outs,
                 in_specs=[pl.BlockSpec(memory_space=space) for space in spaces],
                 out_specs=tuple(pl.BlockSpec(memory_space=pltpu.VMEM) for _ in outs),
-                compiler_params=pltpu.CompilerParams(vmem_limit_bytes=20 * MIB),
+                compiler_params=pltpu.CompilerParams(vmem_limit_bytes=24 * MIB),
                 cost_estimate=pl.CostEstimate(
                     flops=2 * TOK * D * 3 * HW + 4 * TOK * KEYS * HW,
                     bytes_accessed=24 << 20, transcendentals=3 * TOK * KEYS,
@@ -414,18 +399,21 @@
                 modulated = lax.all_to_all(modulated, ("zl", "zh"), 0, 0).reshape(128, HALF)
                 mine = [modulated] + [shift(modulated, "x", k) for k in (1, 2, 3)]
                 blocks = mine + [shift(b, "c", 1) for b in mine]
+    with jax.named_scope("place"):
+        top, keep, mate = call(
+            final_kernel, (struct(8, 128), struct(4, 16, HALF), struct(4, 16, HALF)), 3, 1
+        )(place, part, lat, totals)
+        top = jnp.concatenate([change, top], axis=0)
+        top = jnp.maximum(top, shift(top, "c", 1))
+        *outs, top = call(
+            message_kernel, (struct(2, 16, HALF),) * 4 + (struct(16, 128),), 3, 1
+        )(place, keep, shift(mate, "c", 1), top)
+        outs = [outs[0]] + [shift(outs[k], "zl", k) for k in (1, 2, 3)]
+        out = call(place_kernel, struct(ROWS, D), 4, 1)(place, *outs)
     with jax.named_scope("changes"):
-        top = call(change_kernel, struct(8, 128), 3, 1)(place, part, lat, totals)
-        top = jnp.concatenate([change, top], axis=0)
         top = functools.reduce(jnp.maximum, [top] + [shift(top, "zl", k) for k in (1, 2, 3)])
-    with jax.named_scope("place"):
-        out = call(new_kernel, struct(8, 16, HALF), 2, 1, after=1)(place, part, totals, top)
-        out = lax.all_to_all(out, ("zl", "c"), 0, 0)
-        out = call(place_kernel, struct(ROWS, D), 1, 0)(out)
-    with jax.named_scope("changes"):
+        top = functools.reduce(jnp.maximum, [top] + [shift(top, "x", k) for k in (1, 2, 3)])
         top = jnp.maximum(top, shift(top, "zh", 1))
-        top = functools.reduce(jnp.maximum, [top] + [shift(top, "x", k) for k in (1, 2, 3)])
-        top = jnp.maximum(top, shift(top, "c", 1))
         top = top[:, 0].reshape(SWEEPS, 8)
         top = lax.dynamic_slice_in_dim(top, zl * 2 + c, 1, axis=1)
     return out[None], top

time: 219 us -> 199 us (0.909)
  waiting for transfers between devices: 66.1 us -> 45.5 us
  starting transfers between devices: 49.7 us -> 58.7 us
  Pallas kernels: 24 us -> 19.7 us
  local copies, waits for them, and re-layouts: 5.23 us -> 2.55 us
    ppermute x38 -> x41, waiting for transfers between devices: 66.1 us -> 45.5 us  [permute(): return lax.ppermute(value, axes if len(axes) > 1 else axes[0], pairs)]
    ppermute x38 -> x41, starting transfers between devices: 46.2 us -> 58.7 us  [permute(): return lax.ppermute(value, axes if len(axes) > 1 else axes[0], pairs)]
    pallas_call x2, Pallas kernels: 15.4 us -> 10.4 us  [on_device(): pl.pallas_call(functools.partial(attention_kernel, sweep == 0), out_shape...]
    all_to_all x1 -> x0, starting transfers between devices: 3.45 us -> none  [on_device(): out = lax.all_to_all(out, ('zl', 'c'), 0, 0)]
    unnamed x11 -> x12, local copies, waits for them, and re-layouts: 5.01 us -> 2.37 us
    all_to_all x2, blocking collectives: 37.4 us -> 39.6 us  [on_device(): attended = lax.all_to_all(attended, ('zl', 'x', 'zh'), 0, 0)]
  transfers between devices with their start and end apart: 39 -> 41, of which waited for: 21 -> 18; matrix products, arithmetic and copies ran while one was open for 1% -> 1% of each run, Pallas kernels for 4% -> 3%
where the time goes in v3:
time: 199 us; the launch traced here: 198 us
  blocking collectives  69.5 us (35%)
  starting transfers between devices  58.7 us (29%)
  waiting for transfers between devices  45.5 us (23%)
  Pallas kernels  19.7 us (10%)
  local copies, waits for them, and re-layouts  2.55 us (1%)
    ppermute x41, starting transfers between devices, permute(): return lax.ppermute(value, axes if len(axes) > 1 else axes[0], pairs)  58.7 us
    ppermute x41, waiting for transfers between devices, permute(): return lax.ppermute(value, axes if len(axes) > 1 else axes[0], pairs)  45.5 us
    all_to_all x2, blocking collectives, on_device(): attended = lax.all_to_all(attended, ('zl', 'x', 'zh'), 0, 0)  39.6 us
    all_to_all x2, blocking collectives, on_device(): totals = lax.all_to_all(total, 'y', 0, 0)  18.3 us
    all_to_all x1, blocking collectives, on_device(): modulated = lax.all_to_all(modulated, ('zl', 'zh'), 0, 0).reshape(128, HALF)  11.6 us
    pallas_call x2, Pallas kernels, on_device(): pl.pallas_call(functools.partial(attention_kernel, sweep == 0), out_shape...  10.4 us
  transfers between devices with their start and end apart: 41, of which 18 were waited for; matrix products, arithmetic and copies ran while one was open for 1% of the time, Pallas kernels for 3%

profile of v3, /device:TPU:8, one launch (start us, length us, event | category | flops | bytes accessed | tf_op | source)
XLA Modules:
  0.0 198.0 jit_solution(11589865558618162454)
XLA Ops:
  0.7 1.1 copy.10.w_ref
  2.5 9.7 %collective-permute-start.1 = (bf16[48,576]{1,0:T(8,128)(2,1)S(1)}, bf16[48,576]{1,0:T(8,128)(2,1)S(1)}, u32[]{:S(2)}, u32[]{:S(2)}) collective-permute-start(bf16[48,576]{1,0:T(8,128)(2,1)S(1)} %weights.1), channel_id=1, source_target_pairs={{0,1},{1,8},{2,3},{3,10},{4,5},{5,12},{6,7},{7,14},{16,17},{17,24}... | collective-permute-start | bytes 165896 | tf_op jit(solution)/shard_map/weights/ppermute | solution.py:41
  12.3 1.3 collective-permute-start
  14.3 1.1 collective-permute-done
  15.5 1.6 collective-permute-start.4
  17.0 1.0 collective-permute-start.3
  18.1 2.2 %collective-permute-start.5 = (bf16[96,576]{1,0:T(8,128)(2,1)S(1)}, bf16[96,576]{1,0:T(8,128)(2,1)S(1)}, u32[]{:S(2)}, u32[]{:S(2)}) collective-permute-start(bf16[96,576]{1,0:T(8,128)(2,1)S(1)} %get-tuple-element.65), channel_id=1, source_target_pairs={{0,49},{1,48},{16,0},{17,1},{32,16},{33,17},{48,32},{49,33},{2,51}... | collective-permute-start | bytes 331784 | tf_op jit(solution)/shard_map/weights/ppermute | solution.py:41
  20.4 2.6 %collective-permute-done.4 = bf16[96,576]{1,0:T(8,128)(2,1)S(1)} collective-permute-done((bf16[96,576]{1,0:T(8,128)(2,1)S(1)}, bf16[96,576]{1,0:T(8,128)(2,1)S(1)}, u32[]{:S(2)}, u32[]{:S(2)}) %collective-permute-start.4) | collective-permute-done | bytes 110624 | tf_op jit(solution)/shard_map/weights/ppermute | solution.py:41
  22.9 2.1 %collective-permute-done.3 = bf16[96,576]{1,0:T(8,128)(2,1)S(1)} collective-permute-done((bf16[96,576]{1,0:T(8,128)(2,1)S(1)}, bf16[96,576]{1,0:T(8,128)(2,1)S(1)}, u32[]{:S(2)}, u32[]{:S(2)}) %collective-permute-start.3) | collective-permute-done | bytes 110624 | tf_op jit(solution)/shard_map/weights/ppermute | solution.py:41
  25.8 1.2 start.1
  27.7 2.4 %collective-permute-start.16 = (bf16[4,96,576]{2,1,0:T(8,128)(2,1)S(1)}, bf16[4,96,576]{2,1,0:T(8,128)(2,1)S(1)}, u32[]{:S(2)}, u32[]{:S(2)}) collective-permute-start(bf16[4,96,576]{2,1,0:T(8,128)(2,1)S(1)} %pad_maximum_fusion.after_ref.refs_0_), channel_id=1, source_target_pairs={{0,128},{64,192},{128,0},{192,64},{1,129},{65,193},{129,1},{193,65... | collective-permute-start | bytes 1327112 | tf_op jit(solution)/shard_map/weights_y/ppermute | solution.py:41
  30.1 10.0 %collective-permute-start.17 = (f32[4,24,768]{2,1,0:T(8,128)S(1)}, f32[4,24,768]{2,1,0:T(8,128)S(1)}, u32[]{:S(2)}, u32[]{:S(2)}) collective-permute-start(f32[4,24,768]{2,1,0:T(8,128)S(1)} %get-tuple-element.38), channel_id=1, source_target_pairs={{0,8},{8,0},{1,9},{9,1},{2,10},{10,2},{3,11},{11,3},{4,12},{12,4},... | collective-permute-start | bytes 884744 | tf_op jit(solution)/shard_map/states/ppermute | solution.py:41
  40.0 1.3 collective-permute-start.15
  42.1 1.6 collective-permute-start.7
  43.7 2.7 %collective-permute-start.8 = (bf16[336,384]{1,0:T(8,128)(2,1)S(1)}, bf16[336,384]{1,0:T(8,128)(2,1)S(1)}, u32[]{:S(2)}, u32[]{:S(2)}) collective-permute-start(bf16[336,384]{1,0:T(8,128)(2,1)S(1)} %get-tuple-element.34), channel_id=1, source_target_pairs={{0,4},{2,6},{4,0},{6,2},{1,5},{3,7},{5,1},{7,3},{8,12},{10,14},{12... | collective-permute-start | bytes 774152 | tf_op jit(solution)/shard_map/gather_first/ppermute | solution.py:41
  46.4 1.4 collective-permute-start.9
  48.5 9.4 %collective-permute-done.15.refs_2_.extra_ref = bf16[4,96,576]{2,1,0:T(8,128)(2,1)S(1)} collective-permute-done((bf16[4,96,576]{2,1,0:T(8,128)(2,1)S(1)}, bf16[4,96,576]{2,1,0:T(8,128)(2,1)S(1)}, u32[]{:S(2)}, u32[]{:S(2)}) %collective-permute-start.15) | collective-permute-done | bytes 442400 | tf_op jit(solution)/shard_map/weights_y/ppermute | solution.py:41
  58.4 1.6 collective-permute-start.12
  60.7 3.4 %collective-permute-start.19 = (f32[2,24,768]{2,1,0:T(8,128)S(1)}, f32[2,24,768]{2,1,0:T(8,128)S(1)}, u32[]{:S(2)}, u32[]{:S(2)}) collective-permute-start(f32[2,24,768]{2,1,0:T(8,128)S(1)} %get-tuple-element.40), channel_id=1, source_target_pairs={{0,32},{16,48},{32,0},{48,16},{1,33},{17,49},{33,1},{49,17},{2,34}... | collective-permute-start | bytes 442376 | tf_op jit(solution)/shard_map/states/ppermute | solution.py:41
  65.5 5.0 %attention.2 = (bf16[32,24,128]{2,1,0:T(8,128)(2,1)S(1)}, bf16[2,320,192]{2,1,0:T(8,128)(2,1)S(1)}) custom-call(s32[4]{0:T(128)S(1)} %pad_add_fusion.place_ref, bf16[336,384]{1,0:T(8,128)(2,1)S(1)} %get-tuple-element.32.refs_0_, bf16[336,384]{1,0:T(8,128)(2,1)S(1)} %collective-permute-done.7.refs_1_, bf16[336,384]{1,0:T(8,128)(2,1)S(1)} %collective-permute-done.8.refs_2_, ...), custom_call_target="tpu_custom_call" | custom-call | flops 1233125376 | bytes 25165824 | tf_op jit(solution)/shard_map/attention/pallas_call | solution.py:357
  70.5 4.3 %collective-permute-done.19.refs_1_.refs_2_ = f32[2,24,768]{2,1,0:T(8,128)S(1)} collective-permute-done((f32[2,24,768]{2,1,0:T(8,128)S(1)}, f32[2,24,768]{2,1,0:T(8,128)S(1)}, u32[]{:S(2)}, u32[]{:S(2)}) %collective-permute-start.19) | collective-permute-done | bytes 147488 | tf_op jit(solution)/shard_map/states/ppermute | solution.py:41
  74.8 22.2 %all_to_all.25.att_ref = bf16[32,24,128]{2,1,0:T(8,128)(2,1)S(1)} all-to-all(bf16[32,24,128]{2,1,0:T(8,128)(2,1)S(1)} %to_prefix.1), channel_id=1, replica_groups=mesh['y'=4,'zl'=4,'c'=2,'x'=4,'zh'=2] {'zl','x','zh'}, dimensions={0} | all-to-all | bytes 393216 | tf_op jit(solution)/shard_map/to_prefix/all_to_all | solution.py:375
  97.8 9.6 %all_to_all.26.totals_ref = f32[4,16,768]{2,1,0:T(8,128)S(1)} all-to-all(f32[4,16,768]{2,1,0:T(8,128)S(1)} %get-tuple-element.45), channel_id=1, replica_groups=mesh['y'=4,'zl'=4,'c'=2,'x'=4,'zh'=2] {'y'}, dimensions={0} | all-to-all | bytes 393216 | tf_op jit(solution)/shard_map/prefix/all_to_all | solution.py:387
  108.2 1.2 collective-permute-done.21.other_ref
  109.7 11.6 %all_to_all.27 = bf16[8,16,768]{2,1,0:T(8,128)(2,1)S(1)} all-to-all(bf16[8,16,768]{2,1,0:T(8,128)(2,1)S(1)} %norm.1), channel_id=1, replica_groups=mesh['y'=4,'zl'=4,'c'=2,'x'=4,'zh'=2] {'zl','zh'}, dimensions={0} | all-to-all | bytes 393216 | tf_op jit(solution)/shard_map/gather/all_to_all | solution.py:399
  121.3 1.7 collective-permute-start.24
  123.0 1.0 collective-permute-start.23
  124.0 6.1 %collective-permute-done.24.refs_3_ = bf16[128,768]{1,0:T(8,128)(2,1)S(1)} collective-permute-done((bf16[128,768]{1,0:T(8,128)(2,1)S(1)}, bf16[128,768]{1,0:T(8,128)(2,1)S(1)}, u32[]{:S(2)}, u32[]{:S(2)}) %collective-permute-start.24) | collective-permute-done | bytes 196640 | tf_op jit(solution)/shard_map/gather/ppermute | solution.py:41
  130.1 1.7 collective-permute-done.23.refs_2_
  131.7 2.0 %collective-permute-done.22.refs_1_ = bf16[128,768]{1,0:T(8,128)(2,1)S(1)} collective-permute-done((bf16[128,768]{1,0:T(8,128)(2,1)S(1)}, bf16[128,768]{1,0:T(8,128)(2,1)S(1)}, u32[]{:S(2)}, u32[]{:S(2)}) %collective-permute-start.22) | collective-permute-done | bytes 196640 | tf_op jit(solution)/shard_map/gather/ppermute | solution.py:41
  133.8 1.4 collective-permute-done.26.refs_5_
  135.2 5.4 %attention.3 = bf16[32,24,128]{2,1,0:T(8,128)(2,1)S(1)} custom-call(s32[4]{0:T(128)S(1)} %pad_add_fusion.place_ref, bf16[128,768]{1,0:T(8,128)(2,1)S(1)} %bitcast.22, bf16[128,768]{1,0:T(8,128)(2,1)S(1)} %collective-permute-done.22.refs_1_, bf16[128,768]{1,0:T(8,128)(2,1)S(1)} %collective-permute-done.23.refs_2_, ...), custom_call_target="tpu_custom_call" | custom-call | flops 1233125376 | bytes 25165824 | tf_op jit(solution)/shard_map/attention/pallas_call | solution.py:357
  140.6 17.4 %all_to_all.28.att_ref = bf16[32,24,128]{2,1,0:T(8,128)(2,1)S(1)} all-to-all(bf16[32,24,128]{2,1,0:T(8,128)(2,1)S(1)} %attention.3), channel_id=1, replica_groups=mesh['y'=4,'zl'=4,'c'=2,'x'=4,'zh'=2] {'zl','x','zh'}, dimensions={0} | all-to-all | bytes 393216 | tf_op jit(solution)/shard_map/to_prefix/all_to_all | solution.py:375
  158.7 8.7 %all_to_all.29.totals_ref = f32[4,16,768]{2,1,0:T(8,128)S(1)} all-to-all(f32[4,16,768]{2,1,0:T(8,128)S(1)} %get-tuple-element.50), channel_id=1, replica_groups=mesh['y'=4,'zl'=4,'c'=2,'x'=4,'zh'=2] {'y'}, dimensions={0} | all-to-all | bytes 393216 | tf_op jit(solution)/shard_map/prefix/all_to_all | solution.py:387
  167.4 1.6 place.3
  171.2 1.5 collective-permute-start.36
  172.7 1.7 collective-permute-start.35
  175.1 2.3 %collective-permute-done.35 = f32[16,128]{1,0:T(8,128)S(1)} collective-permute-done((f32[16,128]{1,0:T(8,128)S(1)}, f32[16,128]{1,0:T(8,128)S(1)}, u32[]{:S(2)}, u32[]{:S(2)}) %collective-permute-start.35) | collective-permute-done | bytes 8224 | tf_op jit(solution)/shard_map/changes/ppermute | solution.py:41
  177.3 2.5 %collective-permute-done.34 = f32[16,128]{1,0:T(8,128)S(1)} collective-permute-done((f32[16,128]{1,0:T(8,128)S(1)}, f32[16,128]{1,0:T(8,128)S(1)}, u32[]{:S(2)}, u32[]{:S(2)}) %collective-permute-start.34) | collective-permute-done | bytes 8224 | tf_op jit(solution)/shard_map/changes/ppermute | solution.py:41
  179.9 1.2 collective-permute-start.39
  181.1 1.4 collective-permute-start.38
  182.5 1.0 collective-permute-done.39
  183.5 2.7 %collective-permute-done.38 = f32[16,128]{1,0:T(8,128)S(1)} collective-permute-done((f32[16,128]{1,0:T(8,128)S(1)}, f32[16,128]{1,0:T(8,128)S(1)}, u32[]{:S(2)}, u32[]{:S(2)}) %collective-permute-start.38) | collective-permute-done | bytes 8224 | tf_op jit(solution)/shard_map/changes/ppermute | solution.py:41
  186.3 1.1 collective-permute-done.37
  187.4 1.5 collective-permute-start.40
  189.5 3.2 %collective-permute-start.33 = (f32[2,16,768]{2,1,0:T(8,128)S(1)}, f32[2,16,768]{2,1,0:T(8,128)S(1)}, u32[]{:S(2)}, u32[]{:S(2)}) collective-permute-start(f32[2,16,768]{2,1,0:T(8,128)S(1)} %get-tuple-element.58), channel_id=1, source_target_pairs={{0,48},{16,0},{32,16},{48,32},{1,49},{17,1},{33,17},{49,33},{2,50}... | collective-permute-start | bytes 294920 | tf_op jit(solution)/shard_map/place/ppermute | solution.py:41
  192.7 2.4 %collective-permute-done.40 = f32[16,128]{1,0:T(8,128)S(1)} collective-permute-done((f32[16,128]{1,0:T(8,128)S(1)}, f32[16,128]{1,0:T(8,128)S(1)}, u32[]{:S(2)}, u32[]{:S(2)}) %collective-permute-start.40) | collective-permute-done | bytes 8224 | tf_op jit(solution)/shard_map/changes/ppermute | solution.py:41
  196.6 1.4 place.5
  (79 shorter events, 13.8 us)
Async XLA Ops:
  0.6 13.6 %copy-start = (f32[128,3,1536]{2,0,1:T(8,128)S(1)}, f32[128,3,1536]{2,0,1:T(8,128)}, u32[]{:S(2)}) copy-start(f32[128,3,1536]{2,0,1:T(8,128)} %param.9) | copy-start | bytes 7077892
  0.6 24.5 %copy-start.2 = (bf16[1,40,2,1536]{3,2,1,0:T(2,128)(2,1)S(1)}, bf16[1,40,2,1536]{3,2,1,0:T(2,128)(2,1)}, u32[]{:S(2)}) copy-start(bf16[1,40,2,1536]{3,2,1,0:T(2,128)(2,1)} %text_ref.1) | copy-start | bytes 737284
  0.7 24.5 %copy-start.1 = (f32[1,64,1536]{2,1,0:T(8,128)S(1)}, f32[1,64,1536]{2,1,0:T(8,128)}, u32[]{:S(2)}) copy-start(f32[1,64,1536]{2,1,0:T(8,128)} %lat_ref.1) | copy-start | bytes 1179652
  1.9 12.4 %collective-permute-start.2 = (bf16[48,576]{1,0:T(8,128)(2,1)S(1)}, bf16[48,576]{1,0:T(8,128)(2,1)S(1)}, u32[]{:S(2)}, u32[]{:S(2)}) collective-permute-start(bf16[48,576]{1,0:T(8,128)(2,1)S(1)} %weights.1), channel_id=1, source_target_pairs={{8,1},{9,8},{10,3},{11,10},{12,5},{13,12},{14,7},{15,14},{24,17},{... | collective-permute-start | bytes 165896 | tf_op jit(solution)/shard_map/weights/ppermute | solution.py:41
  2.5 11.8 %collective-permute-start.1 = (bf16[48,576]{1,0:T(8,128)(2,1)S(1)}, bf16[48,576]{1,0:T(8,128)(2,1)S(1)}, u32[]{:S(2)}, u32[]{:S(2)}) collective-permute-start(bf16[48,576]{1,0:T(8,128)(2,1)S(1)} %weights.1), channel_id=1, source_target_pairs={{0,1},{1,8},{2,3},{3,10},{4,5},{5,12},{6,7},{7,14},{16,17},{17,24}... | collective-permute-start | bytes 165896 | tf_op jit(solution)/shard_map/weights/ppermute | solution.py:41
  12.3 3.1 %collective-permute-start = (bf16[48,576]{1,0:T(8,128)(2,1)S(1)}, bf16[48,576]{1,0:T(8,128)(2,1)S(1)}, u32[]{:S(2)}, u32[]{:S(2)}) collective-permute-start(bf16[48,576]{1,0:T(8,128)(2,1)S(1)} %weights.1), channel_id=1, source_target_pairs={{1,9},{8,0},{3,11},{10,2},{5,13},{12,4},{7,15},{14,6},{17,25},{24,... | collective-permute-start | bytes 165896 | tf_op jit(solution)/shard_map/weights/ppermute | solution.py:41
  15.5 7.5 %collective-permute-start.4 = (bf16[96,576]{1,0:T(8,128)(2,1)S(1)}, bf16[96,576]{1,0:T(8,128)(2,1)S(1)}, u32[]{:S(2)}, u32[]{:S(2)}) collective-permute-start(bf16[96,576]{1,0:T(8,128)(2,1)S(1)} %get-tuple-element.65), channel_id=1, source_target_pairs={{0,32},{1,33},{16,48},{17,49},{32,1},{33,0},{48,17},{49,16},{2,34}... | collective-permute-start | bytes 331784 | tf_op jit(solution)/shard_map/weights/ppermute | solution.py:41
  17.0 8.0 %collective-permute-start.3 = (bf16[96,576]{1,0:T(8,128)(2,1)S(1)}, bf16[96,576]{1,0:T(8,128)(2,1)S(1)}, u32[]{:S(2)}, u32[]{:S(2)}) collective-permute-start(bf16[96,576]{1,0:T(8,128)(2,1)S(1)} %get-tuple-element.65), channel_id=1, source_target_pairs={{0,16},{1,17},{16,32},{17,33},{32,48},{33,49},{48,1},{49,0},{2,18}... | collective-permute-start | bytes 331784 | tf_op jit(solution)/shard_map/weights/ppermute | solution.py:41
  18.1 7.0 %collective-permute-start.5 = (bf16[96,576]{1,0:T(8,128)(2,1)S(1)}, bf16[96,576]{1,0:T(8,128)(2,1)S(1)}, u32[]{:S(2)}, u32[]{:S(2)}) collective-permute-start(bf16[96,576]{1,0:T(8,128)(2,1)S(1)} %get-tuple-element.65), channel_id=1, source_target_pairs={{0,49},{1,48},{16,0},{17,1},{32,16},{33,17},{48,32},{49,33},{2,51}... | collective-permute-start | bytes 331784 | tf_op jit(solution)/shard_map/weights/ppermute | solution.py:41
  25.2 0.7 copy-start.3
  27.0 14.4 %collective-permute-start.6 = (bf16[4,144,384]{2,1,0:T(8,128)(2,1)S(1)}, bf16[4,144,384]{2,1,0:T(8,128)(2,1)S(1)}, u32[]{:S(2)}, u32[]{:S(2)}) collective-permute-start(bf16[4,144,384]{2,1,0:T(8,128)(2,1)S(1)} %get-tuple-element.31), channel_id=1, source_target_pairs={{1,8},{8,1},{3,10},{10,3},{5,12},{12,5},{7,14},{14,7},{17,24},{24,... | collective-permute-start | bytes 1327112 | tf_op jit(solution)/shard_map/gather_first/ppermute | solution.py:41
  27.7 20.1 %collective-permute-start.16 = (bf16[4,96,576]{2,1,0:T(8,128)(2,1)S(1)}, bf16[4,96,576]{2,1,0:T(8,128)(2,1)S(1)}, u32[]{:S(2)}, u32[]{:S(2)}) collective-permute-start(bf16[4,96,576]{2,1,0:T(8,128)(2,1)S(1)} %pad_maximum_fusion.after_ref.refs_0_), channel_id=1, source_target_pairs={{0,128},{64,192},{128,0},{192,64},{1,129},{65,193},{129,1},{193,65... | collective-permute-start | bytes 1327112 | tf_op jit(solution)/shard_map/weights_y/ppermute | solution.py:41
  30.1 16.3 %collective-permute-start.17 = (f32[4,24,768]{2,1,0:T(8,128)S(1)}, f32[4,24,768]{2,1,0:T(8,128)S(1)}, u32[]{:S(2)}, u32[]{:S(2)}) collective-permute-start(f32[4,24,768]{2,1,0:T(8,128)S(1)} %get-tuple-element.38), channel_id=1, source_target_pairs={{0,8},{8,0},{1,9},{9,1},{2,10},{10,2},{3,11},{11,3},{4,12},{12,4},... | collective-permute-start | bytes 884744 | tf_op jit(solution)/shard_map/states/ppermute | solution.py:41
  40.0 17.9 %collective-permute-start.15 = (bf16[4,96,576]{2,1,0:T(8,128)(2,1)S(1)}, bf16[4,96,576]{2,1,0:T(8,128)(2,1)S(1)}, u32[]{:S(2)}, u32[]{:S(2)}) collective-permute-start(bf16[4,96,576]{2,1,0:T(8,128)(2,1)S(1)} %pad_maximum_fusion.after_ref.refs_0_), channel_id=1, source_target_pairs={{0,192},{64,0},{128,64},{192,128},{1,193},{65,1},{129,65},{193,129... | collective-permute-start | bytes 1327112 | tf_op jit(solution)/shard_map/weights_y/ppermute | solution.py:41
  42.1 15.8 %collective-permute-start.7 = (bf16[336,384]{1,0:T(8,128)(2,1)S(1)}, bf16[336,384]{1,0:T(8,128)(2,1)S(1)}, u32[]{:S(2)}, u32[]{:S(2)}) collective-permute-start(bf16[336,384]{1,0:T(8,128)(2,1)S(1)} %get-tuple-element.33), channel_id=1, source_target_pairs={{0,2},{2,4},{4,6},{6,0},{1,3},{3,5},{5,7},{7,1},{8,10},{10,12},{12... | collective-permute-start | bytes 774152 | tf_op jit(solution)/shard_map/gather_first/ppermute | solution.py:41
  43.7 14.8 %collective-permute-start.8 = (bf16[336,384]{1,0:T(8,128)(2,1)S(1)}, bf16[336,384]{1,0:T(8,128)(2,1)S(1)}, u32[]{:S(2)}, u32[]{:S(2)}) collective-permute-start(bf16[336,384]{1,0:T(8,128)(2,1)S(1)} %get-tuple-element.34), channel_id=1, source_target_pairs={{0,4},{2,6},{4,0},{6,2},{1,5},{3,7},{5,1},{7,3},{8,12},{10,14},{12... | collective-permute-start | bytes 774152 | tf_op jit(solution)/shard_map/gather_first/ppermute | solution.py:41
  46.4 13.6 %collective-permute-start.9 = (bf16[336,384]{1,0:T(8,128)(2,1)S(1)}, bf16[336,384]{1,0:T(8,128)(2,1)S(1)}, u32[]{:S(2)}, u32[]{:S(2)}) collective-permute-start(bf16[336,384]{1,0:T(8,128)(2,1)S(1)} %get-tuple-element.35), channel_id=1, source_target_pairs={{0,6},{2,0},{4,2},{6,4},{1,7},{3,1},{5,3},{7,5},{8,14},{10,8},{12,... | collective-permute-start | bytes 774152 | tf_op jit(solution)/shard_map/gather_first/ppermute | solution.py:41
  47.8 12.8 %collective-permute-start.14 = (bf16[4,96,576]{2,1,0:T(8,128)(2,1)S(1)}, bf16[4,96,576]{2,1,0:T(8,128)(2,1)S(1)}, u32[]{:S(2)}, u32[]{:S(2)}) collective-permute-start(bf16[4,96,576]{2,1,0:T(8,128)(2,1)S(1)} %pad_maximum_fusion.after_ref.refs_0_), channel_id=1, source_target_pairs={{0,64},{64,128},{128,192},{192,0},{1,65},{65,129},{129,193},{193,1... | collective-permute-start | bytes 1327112 | tf_op jit(solution)/shard_map/weights_y/ppermute | solution.py:41
  57.9 2.8 %collective-permute-start.10 = (bf16[336,384]{1,0:T(8,128)(2,1)S(1)}, bf16[336,384]{1,0:T(8,128)(2,1)S(1)}, u32[]{:S(2)}, u32[]{:S(2)}) collective-permute-start(bf16[336,384]{1,0:T(8,128)(2,1)S(1)} %get-tuple-element.32.refs_0_), channel_id=1, source_target_pairs={{0,8},{8,0},{1,9},{9,1},{2,10},{10,2},{3,11},{11,3},{4,12},{12,4},... | collective-permute-start | bytes 774152 | tf_op jit(solution)/shard_map/gather_first/ppermute | solution.py:41
  57.9 6.2 %collective-permute-start.11 = (bf16[336,384]{1,0:T(8,128)(2,1)S(1)}, bf16[336,384]{1,0:T(8,128)(2,1)S(1)}, u32[]{:S(2)}, u32[]{:S(2)}) collective-permute-start(bf16[336,384]{1,0:T(8,128)(2,1)S(1)} %collective-permute-done.7.refs_1_), channel_id=1, source_target_pairs={{0,8},{8,0},{1,9},{9,1},{2,10},{10,2},{3,11},{11,3},{4,12},{12,4},... | collective-permute-start | bytes 774152 | tf_op jit(solution)/shard_map/gather_first/ppermute | solution.py:41
  58.4 7.1 %collective-permute-start.12 = (bf16[336,384]{1,0:T(8,128)(2,1)S(1)}, bf16[336,384]{1,0:T(8,128)(2,1)S(1)}, u32[]{:S(2)}, u32[]{:S(2)}) collective-permute-start(bf16[336,384]{1,0:T(8,128)(2,1)S(1)} %collective-permute-done.8.refs_2_), channel_id=1, source_target_pairs={{0,8},{8,0},{1,9},{9,1},{2,10},{10,2},{3,11},{11,3},{4,12},{12,4},... | collective-permute-start | bytes 774152 | tf_op jit(solution)/shard_map/gather_first/ppermute | solution.py:41
  60.0 5.5 %collective-permute-start.13 = (bf16[336,384]{1,0:T(8,128)(2,1)S(1)}, bf16[336,384]{1,0:T(8,128)(2,1)S(1)}, u32[]{:S(2)}, u32[]{:S(2)}) collective-permute-start(bf16[336,384]{1,0:T(8,128)(2,1)S(1)} %collective-permute-done.9.refs_3_), channel_id=1, source_target_pairs={{0,8},{8,0},{1,9},{9,1},{2,10},{10,2},{3,11},{11,3},{4,12},{12,4},... | collective-permute-start | bytes 774152 | tf_op jit(solution)/shard_map/gather_first/ppermute | solution.py:41
  60.6 9.9 %collective-permute-start.18 = (f32[2,24,768]{2,1,0:T(8,128)S(1)}, f32[2,24,768]{2,1,0:T(8,128)S(1)}, u32[]{:S(2)}, u32[]{:S(2)}) collective-permute-start(f32[2,24,768]{2,1,0:T(8,128)S(1)} %get-tuple-element.39), channel_id=1, source_target_pairs={{0,16},{16,32},{32,48},{48,0},{1,17},{17,33},{33,49},{49,1},{2,18}... | collective-permute-start | bytes 442376 | tf_op jit(solution)/shard_map/states/ppermute | solution.py:41
  60.7 14.0 %collective-permute-start.19 = (f32[2,24,768]{2,1,0:T(8,128)S(1)}, f32[2,24,768]{2,1,0:T(8,128)S(1)}, u32[]{:S(2)}, u32[]{:S(2)}) collective-permute-start(f32[2,24,768]{2,1,0:T(8,128)S(1)} %get-tuple-element.40), channel_id=1, source_target_pairs={{0,32},{16,48},{32,0},{48,16},{1,33},{17,49},{33,1},{49,17},{2,34}... | collective-permute-start | bytes 442376 | tf_op jit(solution)/shard_map/states/ppermute | solution.py:41
  64.2 10.6 %collective-permute-start.20 = (f32[2,24,768]{2,1,0:T(8,128)S(1)}, f32[2,24,768]{2,1,0:T(8,128)S(1)}, u32[]{:S(2)}, u32[]{:S(2)}) collective-permute-start(f32[2,24,768]{2,1,0:T(8,128)S(1)} %get-tuple-element.41), channel_id=1, source_target_pairs={{0,48},{16,0},{32,16},{48,32},{1,49},{17,1},{33,17},{49,33},{2,50}... | collective-permute-start | bytes 442376 | tf_op jit(solution)/shard_map/states/ppermute | solution.py:41
  108.1 1.3 collective-permute-start.21
  121.3 8.8 %collective-permute-start.24 = (bf16[128,768]{1,0:T(8,128)(2,1)S(1)}, bf16[128,768]{1,0:T(8,128)(2,1)S(1)}, u32[]{:S(2)}, u32[]{:S(2)}) collective-permute-start(bf16[128,768]{1,0:T(8,128)(2,1)S(1)} %bitcast.18), channel_id=1, source_target_pairs={{0,6},{2,0},{4,2},{6,4},{1,7},{3,1},{5,3},{7,5},{8,14},{10,8},{12,... | collective-permute-start | bytes 589832 | tf_op jit(solution)/shard_map/gather/ppermute | solution.py:41
  123.0 8.8 %collective-permute-start.23 = (bf16[128,768]{1,0:T(8,128)(2,1)S(1)}, bf16[128,768]{1,0:T(8,128)(2,1)S(1)}, u32[]{:S(2)}, u32[]{:S(2)}) collective-permute-start(bf16[128,768]{1,0:T(8,128)(2,1)S(1)} %bitcast.19), channel_id=1, source_target_pairs={{0,4},{2,6},{4,0},{6,2},{1,5},{3,7},{5,1},{7,3},{8,12},{10,14},{12... | collective-permute-start | bytes 589832 | tf_op jit(solution)/shard_map/gather/ppermute | solution.py:41
  123.9 9.8 %collective-permute-start.22 = (bf16[128,768]{1,0:T(8,128)(2,1)S(1)}, bf16[128,768]{1,0:T(8,128)(2,1)S(1)}, u32[]{:S(2)}, u32[]{:S(2)}) collective-permute-start(bf16[128,768]{1,0:T(8,128)(2,1)S(1)} %bitcast.20), channel_id=1, source_target_pairs={{0,2},{2,4},{4,6},{6,0},{1,3},{3,5},{5,7},{7,1},{8,10},{10,12},{12... | collective-permute-start | bytes 589832 | tf_op jit(solution)/shard_map/gather/ppermute | solution.py:41
  124.0 9.8 %collective-permute-start.25 = (bf16[128,768]{1,0:T(8,128)(2,1)S(1)}, bf16[128,768]{1,0:T(8,128)(2,1)S(1)}, u32[]{:S(2)}, u32[]{:S(2)}) collective-permute-start(bf16[128,768]{1,0:T(8,128)(2,1)S(1)} %bitcast.21), channel_id=1, source_target_pairs={{0,8},{8,0},{1,9},{9,1},{2,10},{10,2},{3,11},{11,3},{4,12},{12,4},... | collective-permute-start | bytes 589832 | tf_op jit(solution)/shard_map/gather/ppermute | solution.py:41
  130.1 3.7 %collective-permute-start.28 = (bf16[128,768]{1,0:T(8,128)(2,1)S(1)}, bf16[128,768]{1,0:T(8,128)(2,1)S(1)}, u32[]{:S(2)}, u32[]{:S(2)}) collective-permute-start(bf16[128,768]{1,0:T(8,128)(2,1)S(1)} %collective-permute-done.24.refs_3_), channel_id=1, source_target_pairs={{0,8},{8,0},{1,9},{9,1},{2,10},{10,2},{3,11},{11,3},{4,12},{12,4},... | collective-permute-start | bytes 589832 | tf_op jit(solution)/shard_map/gather/ppermute | solution.py:41
  131.7 2.0 %collective-permute-start.27 = (bf16[128,768]{1,0:T(8,128)(2,1)S(1)}, bf16[128,768]{1,0:T(8,128)(2,1)S(1)}, u32[]{:S(2)}, u32[]{:S(2)}) collective-permute-start(bf16[128,768]{1,0:T(8,128)(2,1)S(1)} %collective-permute-done.23.refs_2_), channel_id=1, source_target_pairs={{0,8},{8,0},{1,9},{9,1},{2,10},{10,2},{3,11},{11,3},{4,12},{12,4},... | collective-permute-start | bytes 589832 | tf_op jit(solution)/shard_map/gather/ppermute | solution.py:41
  133.7 1.4 collective-permute-start.26
  169.0 1.5 collective-permute-start.29
  169.1 1.4 collective-permute-start.30
  171.2 3.9 %collective-permute-start.36 = (f32[16,128]{1,0:T(8,128)S(1)}, f32[16,128]{1,0:T(8,128)S(1)}, u32[]{:S(2)}, u32[]{:S(2)}) collective-permute-start(f32[16,128]{1,0:T(8,128)S(1)} %get-tuple-element.59), channel_id=1, source_target_pairs={{0,48},{16,0},{32,16},{48,32},{1,49},{17,1},{33,17},{49,33},{2,50}... | collective-permute-start | bytes 24584 | tf_op jit(solution)/shard_map/changes/ppermute | solution.py:41
  172.7 4.6 %collective-permute-start.35 = (f32[16,128]{1,0:T(8,128)S(1)}, f32[16,128]{1,0:T(8,128)S(1)}, u32[]{:S(2)}, u32[]{:S(2)}) collective-permute-start(f32[16,128]{1,0:T(8,128)S(1)} %get-tuple-element.59), channel_id=1, source_target_pairs={{0,32},{16,48},{32,0},{48,16},{1,33},{17,49},{33,1},{49,17},{2,34}... | collective-permute-start | bytes 24584 | tf_op jit(solution)/shard_map/changes/ppermute | solution.py:41
  174.4 5.4 %collective-permute-start.34 = (f32[16,128]{1,0:T(8,128)S(1)}, f32[16,128]{1,0:T(8,128)S(1)}, u32[]{:S(2)}, u32[]{:S(2)}) collective-permute-start(f32[16,128]{1,0:T(8,128)S(1)} %get-tuple-element.59), channel_id=1, source_target_pairs={{0,16},{16,32},{32,48},{48,0},{1,17},{17,33},{33,49},{49,1},{2,18}... | collective-permute-start | bytes 24584 | tf_op jit(solution)/shard_map/changes/ppermute | solution.py:41
  179.9 3.7 %collective-permute-start.39 = (f32[16,128]{1,0:T(8,128)S(1)}, f32[16,128]{1,0:T(8,128)S(1)}, u32[]{:S(2)}, u32[]{:S(2)}) collective-permute-start(f32[16,128]{1,0:T(8,128)S(1)} %maximum_maximum_fusion.1), channel_id=1, source_target_pairs={{0,6},{2,0},{4,2},{6,4},{1,7},{3,1},{5,3},{7,5},{8,14},{10,8},{12,... | collective-permute-start | bytes 24584 | tf_op jit(solution)/shard_map/changes/ppermute | solution.py:41
  181.1 5.2 %collective-permute-start.38 = (f32[16,128]{1,0:T(8,128)S(1)}, f32[16,128]{1,0:T(8,128)S(1)}, u32[]{:S(2)}, u32[]{:S(2)}) collective-permute-start(f32[16,128]{1,0:T(8,128)S(1)} %maximum_maximum_fusion.1), channel_id=1, source_target_pairs={{0,4},{2,6},{4,0},{6,2},{1,5},{3,7},{5,1},{7,3},{8,12},{10,14},{12... | collective-permute-start | bytes 24584 | tf_op jit(solution)/shard_map/changes/ppermute | solution.py:41
  182.5 4.9 %collective-permute-start.37 = (f32[16,128]{1,0:T(8,128)S(1)}, f32[16,128]{1,0:T(8,128)S(1)}, u32[]{:S(2)}, u32[]{:S(2)}) collective-permute-start(f32[16,128]{1,0:T(8,128)S(1)} %maximum_maximum_fusion.1), channel_id=1, source_target_pairs={{0,2},{2,4},{4,6},{6,0},{1,3},{3,5},{5,7},{7,1},{8,10},{10,12},{12... | collective-permute-start | bytes 24584 | tf_op jit(solution)/shard_map/changes/ppermute | solution.py:41
  187.4 7.8 %collective-permute-start.40 = (f32[16,128]{1,0:T(8,128)S(1)}, f32[16,128]{1,0:T(8,128)S(1)}, u32[]{:S(2)}, u32[]{:S(2)}) collective-permute-start(f32[16,128]{1,0:T(8,128)S(1)} %maximum_maximum_fusion), channel_id=1, source_target_pairs={{0,1},{1,0},{2,3},{3,2},{4,5},{5,4},{6,7},{7,6},{8,9},{9,8},{10,11... | collective-permute-start | bytes 24584 | tf_op jit(solution)/shard_map/changes/ppermute | solution.py:41
  188.9 7.1 %collective-permute-start.31 = (f32[2,16,768]{2,1,0:T(8,128)S(1)}, f32[2,16,768]{2,1,0:T(8,128)S(1)}, u32[]{:S(2)}, u32[]{:S(2)}) collective-permute-start(f32[2,16,768]{2,1,0:T(8,128)S(1)} %get-tuple-element.56), channel_id=1, source_target_pairs={{0,16},{16,32},{32,48},{48,0},{1,17},{17,33},{33,49},{49,1},{2,18}... | collective-permute-start | bytes 294920 | tf_op jit(solution)/shard_map/place/ppermute | solution.py:41
  188.9 7.7 %collective-permute-start.32 = (f32[2,16,768]{2,1,0:T(8,128)S(1)}, f32[2,16,768]{2,1,0:T(8,128)S(1)}, u32[]{:S(2)}, u32[]{:S(2)}) collective-permute-start(f32[2,16,768]{2,1,0:T(8,128)S(1)} %get-tuple-element.57), channel_id=1, source_target_pairs={{0,32},{16,48},{32,0},{48,16},{1,33},{17,49},{33,1},{49,17},{2,34}... | collective-permute-start | bytes 294920 | tf_op jit(solution)/shard_map/place/ppermute | solution.py:41
  189.5 7.1 %collective-permute-start.33 = (f32[2,16,768]{2,1,0:T(8,128)S(1)}, f32[2,16,768]{2,1,0:T(8,128)S(1)}, u32[]{:S(2)}, u32[]{:S(2)}) collective-permute-start(f32[2,16,768]{2,1,0:T(8,128)S(1)} %get-tuple-element.58), channel_id=1, source_target_pairs={{0,48},{16,0},{32,16},{48,32},{1,49},{17,1},{33,17},{49,33},{2,50}... | collective-permute-start | bytes 294920 | tf_op jit(solution)/shard_map/place/ppermute | solution.py:41

commit v4 on v3

--- a/solution.py
+++ b/solution.py
@@ -82,12 +82,11 @@
 
 
 def columns_kernel(w_ref, out_ref):
-    raw = w_ref[...].astype(f32)
-    parts = [raw[:, k, :128] for k in range(3)] + [raw[:, k, 128:] for k in range(3)]
-    out_ref[...] = jnp.concatenate(parts, axis=1).astype(bf16)
-
-
-def start_kernel(place_ref, ids_ref, steps_ref, lat_ref, mod_ref, text_ref, after_ref,
+    parts = [w_ref[k, :, :128] for k in range(3)] + [w_ref[k, :, 128:] for k in range(3)]
+    out_ref[...] = jnp.concatenate(parts, axis=1)
+
+
+def start_kernel(place_ref, ids_ref, steps_ref, lat_ref, mod_ref, text_ref,
                  out_ref, keep_ref, mate_ref):
     latent = lat_ref[0]
     average = jnp.mean(latent, axis=-1, keepdims=True)
@@ -144,7 +143,7 @@
         for kz in range(4):
             from_zl = lax.rem(zl - kz + 4, 4)
             row = (from_zl // 2) * HALF + from_y * HW + lax.rem(from_zl, 2) * 96
-            refs[4][pl.ds(pl.multiple_of(row, 32), 96), :] = refs[piece][kz]
+            refs[-1][pl.ds(pl.multiple_of(row, 32), 96), :] = refs[piece][kz]
 
 
 def attention_kernel(first, place_ref, *refs):
@@ -303,7 +302,9 @@
     place = jnp.stack([y, zl, c, x]).astype(jnp.int32)
 
     with jax.named_scope("weights"):
-        w = call(columns_kernel, struct(48, 3 * HW, dtype=bf16), 1, 0)(qkv_weight)
+        w = call(columns_kernel, struct(48, 3 * HW, dtype=bf16), 1, 0)(
+            jnp.transpose(qkv_weight, (1, 0, 2))
+        )
         w_b = [permute(w, ("c", "zh"), lambda p, k=k: {"c": p["zh"], "zh": 1 - p["zh"]}
                        if p["c"] == k else None) for k in range(2)]
         w_a = permute(w, ("c", "zh"), lambda p: None if p["c"] == p["zh"] else
@@ -318,25 +319,29 @@
         packed, keep, mate = call(
             start_kernel,
             (struct(4, 144, BLOCK, dtype=bf16), struct(4, 24, HALF), struct(4, 24, HALF)),
-            3, 3, after=1,
-        )(place, step_ids, step_table, states, mod_own, text_kv, w8)
+            3, 3,
+        )(place, step_ids, step_table, states, mod_own, text_kv)
     with jax.named_scope("gather_first"):
+        packed = call(hold_kernel, struct(4, 144, BLOCK, dtype=bf16), 1, 0, after=1)(packed, w8)
         packed = swap_core_zh(packed, same)
         sends = call(send_kernel, (struct(336, BLOCK, dtype=bf16),) * 4, 1, 1)(place, packed)
         mine = [sends[0]] + [shift(sends[k], "x", k) for k in (1, 2, 3)]
         blocks = mine + [shift(b, "c", 1) for b in mine]
 
     with jax.named_scope("weights_y"):
-        pieces = [w8] + [shift(w8, "y", k) for k in (1, -1, 2)]
+        pieces = [w8, shift(w8, "y", 1), shift(w8, "y", -1)]
+        pieces.append(shift(pieces[1], "y", 1))
 
     with jax.named_scope("states"):
         messages = call(message_kernel, (struct(2, 24, HALF),) * 4, 2, 1, after=1)(
-            place, keep, shift(mate, "c", 1), pieces[2]
+            place, keep, shift(mate, "c", 1), pieces[1]
         )
         messages = [messages[0]] + [shift(messages[k], "zl", k) for k in (1, 2, 3)]
 
     with jax.named_scope("weights_y"):
-        weight = call(weight_kernel, struct(D, 3 * HW, dtype=bf16), 4, 1)(place, *pieces)
+        weight = call(weight_kernel, struct(D, 3 * HW, dtype=bf16), 4, 1, after=3)(
+            place, *pieces, *messages[1:]
+        )
 
     text = None
     for sweep in range(SWEEPS):
@@ -368,10 +373,6 @@
             )(place, *operands)
             text = text_out[0] if text_out else text
         with jax.named_scope("to_prefix"):
-            if sweep == 0:
-                attended = call(hold_kernel, struct(32, 24, 128, dtype=bf16), 1, 0, after=3)(
-                    attended, *messages[1:]
-                )
             attended = lax.all_to_all(attended, ("zl", "x", "zh"), 0, 0)
         with jax.named_scope("prefix"):
             outs = (struct(8, 16, HALF), struct(4, 16, HALF))

time: 199 us -> 196 us (0.985)
  waiting for transfers between devices: 45.5 us -> 41.7 us
  blocking collectives: 69.5 us -> 66.1 us
  starting transfers between devices: 58.7 us -> 61.4 us
    ppermute x41, waiting for transfers between devices: 45.5 us -> 41.7 us  [permute(): return lax.ppermute(value, axes if len(axes) > 1 else axes[0], pairs)]
    all_to_all x2, blocking collectives: 39.6 us -> 36.8 us  [on_device(): attended = lax.all_to_all(attended, ('zl', 'x', 'zh'), 0, 0)]
    ppermute x41, starting transfers between devices: 58.7 us -> 61.4 us  [permute(): return lax.ppermute(value, axes if len(axes) > 1 else axes[0], pairs)]
    unnamed x12 -> x13, local copies, waits for them, and re-layouts: 2.37 us -> 4.24 us
  transfers between devices with their start and end apart: 41 -> 41, of which waited for: 18 -> 21; matrix products, arithmetic and copies ran while one was open for 1% -> 1% of each run, Pallas kernels for 3% -> 2%
where the time goes in v4:
time: 196 us; the launch traced here: 195 us
  blocking collectives  66.1 us (34%)
  starting transfers between devices  61.4 us (31%)
  waiting for transfers between devices  41.7 us (21%)
  Pallas kernels  19.6 us (10%)
  local copies, waits for them, and re-layouts  4.43 us (2%)
    ppermute x41, starting transfers between devices, permute(): return lax.ppermute(value, axes if len(axes) > 1 else axes[0], pairs)  61.4 us
    ppermute x41, waiting for transfers between devices, permute(): return lax.ppermute(value, axes if len(axes) > 1 else axes[0], pairs)  41.7 us
    all_to_all x2, blocking collectives, on_device(): attended = lax.all_to_all(attended, ('zl', 'x', 'zh'), 0, 0)  36.8 us
    all_to_all x2, blocking collectives, on_device(): totals = lax.all_to_all(total, 'y', 0, 0)  17.9 us
    all_to_all x1, blocking collectives, on_device(): modulated = lax.all_to_all(modulated, ('zl', 'zh'), 0, 0).reshape(128, HALF)  11.4 us
    pallas_call x2, Pallas kernels, on_device(): pl.pallas_call(functools.partial(attention_kernel, sweep == 0), out_shape...  10.4 us
    unnamed x13, local copies, waits for them, and re-layouts  4.24 us
  transfers between devices with their start and end apart: 41, of which 21 were waited for; matrix products, arithmetic and copies ran while one was open for 1% of the time, Pallas kernels for 2%

profile of v4, /device:TPU:8, one launch (start us, length us, event | category | flops | bytes accessed | tf_op | source)
XLA Modules:
  0.0 195.2 jit_solution(17675186184960755347)
XLA Ops:
  0.7 1.0 copy-done.3
  2.4 9.7 %collective-permute-start.1 = (bf16[48,576]{1,0:T(8,128)(2,1)S(1)}, bf16[48,576]{1,0:T(8,128)(2,1)S(1)}, u32[]{:S(2)}, u32[]{:S(2)}) collective-permute-start(bf16[48,576]{1,0:T(8,128)(2,1)S(1)} %weights.1), channel_id=1, source_target_pairs={{0,1},{1,8},{2,3},{3,10},{4,5},{5,12},{6,7},{7,14},{16,17},{17,24}... | collective-permute-start | bytes 165896 | tf_op jit(solution)/shard_map/weights/ppermute | solution.py:41
  12.1 1.3 collective-permute-start
  14.2 1.1 collective-permute-done
  15.3 1.6 collective-permute-start.4
  16.9 1.0 collective-permute-start.3
  17.9 2.2 %collective-permute-start.5 = (bf16[96,576]{1,0:T(8,128)(2,1)S(1)}, bf16[96,576]{1,0:T(8,128)(2,1)S(1)}, u32[]{:S(2)}, u32[]{:S(2)}) collective-permute-start(bf16[96,576]{1,0:T(8,128)(2,1)S(1)} %get-tuple-element.65), channel_id=1, source_target_pairs={{0,49},{1,48},{16,0},{17,1},{32,16},{33,17},{48,32},{49,33},{2,51}... | collective-permute-start | bytes 331784 | tf_op jit(solution)/shard_map/weights/ppermute | solution.py:41
  20.2 2.6 %collective-permute-done.4 = bf16[96,576]{1,0:T(8,128)(2,1)S(1)} collective-permute-done((bf16[96,576]{1,0:T(8,128)(2,1)S(1)}, bf16[96,576]{1,0:T(8,128)(2,1)S(1)}, u32[]{:S(2)}, u32[]{:S(2)}) %collective-permute-start.4) | collective-permute-done | bytes 110624 | tf_op jit(solution)/shard_map/weights/ppermute | solution.py:41
  22.8 2.1 %collective-permute-done.3 = bf16[96,576]{1,0:T(8,128)(2,1)S(1)} collective-permute-done((bf16[96,576]{1,0:T(8,128)(2,1)S(1)}, bf16[96,576]{1,0:T(8,128)(2,1)S(1)}, u32[]{:S(2)}, u32[]{:S(2)}) %collective-permute-start.3) | collective-permute-done | bytes 110624 | tf_op jit(solution)/shard_map/weights/ppermute | solution.py:41
  25.0 1.7 collective-permute-start.14
  26.7 1.0 copy-done.1
  29.3 1.2 start.1
  31.2 10.3 %collective-permute-start.17 = (f32[4,24,768]{2,1,0:T(8,128)S(1)}, f32[4,24,768]{2,1,0:T(8,128)S(1)}, u32[]{:S(2)}, u32[]{:S(2)}) collective-permute-start(f32[4,24,768]{2,1,0:T(8,128)S(1)} %get-tuple-element.37), channel_id=1, source_target_pairs={{0,8},{8,0},{1,9},{9,1},{2,10},{10,2},{3,11},{11,3},{4,12},{12,4},... | collective-permute-start | bytes 884744 | tf_op jit(solution)/shard_map/states/ppermute | solution.py:41
  43.4 2.8 %collective-permute-start.19 = (f32[2,24,768]{2,1,0:T(8,128)S(1)}, f32[2,24,768]{2,1,0:T(8,128)S(1)}, u32[]{:S(2)}, u32[]{:S(2)}) collective-permute-start(f32[2,24,768]{2,1,0:T(8,128)S(1)} %get-tuple-element.39), channel_id=1, source_target_pairs={{0,32},{16,48},{32,0},{48,16},{1,33},{17,49},{33,1},{49,17},{2,34}... | collective-permute-start | bytes 442376 | tf_op jit(solution)/shard_map/states/ppermute | solution.py:41
  46.9 1.6 collective-permute-start.7
  48.4 2.7 %collective-permute-start.8 = (bf16[336,384]{1,0:T(8,128)(2,1)S(1)}, bf16[336,384]{1,0:T(8,128)(2,1)S(1)}, u32[]{:S(2)}, u32[]{:S(2)}) collective-permute-start(bf16[336,384]{1,0:T(8,128)(2,1)S(1)} %get-tuple-element.34), channel_id=1, source_target_pairs={{0,4},{2,6},{4,0},{6,2},{1,5},{3,7},{5,1},{7,3},{8,12},{10,14},{12... | collective-permute-start | bytes 774152 | tf_op jit(solution)/shard_map/gather_first/ppermute | solution.py:41
  51.2 3.6 %collective-permute-done.15.refs_2_ = bf16[4,96,576]{2,1,0:T(8,128)(2,1)S(1)} collective-permute-done((bf16[4,96,576]{2,1,0:T(8,128)(2,1)S(1)}, bf16[4,96,576]{2,1,0:T(8,128)(2,1)S(1)}, u32[]{:S(2)}, u32[]{:S(2)}) %collective-permute-start.15) | collective-permute-done | bytes 442400 | tf_op jit(solution)/shard_map/weights_y/ppermute | solution.py:41
  54.7 2.8 %collective-permute-start.9 = (bf16[336,384]{1,0:T(8,128)(2,1)S(1)}, bf16[336,384]{1,0:T(8,128)(2,1)S(1)}, u32[]{:S(2)}, u32[]{:S(2)}) collective-permute-start(bf16[336,384]{1,0:T(8,128)(2,1)S(1)} %get-tuple-element.35), channel_id=1, source_target_pairs={{0,6},{2,0},{4,2},{6,4},{1,7},{3,1},{5,3},{7,5},{8,14},{10,8},{12,... | collective-permute-start | bytes 774152 | tf_op jit(solution)/shard_map/gather_first/ppermute | solution.py:41
  57.5 1.3 collective-permute-start.16
  59.7 4.4 %collective-permute-start.20 = (f32[2,24,768]{2,1,0:T(8,128)S(1)}, f32[2,24,768]{2,1,0:T(8,128)S(1)}, u32[]{:S(2)}, u32[]{:S(2)}) collective-permute-start(f32[2,24,768]{2,1,0:T(8,128)S(1)} %get-tuple-element.40), channel_id=1, source_target_pairs={{0,48},{16,0},{32,16},{48,32},{1,49},{17,1},{33,17},{49,33},{2,50}... | collective-permute-start | bytes 442376 | tf_op jit(solution)/shard_map/states/ppermute | solution.py:41
  64.1 3.3 %collective-permute-done.20.refs_6_.refs_3_ = f32[2,24,768]{2,1,0:T(8,128)S(1)} collective-permute-done((f32[2,24,768]{2,1,0:T(8,128)S(1)}, f32[2,24,768]{2,1,0:T(8,128)S(1)}, u32[]{:S(2)}, u32[]{:S(2)}) %collective-permute-start.20) | collective-permute-done | bytes 147488 | tf_op jit(solution)/shard_map/states/ppermute | solution.py:41
  68.4 1.3 collective-permute-done.16.refs_3_
  70.5 4.9 %attention.2 = (bf16[32,24,128]{2,1,0:T(8,128)(2,1)S(1)}, bf16[2,320,192]{2,1,0:T(8,128)(2,1)S(1)}) custom-call(s32[4]{0:T(128)S(1)} %pad_add_fusion.place_ref, bf16[336,384]{1,0:T(8,128)(2,1)S(1)} %get-tuple-element.32.refs_0_, bf16[336,384]{1,0:T(8,128)(2,1)S(1)} %collective-permute-done.7.refs_1_, bf16[336,384]{1,0:T(8,128)(2,1)S(1)} %collective-permute-done.8.refs_2_, ...), custom_call_target="tpu_custom_call" | custom-call | flops 1233125376 | bytes 25165824 | tf_op jit(solution)/shard_map/attention/pallas_call | solution.py:362
  75.4 19.3 %all_to_all.25.att_ref = bf16[32,24,128]{2,1,0:T(8,128)(2,1)S(1)} all-to-all(bf16[32,24,128]{2,1,0:T(8,128)(2,1)S(1)} %get-tuple-element.41), channel_id=1, replica_groups=mesh['y'=4,'zl'=4,'c'=2,'x'=4,'zh'=2] {'zl','x','zh'}, dimensions={0} | all-to-all | bytes 393216 | tf_op jit(solution)/shard_map/to_prefix/all_to_all | solution.py:376
  95.5 9.2 %all_to_all.26.totals_ref = f32[4,16,768]{2,1,0:T(8,128)S(1)} all-to-all(f32[4,16,768]{2,1,0:T(8,128)S(1)} %get-tuple-element.45), channel_id=1, replica_groups=mesh['y'=4,'zl'=4,'c'=2,'x'=4,'zh'=2] {'y'}, dimensions={0} | all-to-all | bytes 393216 | tf_op jit(solution)/shard_map/prefix/all_to_all | solution.py:388
  105.6 1.2 collective-permute-done.21.other_ref
  107.1 11.4 %all_to_all.27 = bf16[8,16,768]{2,1,0:T(8,128)(2,1)S(1)} all-to-all(bf16[8,16,768]{2,1,0:T(8,128)(2,1)S(1)} %norm.1), channel_id=1, replica_groups=mesh['y'=4,'zl'=4,'c'=2,'x'=4,'zh'=2] {'zl','zh'}, dimensions={0} | all-to-all | bytes 393216 | tf_op jit(solution)/shard_map/gather/all_to_all | solution.py:400
  118.5 1.7 collective-permute-start.24
  121.2 6.1 %collective-permute-done.24.refs_3_ = bf16[128,768]{1,0:T(8,128)(2,1)S(1)} collective-permute-done((bf16[128,768]{1,0:T(8,128)(2,1)S(1)}, bf16[128,768]{1,0:T(8,128)(2,1)S(1)}, u32[]{:S(2)}, u32[]{:S(2)}) %collective-permute-start.24) | collective-permute-done | bytes 196640 | tf_op jit(solution)/shard_map/gather/ppermute | solution.py:41
  127.3 1.7 collective-permute-done.23.refs_2_
  128.9 2.0 %collective-permute-done.22.refs_1_ = bf16[128,768]{1,0:T(8,128)(2,1)S(1)} collective-permute-done((bf16[128,768]{1,0:T(8,128)(2,1)S(1)}, bf16[128,768]{1,0:T(8,128)(2,1)S(1)}, u32[]{:S(2)}, u32[]{:S(2)}) %collective-permute-start.22) | collective-permute-done | bytes 196640 | tf_op jit(solution)/shard_map/gather/ppermute | solution.py:41
  131.0 1.4 collective-permute-done.26.refs_5_
  132.4 5.4 %attention.3 = bf16[32,24,128]{2,1,0:T(8,128)(2,1)S(1)} custom-call(s32[4]{0:T(128)S(1)} %pad_add_fusion.place_ref, bf16[128,768]{1,0:T(8,128)(2,1)S(1)} %bitcast.23, bf16[128,768]{1,0:T(8,128)(2,1)S(1)} %collective-permute-done.22.refs_1_, bf16[128,768]{1,0:T(8,128)(2,1)S(1)} %collective-permute-done.23.refs_2_, ...), custom_call_target="tpu_custom_call" | custom-call | flops 1233125376 | bytes 25165824 | tf_op jit(solution)/shard_map/attention/pallas_call | solution.py:362
  137.8 17.4 %all_to_all.28.att_ref = bf16[32,24,128]{2,1,0:T(8,128)(2,1)S(1)} all-to-all(bf16[32,24,128]{2,1,0:T(8,128)(2,1)S(1)} %attention.3), channel_id=1, replica_groups=mesh['y'=4,'zl'=4,'c'=2,'x'=4,'zh'=2] {'zl','x','zh'}, dimensions={0} | all-to-all | bytes 393216 | tf_op jit(solution)/shard_map/to_prefix/all_to_all | solution.py:376
  156.0 8.7 %all_to_all.29.totals_ref = f32[4,16,768]{2,1,0:T(8,128)S(1)} all-to-all(f32[4,16,768]{2,1,0:T(8,128)S(1)} %get-tuple-element.50), channel_id=1, replica_groups=mesh['y'=4,'zl'=4,'c'=2,'x'=4,'zh'=2] {'y'}, dimensions={0} | all-to-all | bytes 393216 | tf_op jit(solution)/shard_map/prefix/all_to_all | solution.py:388
  164.7 1.6 place.3
  168.4 1.5 collective-permute-start.36
  169.9 1.7 collective-permute-start.35
  172.3 2.3 %collective-permute-done.35 = f32[16,128]{1,0:T(8,128)S(1)} collective-permute-done((f32[16,128]{1,0:T(8,128)S(1)}, f32[16,128]{1,0:T(8,128)S(1)}, u32[]{:S(2)}, u32[]{:S(2)}) %collective-permute-start.35) | collective-permute-done | bytes 8224 | tf_op jit(solution)/shard_map/changes/ppermute | solution.py:41
  174.6 2.5 %collective-permute-done.34 = f32[16,128]{1,0:T(8,128)S(1)} collective-permute-done((f32[16,128]{1,0:T(8,128)S(1)}, f32[16,128]{1,0:T(8,128)S(1)}, u32[]{:S(2)}, u32[]{:S(2)}) %collective-permute-start.34) | collective-permute-done | bytes 8224 | tf_op jit(solution)/shard_map/changes/ppermute | solution.py:41
  177.1 1.2 collective-permute-start.39
  178.3 1.4 collective-permute-start.38
  180.8 2.7 %collective-permute-done.38 = f32[16,128]{1,0:T(8,128)S(1)} collective-permute-done((f32[16,128]{1,0:T(8,128)S(1)}, f32[16,128]{1,0:T(8,128)S(1)}, u32[]{:S(2)}, u32[]{:S(2)}) %collective-permute-start.38) | collective-permute-done | bytes 8224 | tf_op jit(solution)/shard_map/changes/ppermute | solution.py:41
  183.5 1.1 collective-permute-done.37
  184.6 1.5 collective-permute-start.40
  186.7 3.2 %collective-permute-start.33 = (f32[2,16,768]{2,1,0:T(8,128)S(1)}, f32[2,16,768]{2,1,0:T(8,128)S(1)}, u32[]{:S(2)}, u32[]{:S(2)}) collective-permute-start(f32[2,16,768]{2,1,0:T(8,128)S(1)} %get-tuple-element.58), channel_id=1, source_target_pairs={{0,48},{16,0},{32,16},{48,32},{1,49},{17,1},{33,17},{49,33},{2,50}... | collective-permute-start | bytes 294920 | tf_op jit(solution)/shard_map/place/ppermute | solution.py:41
  190.0 2.4 %collective-permute-done.40 = f32[16,128]{1,0:T(8,128)S(1)} collective-permute-done((f32[16,128]{1,0:T(8,128)S(1)}, f32[16,128]{1,0:T(8,128)S(1)}, u32[]{:S(2)}, u32[]{:S(2)}) %collective-permute-start.40) | collective-permute-done | bytes 8224 | tf_op jit(solution)/shard_map/changes/ppermute | solution.py:41
  193.8 1.4 place.5
  (80 shorter events, 18.0 us)
Async XLA Ops:
  0.6 13.5 %copy-start = (f32[128,3,1536]{2,0,1:T(8,128)S(1)}, f32[128,3,1536]{2,0,1:T(8,128)}, u32[]{:S(2)}) copy-start(f32[128,3,1536]{2,0,1:T(8,128)} %param.9) | copy-start | bytes 7077892
  0.6 1.0 copy-start.3
  1.8 12.4 %collective-permute-start.2 = (bf16[48,576]{1,0:T(8,128)(2,1)S(1)}, bf16[48,576]{1,0:T(8,128)(2,1)S(1)}, u32[]{:S(2)}, u32[]{:S(2)}) collective-permute-start(bf16[48,576]{1,0:T(8,128)(2,1)S(1)} %weights.1), channel_id=1, source_target_pairs={{8,1},{9,8},{10,3},{11,10},{12,5},{13,12},{14,7},{15,14},{24,17},{... | collective-permute-start | bytes 165896 | tf_op jit(solution)/shard_map/weights/ppermute | solution.py:41
  2.4 11.8 %collective-permute-start.1 = (bf16[48,576]{1,0:T(8,128)(2,1)S(1)}, bf16[48,576]{1,0:T(8,128)(2,1)S(1)}, u32[]{:S(2)}, u32[]{:S(2)}) collective-permute-start(bf16[48,576]{1,0:T(8,128)(2,1)S(1)} %weights.1), channel_id=1, source_target_pairs={{0,1},{1,8},{2,3},{3,10},{4,5},{5,12},{6,7},{7,14},{16,17},{17,24}... | collective-permute-start | bytes 165896 | tf_op jit(solution)/shard_map/weights/ppermute | solution.py:41
  12.1 3.1 %collective-permute-start = (bf16[48,576]{1,0:T(8,128)(2,1)S(1)}, bf16[48,576]{1,0:T(8,128)(2,1)S(1)}, u32[]{:S(2)}, u32[]{:S(2)}) collective-permute-start(bf16[48,576]{1,0:T(8,128)(2,1)S(1)} %weights.1), channel_id=1, source_target_pairs={{1,9},{8,0},{3,11},{10,2},{5,13},{12,4},{7,15},{14,6},{17,25},{24,... | collective-permute-start | bytes 165896 | tf_op jit(solution)/shard_map/weights/ppermute | solution.py:41
  15.3 7.5 %collective-permute-start.4 = (bf16[96,576]{1,0:T(8,128)(2,1)S(1)}, bf16[96,576]{1,0:T(8,128)(2,1)S(1)}, u32[]{:S(2)}, u32[]{:S(2)}) collective-permute-start(bf16[96,576]{1,0:T(8,128)(2,1)S(1)} %get-tuple-element.65), channel_id=1, source_target_pairs={{0,32},{1,33},{16,48},{17,49},{32,1},{33,0},{48,17},{49,16},{2,34}... | collective-permute-start | bytes 331784 | tf_op jit(solution)/shard_map/weights/ppermute | solution.py:41
  16.9 8.0 %collective-permute-start.3 = (bf16[96,576]{1,0:T(8,128)(2,1)S(1)}, bf16[96,576]{1,0:T(8,128)(2,1)S(1)}, u32[]{:S(2)}, u32[]{:S(2)}) collective-permute-start(bf16[96,576]{1,0:T(8,128)(2,1)S(1)} %get-tuple-element.65), channel_id=1, source_target_pairs={{0,16},{1,17},{16,32},{17,33},{32,48},{33,49},{48,1},{49,0},{2,18}... | collective-permute-start | bytes 331784 | tf_op jit(solution)/shard_map/weights/ppermute | solution.py:41
  17.9 7.0 %collective-permute-start.5 = (bf16[96,576]{1,0:T(8,128)(2,1)S(1)}, bf16[96,576]{1,0:T(8,128)(2,1)S(1)}, u32[]{:S(2)}, u32[]{:S(2)}) collective-permute-start(bf16[96,576]{1,0:T(8,128)(2,1)S(1)} %get-tuple-element.65), channel_id=1, source_target_pairs={{0,49},{1,48},{16,0},{17,1},{32,16},{33,17},{48,32},{49,33},{2,51}... | collective-permute-start | bytes 331784 | tf_op jit(solution)/shard_map/weights/ppermute | solution.py:41
  25.0 17.7 %collective-permute-start.14 = (bf16[4,96,576]{2,1,0:T(8,128)(2,1)S(1)}, bf16[4,96,576]{2,1,0:T(8,128)(2,1)S(1)}, u32[]{:S(2)}, u32[]{:S(2)}) collective-permute-start(bf16[4,96,576]{2,1,0:T(8,128)(2,1)S(1)} %pad_maximum_fusion.refs_0_), channel_id=1, source_target_pairs={{0,64},{64,128},{128,192},{192,0},{1,65},{65,129},{129,193},{193,1... | collective-permute-start | bytes 1327112 | tf_op jit(solution)/shard_map/weights_y/ppermute | solution.py:41
  26.7 1.0 copy-start.1
  27.7 0.9 copy-start.2
  28.6 0.7 copy-start.4
  30.5 15.7 %collective-permute-start.6 = (bf16[4,144,384]{2,1,0:T(8,128)(2,1)S(1)}, bf16[4,144,384]{2,1,0:T(8,128)(2,1)S(1)}, u32[]{:S(2)}, u32[]{:S(2)}) collective-permute-start(bf16[4,144,384]{2,1,0:T(8,128)(2,1)S(1)} %gather_first.2), channel_id=1, source_target_pairs={{1,8},{8,1},{3,10},{10,3},{5,12},{12,5},{7,14},{14,7},{17,24},{24,... | collective-permute-start | bytes 1327112 | tf_op jit(solution)/shard_map/gather_first/ppermute | solution.py:41
  31.2 11.5 %collective-permute-start.17 = (f32[4,24,768]{2,1,0:T(8,128)S(1)}, f32[4,24,768]{2,1,0:T(8,128)S(1)}, u32[]{:S(2)}, u32[]{:S(2)}) collective-permute-start(f32[4,24,768]{2,1,0:T(8,128)S(1)} %get-tuple-element.37), channel_id=1, source_target_pairs={{0,8},{8,0},{1,9},{9,1},{2,10},{10,2},{3,11},{11,3},{4,12},{12,4},... | collective-permute-start | bytes 884744 | tf_op jit(solution)/shard_map/states/ppermute | solution.py:41
  41.5 13.2 %collective-permute-start.15 = (bf16[4,96,576]{2,1,0:T(8,128)(2,1)S(1)}, bf16[4,96,576]{2,1,0:T(8,128)(2,1)S(1)}, u32[]{:S(2)}, u32[]{:S(2)}) collective-permute-start(bf16[4,96,576]{2,1,0:T(8,128)(2,1)S(1)} %pad_maximum_fusion.refs_0_), channel_id=1, source_target_pairs={{0,192},{64,0},{128,64},{192,128},{1,193},{65,1},{129,65},{193,129... | collective-permute-start | bytes 1327112 | tf_op jit(solution)/shard_map/weights_y/ppermute | solution.py:41
  43.3 14.2 %collective-permute-start.18 = (f32[2,24,768]{2,1,0:T(8,128)S(1)}, f32[2,24,768]{2,1,0:T(8,128)S(1)}, u32[]{:S(2)}, u32[]{:S(2)}) collective-permute-start(f32[2,24,768]{2,1,0:T(8,128)S(1)} %get-tuple-element.38), channel_id=1, source_target_pairs={{0,16},{16,32},{32,48},{48,0},{1,17},{17,33},{33,49},{49,1},{2,18}... | collective-permute-start | bytes 442376 | tf_op jit(solution)/shard_map/states/ppermute | solution.py:41
  43.4 16.3 %collective-permute-start.19 = (f32[2,24,768]{2,1,0:T(8,128)S(1)}, f32[2,24,768]{2,1,0:T(8,128)S(1)}, u32[]{:S(2)}, u32[]{:S(2)}) collective-permute-start(f32[2,24,768]{2,1,0:T(8,128)S(1)} %get-tuple-element.39), channel_id=1, source_target_pairs={{0,32},{16,48},{32,0},{48,16},{1,33},{17,49},{33,1},{49,17},{2,34}... | collective-permute-start | bytes 442376 | tf_op jit(solution)/shard_map/states/ppermute | solution.py:41
  46.9 20.5 %collective-permute-start.7 = (bf16[336,384]{1,0:T(8,128)(2,1)S(1)}, bf16[336,384]{1,0:T(8,128)(2,1)S(1)}, u32[]{:S(2)}, u32[]{:S(2)}) collective-permute-start(bf16[336,384]{1,0:T(8,128)(2,1)S(1)} %get-tuple-element.33), channel_id=1, source_target_pairs={{0,2},{2,4},{4,6},{6,0},{1,3},{3,5},{5,7},{7,1},{8,10},{10,12},{12... | collective-permute-start | bytes 774152 | tf_op jit(solution)/shard_map/gather_first/ppermute | solution.py:41
  48.4 19.4 %collective-permute-start.8 = (bf16[336,384]{1,0:T(8,128)(2,1)S(1)}, bf16[336,384]{1,0:T(8,128)(2,1)S(1)}, u32[]{:S(2)}, u32[]{:S(2)}) collective-permute-start(bf16[336,384]{1,0:T(8,128)(2,1)S(1)} %get-tuple-element.34), channel_id=1, source_target_pairs={{0,4},{2,6},{4,0},{6,2},{1,5},{3,7},{5,1},{7,3},{8,12},{10,14},{12... | collective-permute-start | bytes 774152 | tf_op jit(solution)/shard_map/gather_first/ppermute | solution.py:41
  54.7 13.4 %collective-permute-start.9 = (bf16[336,384]{1,0:T(8,128)(2,1)S(1)}, bf16[336,384]{1,0:T(8,128)(2,1)S(1)}, u32[]{:S(2)}, u32[]{:S(2)}) collective-permute-start(bf16[336,384]{1,0:T(8,128)(2,1)S(1)} %get-tuple-element.35), channel_id=1, source_target_pairs={{0,6},{2,0},{4,2},{6,4},{1,7},{3,1},{5,3},{7,5},{8,14},{10,8},{12,... | collective-permute-start | bytes 774152 | tf_op jit(solution)/shard_map/gather_first/ppermute | solution.py:41
  57.5 12.2 %collective-permute-start.16 = (bf16[4,96,576]{2,1,0:T(8,128)(2,1)S(1)}, bf16[4,96,576]{2,1,0:T(8,128)(2,1)S(1)}, u32[]{:S(2)}, u32[]{:S(2)}) collective-permute-start(bf16[4,96,576]{2,1,0:T(8,128)(2,1)S(1)} %collective-permute-done.14.extra_ref.refs_1_), channel_id=1, source_target_pairs={{0,64},{64,128},{128,192},{192,0},{1,65},{65,129},{129,193},{193,1... | collective-permute-start | bytes 1327112 | tf_op jit(solution)/shard_map/weights_y/ppermute | solution.py:41
  59.7 7.6 %collective-permute-start.20 = (f32[2,24,768]{2,1,0:T(8,128)S(1)}, f32[2,24,768]{2,1,0:T(8,128)S(1)}, u32[]{:S(2)}, u32[]{:S(2)}) collective-permute-start(f32[2,24,768]{2,1,0:T(8,128)S(1)} %get-tuple-element.40), channel_id=1, source_target_pairs={{0,48},{16,0},{32,16},{48,32},{1,49},{17,1},{33,17},{49,33},{2,50}... | collective-permute-start | bytes 442376 | tf_op jit(solution)/shard_map/states/ppermute | solution.py:41
  67.4 3.1 %collective-permute-start.10 = (bf16[336,384]{1,0:T(8,128)(2,1)S(1)}, bf16[336,384]{1,0:T(8,128)(2,1)S(1)}, u32[]{:S(2)}, u32[]{:S(2)}) collective-permute-start(bf16[336,384]{1,0:T(8,128)(2,1)S(1)} %get-tuple-element.32.refs_0_), channel_id=1, source_target_pairs={{0,8},{8,0},{1,9},{9,1},{2,10},{10,2},{3,11},{11,3},{4,12},{12,4},... | collective-permute-start | bytes 774152 | tf_op jit(solution)/shard_map/gather_first/ppermute | solution.py:41
  67.4 3.1 %collective-permute-start.11 = (bf16[336,384]{1,0:T(8,128)(2,1)S(1)}, bf16[336,384]{1,0:T(8,128)(2,1)S(1)}, u32[]{:S(2)}, u32[]{:S(2)}) collective-permute-start(bf16[336,384]{1,0:T(8,128)(2,1)S(1)} %collective-permute-done.7.refs_1_), channel_id=1, source_target_pairs={{0,8},{8,0},{1,9},{9,1},{2,10},{10,2},{3,11},{11,3},{4,12},{12,4},... | collective-permute-start | bytes 774152 | tf_op jit(solution)/shard_map/gather_first/ppermute | solution.py:41
  67.9 2.6 %collective-permute-start.12 = (bf16[336,384]{1,0:T(8,128)(2,1)S(1)}, bf16[336,384]{1,0:T(8,128)(2,1)S(1)}, u32[]{:S(2)}, u32[]{:S(2)}) collective-permute-start(bf16[336,384]{1,0:T(8,128)(2,1)S(1)} %collective-permute-done.8.refs_2_), channel_id=1, source_target_pairs={{0,8},{8,0},{1,9},{9,1},{2,10},{10,2},{3,11},{11,3},{4,12},{12,4},... | collective-permute-start | bytes 774152 | tf_op jit(solution)/shard_map/gather_first/ppermute | solution.py:41
  68.1 2.3 %collective-permute-start.13 = (bf16[336,384]{1,0:T(8,128)(2,1)S(1)}, bf16[336,384]{1,0:T(8,128)(2,1)S(1)}, u32[]{:S(2)}, u32[]{:S(2)}) collective-permute-start(bf16[336,384]{1,0:T(8,128)(2,1)S(1)} %collective-permute-done.9.refs_3_), channel_id=1, source_target_pairs={{0,8},{8,0},{1,9},{9,1},{2,10},{10,2},{3,11},{11,3},{4,12},{12,4},... | collective-permute-start | bytes 774152 | tf_op jit(solution)/shard_map/gather_first/ppermute | solution.py:41
  105.5 1.3 collective-permute-start.21
  118.5 8.8 %collective-permute-start.24 = (bf16[128,768]{1,0:T(8,128)(2,1)S(1)}, bf16[128,768]{1,0:T(8,128)(2,1)S(1)}, u32[]{:S(2)}, u32[]{:S(2)}) collective-permute-start(bf16[128,768]{1,0:T(8,128)(2,1)S(1)} %bitcast.19), channel_id=1, source_target_pairs={{0,6},{2,0},{4,2},{6,4},{1,7},{3,1},{5,3},{7,5},{8,14},{10,8},{12,... | collective-permute-start | bytes 589832 | tf_op jit(solution)/shard_map/gather/ppermute | solution.py:41
  120.2 8.8 %collective-permute-start.23 = (bf16[128,768]{1,0:T(8,128)(2,1)S(1)}, bf16[128,768]{1,0:T(8,128)(2,1)S(1)}, u32[]{:S(2)}, u32[]{:S(2)}) collective-permute-start(bf16[128,768]{1,0:T(8,128)(2,1)S(1)} %bitcast.20), channel_id=1, source_target_pairs={{0,4},{2,6},{4,0},{6,2},{1,5},{3,7},{5,1},{7,3},{8,12},{10,14},{12... | collective-permute-start | bytes 589832 | tf_op jit(solution)/shard_map/gather/ppermute | solution.py:41
  121.1 9.8 %collective-permute-start.22 = (bf16[128,768]{1,0:T(8,128)(2,1)S(1)}, bf16[128,768]{1,0:T(8,128)(2,1)S(1)}, u32[]{:S(2)}, u32[]{:S(2)}) collective-permute-start(bf16[128,768]{1,0:T(8,128)(2,1)S(1)} %bitcast.21), channel_id=1, source_target_pairs={{0,2},{2,4},{4,6},{6,0},{1,3},{3,5},{5,7},{7,1},{8,10},{10,12},{12... | collective-permute-start | bytes 589832 | tf_op jit(solution)/shard_map/gather/ppermute | solution.py:41
  121.2 9.8 %collective-permute-start.25 = (bf16[128,768]{1,0:T(8,128)(2,1)S(1)}, bf16[128,768]{1,0:T(8,128)(2,1)S(1)}, u32[]{:S(2)}, u32[]{:S(2)}) collective-permute-start(bf16[128,768]{1,0:T(8,128)(2,1)S(1)} %bitcast.22), channel_id=1, source_target_pairs={{0,8},{8,0},{1,9},{9,1},{2,10},{10,2},{3,11},{11,3},{4,12},{12,4},... | collective-permute-start | bytes 589832 | tf_op jit(solution)/shard_map/gather/ppermute | solution.py:41
  127.3 3.7 %collective-permute-start.28 = (bf16[128,768]{1,0:T(8,128)(2,1)S(1)}, bf16[128,768]{1,0:T(8,128)(2,1)S(1)}, u32[]{:S(2)}, u32[]{:S(2)}) collective-permute-start(bf16[128,768]{1,0:T(8,128)(2,1)S(1)} %collective-permute-done.24.refs_3_), channel_id=1, source_target_pairs={{0,8},{8,0},{1,9},{9,1},{2,10},{10,2},{3,11},{11,3},{4,12},{12,4},... | collective-permute-start | bytes 589832 | tf_op jit(solution)/shard_map/gather/ppermute | solution.py:41
  128.9 2.0 %collective-permute-start.27 = (bf16[128,768]{1,0:T(8,128)(2,1)S(1)}, bf16[128,768]{1,0:T(8,128)(2,1)S(1)}, u32[]{:S(2)}, u32[]{:S(2)}) collective-permute-start(bf16[128,768]{1,0:T(8,128)(2,1)S(1)} %collective-permute-done.23.refs_2_), channel_id=1, source_target_pairs={{0,8},{8,0},{1,9},{9,1},{2,10},{10,2},{3,11},{11,3},{4,12},{12,4},... | collective-permute-start | bytes 589832 | tf_op jit(solution)/shard_map/gather/ppermute | solution.py:41
  130.9 1.4 collective-permute-start.26
  166.2 1.5 collective-permute-start.29
  166.4 1.4 collective-permute-start.30
  168.4 3.9 %collective-permute-start.36 = (f32[16,128]{1,0:T(8,128)S(1)}, f32[16,128]{1,0:T(8,128)S(1)}, u32[]{:S(2)}, u32[]{:S(2)}) collective-permute-start(f32[16,128]{1,0:T(8,128)S(1)} %get-tuple-element.59), channel_id=1, source_target_pairs={{0,48},{16,0},{32,16},{48,32},{1,49},{17,1},{33,17},{49,33},{2,50}... | collective-permute-start | bytes 24584 | tf_op jit(solution)/shard_map/changes/ppermute | solution.py:41
  169.9 4.6 %collective-permute-start.35 = (f32[16,128]{1,0:T(8,128)S(1)}, f32[16,128]{1,0:T(8,128)S(1)}, u32[]{:S(2)}, u32[]{:S(2)}) collective-permute-start(f32[16,128]{1,0:T(8,128)S(1)} %get-tuple-element.59), channel_id=1, source_target_pairs={{0,32},{16,48},{32,0},{48,16},{1,33},{17,49},{33,1},{49,17},{2,34}... | collective-permute-start | bytes 24584 | tf_op jit(solution)/shard_map/changes/ppermute | solution.py:41
  171.6 5.4 %collective-permute-start.34 = (f32[16,128]{1,0:T(8,128)S(1)}, f32[16,128]{1,0:T(8,128)S(1)}, u32[]{:S(2)}, u32[]{:S(2)}) collective-permute-start(f32[16,128]{1,0:T(8,128)S(1)} %get-tuple-element.59), channel_id=1, source_target_pairs={{0,16},{16,32},{32,48},{48,0},{1,17},{17,33},{33,49},{49,1},{2,18}... | collective-permute-start | bytes 24584 | tf_op jit(solution)/shard_map/changes/ppermute | solution.py:41
  177.1 3.7 %collective-permute-start.39 = (f32[16,128]{1,0:T(8,128)S(1)}, f32[16,128]{1,0:T(8,128)S(1)}, u32[]{:S(2)}, u32[]{:S(2)}) collective-permute-start(f32[16,128]{1,0:T(8,128)S(1)} %maximum_maximum_fusion.1), channel_id=1, source_target_pairs={{0,6},{2,0},{4,2},{6,4},{1,7},{3,1},{5,3},{7,5},{8,14},{10,8},{12,... | collective-permute-start | bytes 24584 | tf_op jit(solution)/shard_map/changes/ppermute | solution.py:41
  178.3 5.2 %collective-permute-start.38 = (f32[16,128]{1,0:T(8,128)S(1)}, f32[16,128]{1,0:T(8,128)S(1)}, u32[]{:S(2)}, u32[]{:S(2)}) collective-permute-start(f32[16,128]{1,0:T(8,128)S(1)} %maximum_maximum_fusion.1), channel_id=1, source_target_pairs={{0,4},{2,6},{4,0},{6,2},{1,5},{3,7},{5,1},{7,3},{8,12},{10,14},{12... | collective-permute-start | bytes 24584 | tf_op jit(solution)/shard_map/changes/ppermute | solution.py:41
  179.8 4.9 %collective-permute-start.37 = (f32[16,128]{1,0:T(8,128)S(1)}, f32[16,128]{1,0:T(8,128)S(1)}, u32[]{:S(2)}, u32[]{:S(2)}) collective-permute-start(f32[16,128]{1,0:T(8,128)S(1)} %maximum_maximum_fusion.1), channel_id=1, source_target_pairs={{0,2},{2,4},{4,6},{6,0},{1,3},{3,5},{5,7},{7,1},{8,10},{10,12},{12... | collective-permute-start | bytes 24584 | tf_op jit(solution)/shard_map/changes/ppermute | solution.py:41
  184.6 7.8 %collective-permute-start.40 = (f32[16,128]{1,0:T(8,128)S(1)}, f32[16,128]{1,0:T(8,128)S(1)}, u32[]{:S(2)}, u32[]{:S(2)}) collective-permute-start(f32[16,128]{1,0:T(8,128)S(1)} %maximum_maximum_fusion), channel_id=1, source_target_pairs={{0,1},{1,0},{2,3},{3,2},{4,5},{5,4},{6,7},{7,6},{8,9},{9,8},{10,11... | collective-permute-start | bytes 24584 | tf_op jit(solution)/shard_map/changes/ppermute | solution.py:41
  186.1 7.1 %collective-permute-start.31 = (f32[2,16,768]{2,1,0:T(8,128)S(1)}, f32[2,16,768]{2,1,0:T(8,128)S(1)}, u32[]{:S(2)}, u32[]{:S(2)}) collective-permute-start(f32[2,16,768]{2,1,0:T(8,128)S(1)} %get-tuple-element.56), channel_id=1, source_target_pairs={{0,16},{16,32},{32,48},{48,0},{1,17},{17,33},{33,49},{49,1},{2,18}... | collective-permute-start | bytes 294920 | tf_op jit(solution)/shard_map/place/ppermute | solution.py:41
  186.1 7.7 %collective-permute-start.32 = (f32[2,16,768]{2,1,0:T(8,128)S(1)}, f32[2,16,768]{2,1,0:T(8,128)S(1)}, u32[]{:S(2)}, u32[]{:S(2)}) collective-permute-start(f32[2,16,768]{2,1,0:T(8,128)S(1)} %get-tuple-element.57), channel_id=1, source_target_pairs={{0,32},{16,48},{32,0},{48,16},{1,33},{17,49},{33,1},{49,17},{2,34}... | collective-permute-start | bytes 294920 | tf_op jit(solution)/shard_map/place/ppermute | solution.py:41
  186.7 7.1 %collective-permute-start.33 = (f32[2,16,768]{2,1,0:T(8,128)S(1)}, f32[2,16,768]{2,1,0:T(8,128)S(1)}, u32[]{:S(2)}, u32[]{:S(2)}) collective-permute-start(f32[2,16,768]{2,1,0:T(8,128)S(1)} %get-tuple-element.58), channel_id=1, source_target_pairs={{0,48},{16,0},{32,16},{48,32},{1,49},{17,1},{33,17},{49,33},{2,50}... | collective-permute-start | bytes 294920 | tf_op jit(solution)/shard_map/place/ppermute | solution.py:41
